TPU v7x, 32 devices: a whole 2x2x4 slice. The times are simulated.
32 devices in a mesh: feat: 16 (over z, y, x), samp: 2 (over core).
Axes of the slice: x: 2, y: 2, z: 4, core: 2. Of those that a mesh axis runs over, the one named last changes fastest.
Arguments:
- spectra: bfloat16 [16384, 512], P('feat', 'samp'), may hold values from -6 to 6
- pair_blocks: int32 [512, 2], P('feat'), may hold values from -1 to 63, as said below
- windows: int32 [64, 2], replicated, may hold values from 0 to 2998, as said below
Outputs:
- corr: float32 [512, 256, 256], P(('feat', 'samp'))
- profiles: bfloat16 [16384, 512], P('feat', 'samp')
Inputs may be any that keep to these rules, and one draw needn't show every extreme that they name: `pair_blocks`: slots lie in groups of 8; slot s of the device at index d along feat is in group g = s // 8. A live entry (i, j) has block i among the 4 blocks of device d and block j among those of device d + g, with i <= j in group 0; no pair appears twice; unused slots hold -1 in both columns. At most 8 slots of a group are live, and some group has all 8 live. `windows`: column 0 is a block's first retention index and column 1 its last, which is at least 20 larger.
All inputs are finite; a program needn't handle non-finite values.
Results may differ from a plain program's by a relative error of at most 0.0075.
Values may be sent and summed in bfloat16 or wider, within the bound.
No kernel may reach another device: no remote copies, remote signals or barrier semaphores. Data moves between devices by JAX's collectives and lax.ppermute only.
A program may use at most 64 MiB of HBM per device.

v0:
```python
import jax
import jax.numpy as jnp
from jax import lax
from jax.sharding import PartitionSpec as P

BS = 256
BLK_DEV = 4
CAP = 8
REACH = 3
SLOTS = 32


def from_behind(value, axis, by):
    length = lax.axis_size(axis)
    pairs = [(i, i + by) for i in range(length) if 0 <= i + by < length]
    return lax.ppermute(value, axis, pairs)


def place_tiles(rows_hot, cols_hot, tiles):
    placed = jnp.einsum(
        "pa,pc,pfg->afcg", rows_hot, cols_hot, tiles, preferred_element_type=jnp.float32
    )
    count = rows_hot.shape[1] * tiles.shape[1]
    return placed.astype(jnp.bfloat16).reshape(count, count)


def body(spectra, pair_blocks, windows):
    position = lax.axis_index("feat")
    shards = lax.axis_size("samp")
    rows, width = spectra.shape
    values = spectra.astype(jnp.float32)
    sums, squares = lax.psum((jnp.sum(values, axis=1), jnp.sum(values * values, axis=1)), "samp")
    total = width * shards
    mean = sums / total
    var = squares / total - mean * mean
    inv = lax.rsqrt(var + 1e-05)
    z = ((values - mean[:, None]) * inv[:, None]).astype(jnp.bfloat16).reshape(BLK_DEV, BS, width)
    z_flat = z.reshape(rows, width)
    pieces = [z]
    for offset in range(1, REACH + 1):
        pieces.append(from_behind(z, "feat", -offset))
    window = jnp.concatenate(pieces, axis=0)
    span = window.shape[0]
    first = pair_blocks[:, 0]
    second = pair_blocks[:, 1]
    live = first >= 0
    base = position * BLK_DEV
    near = jnp.clip(first - base, 0, BLK_DEV - 1)
    far = jnp.clip(second - base, 0, span - 1)
    ia = jnp.maximum(first, 0)
    ja = jnp.maximum(second, 0)
    lo_i = windows[ia, 0]
    hi_i = windows[ia, 1]
    lo_j = windows[ja, 0]
    hi_j = windows[ja, 1]
    intersection = jnp.maximum(jnp.minimum(hi_i, hi_j) - jnp.maximum(lo_i, lo_j), 0)
    weight = (intersection + 16).astype(jnp.float32) / (hi_i - lo_i + hi_j - lo_j + 16).astype(
        jnp.float32
    )
    weight = jnp.where(live, weight, jnp.float32(0.0))
    half = SLOTS // shards
    start = lax.axis_index("samp") * half
    grams = []
    for group in range(REACH + 1):
        lower = group * CAP
        ahead_blocks = window[group * BLK_DEV : (group + 1) * BLK_DEV]
        dense = jnp.einsum("afs,cgs->acfg", z, ahead_blocks, preferred_element_type=jnp.float32)
        near_g = near[lower : lower + CAP]
        far_g = jnp.clip(far[lower : lower + CAP] - group * BLK_DEV, 0, BLK_DEV - 1)
        grams.append(dense[near_g, far_g])
    gram = jnp.concatenate(grams, axis=0)
    shares = lax.psum_scatter(gram, "samp", scatter_dimension=0, tiled=True)
    own_weight = lax.dynamic_slice_in_dim(weight, start, half)
    corr = shares * (own_weight / total)[:, None, None]
    tiles_all = lax.all_gather(corr.astype(jnp.bfloat16), "samp", axis=0, tiled=True)
    acc = values * 0.0 + z_flat.astype(jnp.float32)
    labels = jnp.arange(BLK_DEV, dtype=jnp.int32)
    for group in range(REACH + 1):
        lower = group * CAP
        tiles = tiles_all[lower : lower + CAP]
        near_g = near[lower : lower + CAP]
        far_g = far[lower : lower + CAP]
        ahead_flat = window[group * BLK_DEV : (group + 1) * BLK_DEV].reshape(rows, width)
        home = (near_g[:, None] == labels[None, :]).astype(jnp.bfloat16)
        target = ((far_g - group * BLK_DEV)[:, None] == labels[None, :]).astype(jnp.bfloat16)
        placed = place_tiles(home, target, tiles)
        acc = acc + jnp.dot(placed, ahead_flat, preferred_element_type=jnp.float32)
        if group == 0:
            differ = (first[lower : lower + CAP] != second[lower : lower + CAP]).astype(
                jnp.bfloat16
            )
            placed_off = place_tiles(home, target * differ[:, None], tiles)
            acc = acc + jnp.dot(placed_off.T, z_flat, preferred_element_type=jnp.float32)
        else:
            outgoing = jnp.dot(placed.T, z_flat, preferred_element_type=jnp.float32)
            acc = acc + from_behind(outgoing.astype(jnp.bfloat16), "feat", group).astype(
                outgoing.dtype
            )
    profiles = acc.astype(jnp.bfloat16)
    return (corr, profiles)


def solution(mesh):
    placed = (P("feat", "samp"), P("feat", None), P())
    return jax.shard_map(
        body,
        mesh=mesh,
        in_specs=placed,
        out_specs=(P(("feat", "samp"), None, None), P("feat", "samp")),
        check_vma=False,
    )
```

profile of v0, /device:TPU:12, one launch (start us, length us, event | category | flops | bytes accessed | tf_op | source)
XLA Modules:
  0.0 197.6 jit_solution(17001883758933175263)
XLA Ops:
  8.6 2.5 %all-reduce.4 = (f32[1024]{0:T(1024)S(1)}, f32[1024]{0:T(1024)S(1)}) all-reduce(f32[1024]{0:T(1024)S(1)} %get-tuple-element.9, f32[1024]{0:T(1024)S(1)} %get-tuple-element.8), channel_id=1, replica_groups=mesh['feat'=16,'samp'=2] {'samp'}, use_global_device_ids=true, to_apply=%region_3.0 | all-reduce | flops 2048 | bytes 16384 | tf_op jit(solution)/shard_map/psum | solution.py:32
  12.5 3.3 %collective-permute-start = (bf16[4,256,256]{2,1,0:T(8,128)(2,1)S(1)}, bf16[4,256,256]{2,1,0:T(8,128)(2,1)S(1)}, u32[]{:S(2)}, u32[]{:S(2)}) collective-permute-start(bf16[4,256,256]{2,1,0:T(8,128)(2,1)S(1)} %bitcast.154), channel_id=1, source_target_pairs={{2,0},{4,2},{6,4},{8,6},{10,8},{12,10},{14,12},{16,14},{18,16},{20... | collective-permute-start | bytes 1572872 | tf_op jit(solution)/shard_map/ppermute | solution.py:16
  15.9 3.3 %collective-permute-start.1 = (bf16[4,256,256]{2,1,0:T(8,128)(2,1)S(1)}, bf16[4,256,256]{2,1,0:T(8,128)(2,1)}, u32[]{:S(2)}, u32[]{:S(2)}) collective-permute-start(bf16[4,256,256]{2,1,0:T(8,128)(2,1)S(1)} %bitcast.155), channel_id=1, source_target_pairs={{4,0},{6,2},{8,4},{10,6},{12,8},{14,10},{16,12},{18,14},{20,16},{2... | collective-permute-start | bytes 1572872 | tf_op jit(solution)/shard_map/ppermute | solution.py:16
  19.2 1.9 collective-permute-start.2
  21.9 2.8 %convolution_bitcast_fusion.3 = f32[4,4,256,256]{2,3,0,1:T(8,128)} fusion(bf16[4,256,256,1]{2,1,3,0:T(8,128)(2,1)S(1)} %bitcast.158, bf16[4,256,256,1]{2,1,0,3:T(8,128)(2,1)S(1)} %bitcast.157), kind=kOutput, calls=%fused_computation.12 | convolution fusion | flops 536870912 | bytes 5242880 | tf_op jit(solution)/shard_map/afs,cgs->acfg/dot_general | solution.py:67
  24.7 2.9 %gather_fusion = f32[8,256,256]{1,2,0:T(8,128)S(1)} fusion(f32[4,4,256,256]{2,3,0,1:T(8,128)} %convolution_bitcast_fusion.3, s32[8]{0:T(128)S(1)} %get-tuple-element.26), kind=kCustom, calls=%fused_computation | custom fusion | bytes 4194368 | tf_op jit(solution)/shard_map/gather | solution.py:70
  27.6 11.0 %collective-permute-done = bf16[4,256,256]{2,1,0:T(8,128)(2,1)S(1)} collective-permute-done((bf16[4,256,256]{2,1,0:T(8,128)(2,1)S(1)}, bf16[4,256,256]{2,1,0:T(8,128)(2,1)S(1)}, u32[]{:S(2)}, u32[]{:S(2)}) %collective-permute-start) | collective-permute-done | bytes 524320 | tf_op jit(solution)/shard_map/ppermute | solution.py:16
  38.6 2.8 %convolution_bitcast_fusion.2 = f32[4,4,256,256]{2,3,0,1:T(8,128)} fusion(bf16[4,256,256,1]{2,1,0,3:T(8,128)(2,1)S(1)} %bitcast.159, bf16[4,256,256]{2,1,0:T(8,128)(2,1)S(1)} %collective-permute-done), kind=kOutput, calls=%fused_computation.11 | convolution fusion | flops 536870912 | bytes 5242880 | tf_op jit(solution)/shard_map/afs,cgs->acfg/dot_general | solution.py:67
  41.4 4.2 %gather_fusion.1 = f32[8,256,256]{1,2,0:T(8,128)} fusion(f32[4,4,256,256]{2,3,0,1:T(8,128)} %convolution_bitcast_fusion.2, s32[8]{0:T(128)S(1)} %get-tuple-element.29), kind=kCustom, calls=%fused_computation.1 | custom fusion | bytes 4194368 | tf_op jit(solution)/shard_map/gather | solution.py:70
  45.6 8.4 %collective-permute-done.1 = bf16[4,256,256]{2,1,0:T(8,128)(2,1)} collective-permute-done((bf16[4,256,256]{2,1,0:T(8,128)(2,1)S(1)}, bf16[4,256,256]{2,1,0:T(8,128)(2,1)}, u32[]{:S(2)}, u32[]{:S(2)}) %collective-permute-start.1) | collective-permute-done | bytes 524320 | tf_op jit(solution)/shard_map/ppermute | solution.py:16
  54.0 3.8 %convolution_bitcast_fusion.1 = f32[4,4,256,256]{2,3,0,1:T(8,128)} fusion(bf16[4,256,256,1]{2,1,0,3:T(8,128)(2,1)S(1)} %bitcast.160, bf16[4,256,256]{2,1,0:T(8,128)(2,1)} %collective-permute-done.1), kind=kOutput, calls=%fused_computation.10 | convolution fusion | flops 536870912 | bytes 5242880 | tf_op jit(solution)/shard_map/afs,cgs->acfg/dot_general | solution.py:67
  57.8 4.2 %gather_fusion.2 = f32[8,256,256]{1,2,0:T(8,128)} fusion(f32[4,4,256,256]{2,3,0,1:T(8,128)} %convolution_bitcast_fusion.1, s32[8]{0:T(128)S(1)} %get-tuple-element.28), kind=kCustom, calls=%fused_computation.2 | custom fusion | bytes 4194368 | tf_op jit(solution)/shard_map/gather | solution.py:70
  62.0 3.8 %convolution_bitcast_fusion = f32[4,4,256,256]{2,3,0,1:T(8,128)} fusion(bf16[4,256,256,1]{2,1,0,3:T(8,128)(2,1)S(1)} %bitcast.161, bf16[4,256,256]{2,1,0:T(8,128)(2,1)} %collective-permute-done.2), kind=kOutput, calls=%fused_computation.9 | convolution fusion | flops 536870912 | bytes 5242880 | tf_op jit(solution)/shard_map/afs,cgs->acfg/dot_general | solution.py:67
  65.8 4.2 %gather_fusion.3 = f32[8,256,256]{1,2,0:T(8,128)} fusion(f32[4,4,256,256]{2,3,0,1:T(8,128)} %convolution_bitcast_fusion, s32[8]{0:T(128)S(1)} %get-tuple-element.27), kind=kCustom, calls=%fused_computation.3 | custom fusion | bytes 4194368 | tf_op jit(solution)/shard_map/gather | solution.py:70
  70.0 5.7 %pad_maximum_fusion = f32[32,256,256]{1,2,0:T(8,128)} fusion(f32[8,256,256]{1,2,0:T(8,128)} %gather_fusion.3, f32[8,256,256]{1,2,0:T(8,128)} %gather_fusion.2, f32[8,256,256]{1,2,0:T(8,128)} %gather_fusion.1, f32[8,256,256]{1,2,0:T(8,128)S(1)} %gather_fusion), kind=kLoop, calls=%fused_computation.8 | loop fusion | flops 6291456 | bytes 16777216 | tf_op jit(solution)/shard_map/concatenate | solution.py:71
  78.9 14.5 %reduce-scatter.2.cloned.1.call-done = f32[16,256,256]{1,2,0:T(8,128)} async-done(((f32[32,256,256]{1,2,0:T(8,128)}), f32[16,256,256]{1,2,0:T(8,128)}) %reduce-scatter.2.cloned.1.call-update) | async-done | bytes 4194320 | tf_op jit(solution)/shard_map/reduce_scatter | solution.py:72
  93.4 4.8 %fusion.71 = (bf16[16,256,256]{1,2,0:T(8,128)(2,1)S(1)}, f32[16,256,256]{1,2,0:T(8,128)}) fusion(f32[16,256,256]{1,2,0:T(8,128)} %reduce-scatter.2.cloned.1.call-done, f32[16]{0:T(128)S(1)} %dynamic-slice_multiply_fusion), kind=kLoop, calls=%fused_computation.134 | loop fusion | flops 2097152 | bytes 10485824 | tf_op jit(solution)/shard_map/convert_element_type | solution.py:75
  98.2 2.4 %copy.22 = bf16[16,256,256]{2,1,0:T(8,128)(2,1)} copy(bf16[16,256,256]{1,2,0:T(8,128)(2,1)S(1)} %get-tuple-element.12) | data formatting | bytes 4194304 | tf_op jit(solution)/shard_map/convert_element_type | solution.py:75
  100.9 5.3 %copy.32 = f32[16,256,256]{2,1,0:T(8,128)} copy(f32[16,256,256]{1,2,0:T(8,128)} %get-tuple-element.13) | data formatting | bytes 8388608
  106.2 9.5 %all-gather.2.cloned.1.call-done = bf16[32,256,256]{2,1,0:T(8,128)(2,1)} async-done(((bf16[16,256,256]{2,1,0:T(8,128)(2,1)}), bf16[32,256,256]{2,1,0:T(8,128)(2,1)}) %all-gather.2.cloned.1.call-update) | async-done | bytes 4194320 | tf_op jit(solution)/shard_map/all_gather | solution.py:75
  115.7 2.6 %fusion.72 = (bf16[8,256,256]{2,1,0:T(8,128)(2,1)S(1)}, bf16[8,256,256]{2,1,0:T(8,128)(2,1)S(1)}, bf16[8,256,256]{2,1,0:T(8,128)(2,1)S(1)}, bf16[8,256,256]{2,1,0:T(8,128)(2,1)S(1)}) fusion(bf16[32,256,256]{2,1,0:T(8,128)(2,1)} %all-gather.2.cloned.1.call-done), kind=kLoop, calls=%fused_computation.135 | loop fusion | bytes 8388608 | tf_op jit(solution)/shard_map/slice | solution.py:80
  119.5 1.6 copy.24
  127.6 1.6 copy.29
  131.1 1.8 fusion.73
  134.0 1.6 copy.31
  140.6 3.4 %collective-permute-start.3 = (bf16[1024,256]{1,0:T(8,128)(2,1)S(1)}, bf16[1024,256]{1,0:T(8,128)(2,1)S(1)}, u32[]{:S(2)}, u32[]{:S(2)}) collective-permute-start(bf16[1024,256]{1,0:T(8,128)(2,1)S(1)} %convolution_convert_fusion.2), channel_id=1, source_target_pairs={{0,2},{2,4},{4,6},{6,8},{8,10},{10,12},{12,14},{14,16},{16,18},{18... | collective-permute-start | bytes 1572872 | tf_op jit(solution)/shard_map/ppermute | solution.py:16
  143.9 3.4 %collective-permute-start.4 = (bf16[1024,256]{1,0:T(8,128)(2,1)S(1)}, bf16[1024,256]{1,0:T(8,128)(2,1)S(1)}, u32[]{:S(2)}, u32[]{:S(2)}) collective-permute-start(bf16[1024,256]{1,0:T(8,128)(2,1)S(1)} %convolution_convert_fusion.1), channel_id=1, source_target_pairs={{0,4},{2,6},{4,8},{6,10},{8,12},{10,14},{12,16},{14,18},{16,20},{1... | collective-permute-start | bytes 1572872 | tf_op jit(solution)/shard_map/ppermute | solution.py:16
  148.4 4.3 %collective-permute-start.5 = (bf16[1024,256]{1,0:T(8,128)(2,1)S(1)}, bf16[1024,256]{1,0:T(8,128)(2,1)S(1)}, u32[]{:S(2)}, u32[]{:S(2)}) collective-permute-start(bf16[1024,256]{1,0:T(8,128)(2,1)S(1)} %convolution_convert_fusion), channel_id=1, source_target_pairs={{0,6},{2,8},{4,10},{6,12},{8,14},{10,16},{12,18},{14,20},{16,22},{... | collective-permute-start | bytes 1572872 | tf_op jit(solution)/shard_map/ppermute | solution.py:16
  152.7 1.8 fusion.74
  155.6 13.2 %collective-permute-done.3 = bf16[1024,256]{1,0:T(8,128)(2,1)S(1)} collective-permute-done((bf16[1024,256]{1,0:T(8,128)(2,1)S(1)}, bf16[1024,256]{1,0:T(8,128)(2,1)S(1)}, u32[]{:S(2)}, u32[]{:S(2)}) %collective-permute-start.3) | collective-permute-done | bytes 524320 | tf_op jit(solution)/shard_map/ppermute | solution.py:16
  168.8 20.2 %collective-permute-done.5 = bf16[1024,256]{1,0:T(8,128)(2,1)S(1)} collective-permute-done((bf16[1024,256]{1,0:T(8,128)(2,1)S(1)}, bf16[1024,256]{1,0:T(8,128)(2,1)S(1)}, u32[]{:S(2)}, u32[]{:S(2)}) %collective-permute-start.5) | collective-permute-done | bytes 524320 | tf_op jit(solution)/shard_map/ppermute | solution.py:16
  189.0 1.7 fusion.5
  (53 shorter events, 24.7 us)
Async XLA Ops:
  7.2 68.6 %copy-start = (s32[64,2]{0,1:T(2,128)S(1)}, s32[64,2]{0,1:T(2,128)}, u32[]{:S(2)}) copy-start(s32[64,2]{0,1:T(2,128)} %param.5) | copy-start | bytes 1540
  7.2 86.2 %reduce-scatter.2.cloned.1.call-start = ((), (), s32[]{:S(2)}) async-start(), calls=%async_computation.1 | async-start | bytes 12582912 | tf_op jit(solution)/shard_map/reduce_scatter | solution.py:72
  12.5 26.1 %collective-permute-start = (bf16[4,256,256]{2,1,0:T(8,128)(2,1)S(1)}, bf16[4,256,256]{2,1,0:T(8,128)(2,1)S(1)}, u32[]{:S(2)}, u32[]{:S(2)}) collective-permute-start(bf16[4,256,256]{2,1,0:T(8,128)(2,1)S(1)} %bitcast.154), channel_id=1, source_target_pairs={{2,0},{4,2},{6,4},{8,6},{10,8},{12,10},{14,12},{16,14},{18,16},{20... | collective-permute-start | bytes 1572872 | tf_op jit(solution)/shard_map/ppermute | solution.py:16
  15.9 38.1 %collective-permute-start.1 = (bf16[4,256,256]{2,1,0:T(8,128)(2,1)S(1)}, bf16[4,256,256]{2,1,0:T(8,128)(2,1)}, u32[]{:S(2)}, u32[]{:S(2)}) collective-permute-start(bf16[4,256,256]{2,1,0:T(8,128)(2,1)S(1)} %bitcast.155), channel_id=1, source_target_pairs={{4,0},{6,2},{8,4},{10,6},{12,8},{14,10},{16,12},{18,14},{20,16},{2... | collective-permute-start | bytes 1572872 | tf_op jit(solution)/shard_map/ppermute | solution.py:16
  19.2 42.8 %collective-permute-start.2 = (bf16[4,256,256]{2,1,0:T(8,128)(2,1)S(1)}, bf16[4,256,256]{2,1,0:T(8,128)(2,1)}, u32[]{:S(2)}, u32[]{:S(2)}) collective-permute-start(bf16[4,256,256]{2,1,0:T(8,128)(2,1)S(1)} %bitcast.156), channel_id=1, source_target_pairs={{6,0},{8,2},{10,4},{12,6},{14,8},{16,10},{18,12},{20,14},{22,16},{... | collective-permute-start | bytes 1572872 | tf_op jit(solution)/shard_map/ppermute | solution.py:16
  75.7 3.1 %copy-start.3 = (s32[32,2]{0,1:T(2,128)S(1)}, s32[32,2]{0,1:T(2,128)}, u32[]{:S(2)}) copy-start(s32[32,2]{0,1:T(2,128)} %param.4) | copy-start | bytes 772
  75.7 40.0 %all-gather.2.cloned.1.call-start = ((), (), s32[]{:S(2)}) async-start(), calls=%async_computation.2 | async-start | bytes 6291456 | tf_op jit(solution)/shard_map/all_gather | solution.py:75
  121.1 1.0 copy-start.2
  140.6 28.2 %collective-permute-start.3 = (bf16[1024,256]{1,0:T(8,128)(2,1)S(1)}, bf16[1024,256]{1,0:T(8,128)(2,1)S(1)}, u32[]{:S(2)}, u32[]{:S(2)}) collective-permute-start(bf16[1024,256]{1,0:T(8,128)(2,1)S(1)} %convolution_convert_fusion.2), channel_id=1, source_target_pairs={{0,2},{2,4},{4,6},{6,8},{8,10},{10,12},{12,14},{14,16},{16,18},{18... | collective-permute-start | bytes 1572872 | tf_op jit(solution)/shard_map/ppermute | solution.py:16
  143.9 24.8 %collective-permute-start.4 = (bf16[1024,256]{1,0:T(8,128)(2,1)S(1)}, bf16[1024,256]{1,0:T(8,128)(2,1)S(1)}, u32[]{:S(2)}, u32[]{:S(2)}) collective-permute-start(bf16[1024,256]{1,0:T(8,128)(2,1)S(1)} %convolution_convert_fusion.1), channel_id=1, source_target_pairs={{0,4},{2,6},{4,8},{6,10},{8,12},{10,14},{12,16},{14,18},{16,20},{1... | collective-permute-start | bytes 1572872 | tf_op jit(solution)/shard_map/ppermute | solution.py:16
  148.4 40.6 %collective-permute-start.5 = (bf16[1024,256]{1,0:T(8,128)(2,1)S(1)}, bf16[1024,256]{1,0:T(8,128)(2,1)S(1)}, u32[]{:S(2)}, u32[]{:S(2)}) collective-permute-start(bf16[1024,256]{1,0:T(8,128)(2,1)S(1)} %convolution_convert_fusion), channel_id=1, source_target_pairs={{0,6},{2,8},{4,10},{6,12},{8,14},{10,16},{12,18},{14,20},{16,22},{... | collective-permute-start | bytes 1572872 | tf_op jit(solution)/shard_map/ppermute | solution.py:16
  189.0 1.7 copy-start.1
Sparse Core Ops, SparseCore 0:
  75.8 17.5 reduce-scatter.1
  100.8 14.8 all-gather.1
where the time goes:
time: 198 us
  waiting for transfers between devices  76.9 us (39%)
  local copies, waits for them, and re-layouts  40 us (20%)
  matrix products  29.8 us (15%)
  starting transfers between devices  19.7 us (10%)
  between operations  14.4 us (7%)
  other arithmetic  14.3 us (7%)
  blocking collectives  2.5 us (1%)
    ppermute x6, waiting for transfers between devices, from_behind(): return lax.ppermute(value, axis, pairs)  52.9 us
    ppermute x6, starting transfers between devices, from_behind(): return lax.ppermute(value, axis, pairs)  19.6 us
    gather x4, local copies, waits for them, and re-layouts, body(): grams.append(dense[near_g, far_g])  15.5 us
    reduce_scatter x1, waiting for transfers between devices, body(): shares = lax.psum_scatter(gram, 'samp', scatter_dimension=0, tiled=True)  14.5 us
    dot_general x4, matrix products, body(): jnp.einsum('afs,cgs->acfg', z, ahead_blocks, preferred_element_type=jnp.f...  13.1 us
    all_gather x1, waiting for transfers between devices, body(): lax.all_gather(corr.astype(jnp.bfloat16), 'samp', axis=0, tiled=True)  9.47 us
    unnamed x14, local copies, waits for them, and re-layouts  8.34 us
    convert_element_type x5, local copies, waits for them, and re-layouts, place_tiles(): return placed.astype(jnp.bfloat16).reshape(count, count)  8.11 us
  transfers between devices with their start and end apart: 8, of which 6 were waited for; matrix products, arithmetic and copies ran while one was open for 17% of the time, Pallas kernels for 0%

commit v1 on v0

v1 whole, which is shorter than its diff:
```python
import functools

import jax
import jax.numpy as jnp
from jax import lax
from jax.experimental import pallas as pl
from jax.experimental.pallas import tpu as pltpu
from jax.sharding import PartitionSpec as P

BS = 256
BLK_DEV = 4
CAP = 8
REACH = 3
QUAD = 4
EPS = 1e-05
VMEM = 24 * 1024 * 1024


def along_x(i):
    return i ^ 1


def along_y(i):
    return i ^ 2


def along_z_own(i):
    return i - QUAD if i % 2 == 0 else i + QUAD


def along_z_side(i):
    return i + QUAD if i % QUAD < 2 else i - QUAD


def send(value, move):
    length = lax.axis_size("feat")
    pairs = [(i, move(i)) for i in range(length) if 0 <= move(i) < length]
    return lax.ppermute(value, "feat", pairs)


def swap(value):
    return lax.ppermute(value, "samp", [(0, 1), (1, 0)])


def off_x(r):
    return 1 - 2 * (r % 2)


def off_y(r):
    return 2 - 4 * (r // 2)


def off_diag(r):
    return 3 - 2 * r


def off_zx(r):
    return 6 * (r % 2) - 3


def off_zy(r):
    return 4 * (r // 2) - 2


def off_last(r):
    return jnp.where(r == 0, -1, jnp.where(r == 1, -3, jnp.where(r == 2, 3, 1)))


def normalise(own_ref, par_ref, z_ref, start):
    rows, width = own_ref.shape
    step = 128

    def one(k, _):
        at = pl.multiple_of(k * step, step)
        a = own_ref[pl.ds(at, step), :].astype(jnp.float32)
        b = par_ref[pl.ds(at, step), :].astype(jnp.float32)
        total = 2 * width
        mean = jnp.sum(a + b, axis=1, keepdims=True) / total
        var = jnp.sum(a * a + b * b, axis=1, keepdims=True) / total - mean * mean
        inv = lax.rsqrt(var + EPS)
        to = pl.multiple_of(start + k * step, step)
        z_ref[pl.ds(to, step), :width] = ((a - mean) * inv).astype(jnp.bfloat16)
        z_ref[pl.ds(to, step), width:] = ((b - mean) * inv).astype(jnp.bfloat16)
        return 0

    lax.fori_loop(0, rows // step, one, 0)


def slot_of(meta, wins, off, slot):
    position = meta[0]
    at = 2 + ((off + REACH) * CAP + slot) * 2
    mine = meta[at]
    other = meta[at + 1]
    live = mine >= 0
    b = jnp.where(live, mine - position * BLK_DEV, 0)
    o = jnp.where(live, other - (position + off) * BLK_DEV, 0)
    mine = jnp.maximum(mine, 0)
    other = jnp.maximum(other, 0)
    lo_b = wins[2 * mine]
    hi_b = wins[2 * mine + 1]
    lo_o = wins[2 * other]
    hi_o = wins[2 * other + 1]
    meet = jnp.maximum(jnp.minimum(hi_b, hi_o) - jnp.maximum(lo_b, lo_o), 0)
    num = jnp.where(live, meet + 16, 0)
    den = hi_b - lo_b + hi_o - lo_o + 16
    return b, o, num, den


def scale_of(num, den, samples):
    top = jnp.full((1, BS), num, jnp.int32).astype(jnp.float32)
    low = jnp.full((1, BS), den, jnp.int32).astype(jnp.float32)
    return top / low / samples


def block(ref, index):
    return ref[pl.ds(pl.multiple_of(index * BS, BS), BS), :]


def pair_slots(meta, wins, off, zown_ref, z_ref, acc_ref, tile_ref, itself):
    width = acc_ref.shape[1]
    samples = 2 * width

    def one(slot, _):
        b, o, num, den = slot_of(meta, wins, off, slot)
        scale = scale_of(num, den, samples)
        zb = block(zown_ref, b)
        zo = block(z_ref, o)
        gram = lax.dot_general(
            zb, zo, (((1,), (1,)), ((), ())), preferred_element_type=jnp.float32
        )
        corr = gram * scale
        tile_ref[slot] = corr
        tile = corr.astype(jnp.bfloat16)
        at = pl.ds(pl.multiple_of(b * BS, BS), BS)
        acc_ref[at, :] += jnp.dot(tile, zo[:, :width], preferred_element_type=jnp.float32)
        if itself:
            differ = jnp.where(b == o, 0.0, 1.0)
            back = lax.dot_general(
                tile, zb[:, :width], (((0,), (0,)), ((), ())), preferred_element_type=jnp.float32
            )
            at = pl.ds(pl.multiple_of(o * BS, BS), BS)
            acc_ref[at, :] += back * differ
        return 0

    lax.fori_loop(0, CAP, one, 0)


def put_tiles(meta, off, tile_ref, corr_ref, sem):
    mine = jnp.logical_and(off >= 0, off // 2 == meta[1])
    first = pl.multiple_of(jnp.where(off == 1, CAP, jnp.where(off == 3, CAP, 0)), CAP)
    copy = pltpu.make_async_copy(tile_ref, corr_ref.at[pl.ds(first, CAP)], sem)
    return mine, copy


def self_kernel(meta, wins, own_ref, par_ref, zown_ref, acc_ref, corr_ref, tile_ref, sem):
    width = own_ref.shape[1]
    normalise(own_ref, par_ref, zown_ref, 0)
    acc_ref[...] = zown_ref[:, :width].astype(jnp.float32)
    pair_slots(meta, wins, 0, zown_ref, zown_ref, acc_ref, tile_ref, True)
    mine, copy = put_tiles(meta, jnp.int32(0), tile_ref, corr_ref, sem)

    @pl.when(mine)
    def _():
        copy.start()
        copy.wait()


def unit_kernel(offs, pieces, final, *refs):
    count = len(offs)
    meta, wins, zown_ref, acc_in = refs[:4]
    raws = refs[4 : 4 + 2 * count * pieces]
    rest = refs[4 + 2 * count * pieces + 1 :]
    out_ref, corr_ref, acc_ref, z_ref, tile_ref, sems = rest
    acc_ref[...] = acc_in[...]
    r = lax.rem(meta[0], QUAD)
    pending = []
    for k, off_of in enumerate(offs):
        off = off_of(r)
        start = 0
        for piece in range(pieces):
            own_ref, par_ref = raws[2 * (k * pieces + piece) : 2 * (k * pieces + piece) + 2]
            normalise(own_ref, par_ref, z_ref, start)
            start += own_ref.shape[0]
        if k >= 2:
            was, before = pending[k - 2]

            @pl.when(was)
            def _(before=before):
                before.wait()

        tiles = tile_ref.at[k % 2]
        pair_slots(meta, wins, off, zown_ref, z_ref, acc_ref, tiles, False)
        mine, copy = put_tiles(meta, off, tiles, corr_ref, sems.at[k % 2])
        pending.append((mine, copy))

        @pl.when(mine)
        def _(copy=copy):
            copy.start()

    out_ref[...] = acc_ref[...].astype(out_ref.dtype)
    for was, before in pending[-2:]:

        @pl.when(was)
        def _(before=before):
            before.wait()


def estimate(units):
    return pl.CostEstimate(
        flops=units * CAP * 2 * BS * BS * BS * 3, bytes_accessed=units * 8 * 2**20, transcendentals=0
    )


SMEM = pl.BlockSpec(memory_space=pltpu.SMEM)
INSIDE = pl.BlockSpec(memory_space=pltpu.VMEM)
ANY = pl.BlockSpec(memory_space=pl.ANY)


def run_self(meta, wins, own, par):
    rows, width = own.shape
    return pl.pallas_call(
        self_kernel,
        out_shape=(
            jax.ShapeDtypeStruct((rows, 2 * width), jnp.bfloat16),
            jax.ShapeDtypeStruct((rows, width), jnp.float32),
            jax.ShapeDtypeStruct((2 * CAP, BS, BS), jnp.float32),
        ),
        in_specs=[SMEM, SMEM, INSIDE, INSIDE],
        out_specs=(INSIDE, INSIDE, ANY),
        scratch_shapes=[pltpu.VMEM((CAP, BS, BS), jnp.float32), pltpu.SemaphoreType.DMA],
        compiler_params=pltpu.CompilerParams(vmem_limit_bytes=VMEM),
        cost_estimate=estimate(1),
        name="self_pairs",
    )(meta, wins, own, par)


def run_units(meta, wins, zown, acc, corr, offs, raws, pieces, final):
    rows, width = acc.shape
    name = "last_pairs" if final else "unit_pairs"
    return pl.pallas_call(
        functools.partial(unit_kernel, offs, pieces, final),
        out_shape=(
            jax.ShapeDtypeStruct((rows, width), jnp.bfloat16 if final else jnp.float32),
            jax.ShapeDtypeStruct(corr.shape, corr.dtype),
        ),
        in_specs=[SMEM, SMEM, INSIDE, INSIDE] + [INSIDE] * len(raws) + [ANY],
        out_specs=(INSIDE, ANY),
        scratch_shapes=[
            pltpu.VMEM((rows, width), jnp.float32),
            pltpu.VMEM((rows, 2 * width), jnp.bfloat16),
            pltpu.VMEM((2, CAP, BS, BS), jnp.float32),
            pltpu.SemaphoreType.DMA((2,)),
        ],
        input_output_aliases={4 + len(raws): 1},
        compiler_params=pltpu.CompilerParams(vmem_limit_bytes=VMEM),
        cost_estimate=estimate(len(offs)),
        name=name,
    )(meta, wins, zown, acc, *raws, corr)


def body(spectra, pair_blocks, windows):
    position = lax.axis_index("feat")
    half = spectra.shape[0] // 2
    par = swap(spectra)
    from_x = send(spectra, along_x)
    from_y = send(spectra, along_y)
    from_z = send(spectra, along_z_own)
    groups = pair_blocks.reshape(REACH + 1, CAP, 2)
    behind = [send(groups[g], lambda i, g=g: i + g) for g in range(1, REACH + 1)]
    tables = [
        jnp.where(position >= g, behind[g - 1][:, ::-1], -1) for g in range(REACH, 0, -1)
    ]
    ids = jnp.stack([position, lax.axis_index("samp")]).astype(jnp.int32)
    none = jnp.full((REACH * CAP * 2,), -1, jnp.int32)
    wins = windows.reshape(-1)
    meta0 = jnp.concatenate([ids, none, pair_blocks.reshape(-1)])
    zown, acc, corr = run_self(meta0, wins, spectra, par)
    meta = jnp.concatenate([ids] + [t.reshape(-1) for t in tables] + [pair_blocks.reshape(-1)])
    diag = send(from_x, along_y)
    zx = send(from_z, along_x)
    zy = send(from_y, along_z_side)
    raws = (from_x, swap(from_x), from_y, swap(from_y))
    acc, corr = run_units(meta, wins, zown, acc, corr, (off_x, off_y), raws, 1, False)
    last_a = send(zy[:half], along_x)
    last_b = send(diag[half:], along_z_side)
    raws = (diag, swap(diag), zx, swap(zx), zy, swap(zy))
    acc, corr = run_units(meta, wins, zown, acc, corr, (off_diag, off_zx, off_zy), raws, 1, False)
    raws = (last_a, swap(last_a), last_b, swap(last_b))
    profiles, corr = run_units(meta, wins, zown, acc, corr, (off_last,), raws, 2, True)
    return (corr, profiles)


def solution(mesh):
    placed = (P("feat", "samp"), P("feat", None), P())
    return jax.shard_map(
        body,
        mesh=mesh,
        in_specs=placed,
        out_specs=(P(("feat", "samp"), None, None), P("feat", "samp")),
        check_vma=False,
    )
```

time: 198 us -> 97 us (0.49)
  the two profiles are of different devices: /device:TPU:12 before, /device:TPU:1 now
where the time goes in v1:
time: 97 us; the launch traced here: 96.5 us
  Pallas kernels  40.9 us (42%)
  starting transfers between devices  35 us (36%)
  waiting for transfers between devices  14 us (14%)
  local copies, waits for them, and re-layouts  5.78 us (6%)
    pallas_call x3, Pallas kernels, run_units(): pl.pallas_call(functools.partial(unit_kernel, offs, pieces, final), out_s...  34.3 us
    ppermute x11, starting transfers between devices, send(): return lax.ppermute(value, 'feat', pairs)  26.2 us
    ppermute x11, waiting for transfers between devices, send(): return lax.ppermute(value, 'feat', pairs)  14 us
    ppermute x8, starting transfers between devices, swap(): return lax.ppermute(value, 'samp', [(0, 1), (1, 0)])  8.77 us
    pallas_call x1, Pallas kernels, run_self(): pl.pallas_call(self_kernel, out_shape=(jax.ShapeDtypeStruct((rows, 2 * wi...  6.58 us
    unnamed x4, local copies, waits for them, and re-layouts  2.58 us
  transfers between devices with their start and end apart: 19, of which 4 were waited for; matrix products, arithmetic and copies ran while one was open for 5% of the time, Pallas kernels for 35%

profile of v1, /device:TPU:1, one launch (start us, length us, event | category | flops | bytes accessed | tf_op | source)
XLA Modules:
  0.0 96.5 jit_solution(5667468029937633948)
XLA Ops:
  0.6 2.1 %collective-permute-start.6 = (bf16[1024,256]{1,0:T(8,128)(2,1)}, bf16[1024,256]{1,0:T(8,128)(2,1)S(1)}, u32[]{:S(2)}, u32[]{:S(2)}) collective-permute-start(bf16[1024,256]{1,0:T(8,128)(2,1)} %own_ref.1), channel_id=1, source_target_pairs={{0,4},{2,6},{4,0},{6,2},{8,12},{10,14},{12,8},{14,10},{16,20},{18,... | collective-permute-start | bytes 1572872 | tf_op jit(solution)/shard_map/ppermute | solution.py:38
  2.8 1.2 %collective-permute-start.4 = (bf16[1024,256]{1,0:T(8,128)(2,1)}, bf16[1024,256]{1,0:T(8,128)(2,1)S(1)}, u32[]{:S(2)}, u32[]{:S(2)}) collective-permute-start(bf16[1024,256]{1,0:T(8,128)(2,1)} %own_ref.1), channel_id=1, source_target_pairs={{0,2},{2,0},{4,6},{6,4},{8,10},{10,8},{12,14},{14,12},{16,18},{18,... | collective-permute-start | bytes 1572872 | tf_op jit(solution)/shard_map/ppermute | solution.py:38
  4.0 1.3 %collective-permute-start.10 = (bf16[1024,256]{1,0:T(8,128)(2,1)}, bf16[1024,256]{1,0:T(8,128)(2,1)}, u32[]{:S(2)}, u32[]{:S(2)}) collective-permute-start(bf16[1024,256]{1,0:T(8,128)(2,1)} %own_ref.1), channel_id=1, source_target_pairs={{2,10},{6,14},{8,0},{10,18},{12,4},{14,22},{16,8},{18,26},{20,12},... | collective-permute-start | bytes 1572872 | tf_op jit(solution)/shard_map/ppermute | solution.py:38
  5.3 1.3 %collective-permute-start.3 = (bf16[1024,256]{1,0:T(8,128)(2,1)}, bf16[1024,256]{1,0:T(8,128)(2,1)}, u32[]{:S(2)}, u32[]{:S(2)}) collective-permute-start(bf16[1024,256]{1,0:T(8,128)(2,1)} %own_ref.1), channel_id=1, source_target_pairs={{0,1},{1,0},{2,3},{3,2},{4,5},{5,4},{6,7},{7,6},{8,9},{9,8},{10,11... | collective-permute-start | bytes 1572872 | tf_op jit(solution)/shard_map/ppermute | solution.py:42
  6.6 8.2 %collective-permute-done.6.refs_6_ = bf16[1024,256]{1,0:T(8,128)(2,1)S(1)} collective-permute-done((bf16[1024,256]{1,0:T(8,128)(2,1)}, bf16[1024,256]{1,0:T(8,128)(2,1)S(1)}, u32[]{:S(2)}, u32[]{:S(2)}) %collective-permute-start.6) | collective-permute-done | bytes 524320 | tf_op jit(solution)/shard_map/ppermute | solution.py:38
  14.7 3.1 %collective-permute-start.13 = (bf16[1024,256]{1,0:T(8,128)(2,1)S(1)}, bf16[1024,256]{1,0:T(8,128)(2,1)S(1)}, u32[]{:S(2)}, u32[]{:S(2)}) collective-permute-start(bf16[1024,256]{1,0:T(8,128)(2,1)S(1)} %collective-permute-done.6.refs_6_), channel_id=1, source_target_pairs={{0,8},{2,10},{8,16},{10,18},{12,4},{14,6},{16,24},{18,26},{20,12},... | collective-permute-start | bytes 1572872 | tf_op jit(solution)/shard_map/ppermute | solution.py:38
  18.0 0.4 collective-permute-done.10
  18.4 0.9 collective-permute-start.11
  19.2 0.9 fusion
  20.1 3.2 %collective-permute-start = (s32[8,2]{0,1:T(2,128)S(1)}, s32[8,2]{0,1:T(2,128)S(1)}, u32[]{:S(2)}, u32[]{:S(2)}) collective-permute-start(s32[8,2]{0,1:T(2,128)S(1)} %get-tuple-element.22), channel_id=1, source_target_pairs={{0,6},{2,8},{4,10},{6,12},{8,14},{10,16},{12,18},{14,20},{16,22},{... | collective-permute-start | bytes 200 | tf_op jit(solution)/shard_map/ppermute | solution.py:38
  23.4 0.8 copy.16
  24.1 0.1 reshape.30
  24.2 4.8 %collective-permute-done = s32[8,2]{0,1:T(2,128)S(1)} collective-permute-done((s32[8,2]{0,1:T(2,128)S(1)}, s32[8,2]{0,1:T(2,128)S(1)}, u32[]{:S(2)}, u32[]{:S(2)}) %collective-permute-start) | collective-permute-done | bytes 96 | tf_op jit(solution)/shard_map/ppermute | solution.py:38
  29.0 1.3 %collective-permute-start.1 = (s32[8,2]{0,1:T(2,128)S(1)}, s32[8,2]{0,1:T(2,128)S(1)}, u32[]{:S(2)}, u32[]{:S(2)}) collective-permute-start(s32[8,2]{0,1:T(2,128)S(1)} %get-tuple-element.21), channel_id=1, source_target_pairs={{0,4},{2,6},{4,8},{6,10},{8,12},{10,14},{12,16},{14,18},{16,20},{1... | collective-permute-start | bytes 200 | tf_op jit(solution)/shard_map/ppermute | solution.py:38
  30.3 0.8 copy.17
  31.1 5.5 %collective-permute-start.2 = (s32[8,2]{0,1:T(2,128)S(1)}, s32[8,2]{0,1:T(2,128)S(1)}, u32[]{:S(2)}, u32[]{:S(2)}) collective-permute-start(s32[8,2]{0,1:T(2,128)S(1)} %get-tuple-element.20), channel_id=1, source_target_pairs={{0,2},{2,4},{4,6},{6,8},{8,10},{10,12},{12,14},{14,16},{16,18},{18... | collective-permute-start | bytes 200 | tf_op jit(solution)/shard_map/ppermute | solution.py:38
  36.6 0.1 reshape.31.wins.refs_1_
  36.8 0.6 collective-permute-done.2
  37.3 4.6 %collective-permute-start.5 = (bf16[1024,256]{1,0:T(8,128)(2,1)S(1)}, bf16[1024,256]{1,0:T(8,128)(2,1)S(1)}, u32[]{:S(2)}, u32[]{:S(2)}) collective-permute-start(bf16[1024,256]{1,0:T(8,128)(2,1)S(1)} %collective-permute-done.4.refs_4_), channel_id=1, source_target_pairs={{0,1},{1,0},{2,3},{3,2},{4,5},{5,4},{6,7},{7,6},{8,9},{9,8},{10,11... | collective-permute-start | bytes 1572872 | tf_op jit(solution)/shard_map/ppermute | solution.py:42
  42.1 0.6 collective-permute-start.14
  42.6 0.1 collective-permute-start.9
  42.7 0.4 collective-permute-start.12
  43.5 0.7 slice.23
  44.2 0.7 slice.24
  45.0 2.0 %collective-permute-start.15 = (bf16[512,256]{1,0:T(8,128)(2,1)}, bf16[512,256]{1,0:T(8,128)(2,1)S(1)}, u32[]{:S(2)}, u32[]{:S(2)}) collective-permute-start(bf16[512,256]{1,0:T(8,128)(2,1)} %slice.23), channel_id=1, source_target_pairs={{0,2},{2,0},{4,6},{6,4},{8,10},{10,8},{12,14},{14,12},{16,18},{18,... | collective-permute-start | bytes 786440 | tf_op jit(solution)/shard_map/ppermute | solution.py:38
  47.0 5.4 %collective-permute-start.17 = (bf16[512,256]{1,0:T(8,128)(2,1)}, bf16[512,256]{1,0:T(8,128)(2,1)}, u32[]{:S(2)}, u32[]{:S(2)}) collective-permute-start(bf16[512,256]{1,0:T(8,128)(2,1)} %slice.24), channel_id=1, source_target_pairs={{0,8},{2,10},{8,16},{10,18},{12,4},{14,6},{16,24},{18,26},{20,12},... | collective-permute-start | bytes 786440 | tf_op jit(solution)/shard_map/ppermute | solution.py:38
  52.7 1.1 %copy-done = bf16[1024,256]{1,0:T(8,128)(2,1)S(1)} copy-done((bf16[1024,256]{1,0:T(8,128)(2,1)S(1)}, bf16[1024,256]{1,0:T(8,128)(2,1)}, u32[]{:S(2)}) %copy-start) | copy-done | bytes 524312
  53.7 6.6 %self_pairs.1 = (bf16[1024,512]{1,0:T(8,128)(2,1)S(1)}, f32[1024,256]{1,0:T(8,128)S(1)}, f32[16,256,256]{2,1,0:T(8,128)}) custom-call(s32[114]{0:T(128)S(1)} %pad_add_fusion.meta, s32[128]{0:T(128)S(1)} %reshape.31.wins.refs_1_, bf16[1024,256]{1,0:T(8,128)(2,1)S(1)} %copy-done, bf16[1024,256]{1,0:T(8,128)(2,1)} %collective-permute-done.3.par_ref), custom_call_target="tpu_custom_call" | custom-call | flops 805306368 | bytes 8388608 | tf_op jit(solution)/shard_map/self_pairs/pallas_call | solution.py:221
  60.3 1.7 %collective-permute-start.16 = (bf16[512,256]{1,0:T(8,128)(2,1)S(1)}, bf16[512,256]{1,0:T(8,128)(2,1)S(1)}, u32[]{:S(2)}, u32[]{:S(2)}) collective-permute-start(bf16[512,256]{1,0:T(8,128)(2,1)S(1)} %collective-permute-done.15.refs_4_), channel_id=1, source_target_pairs={{0,1},{1,0},{2,3},{3,2},{4,5},{5,4},{6,7},{7,6},{8,9},{9,8},{10,11... | collective-permute-start | bytes 786440 | tf_op jit(solution)/shard_map/ppermute | solution.py:42
  62.1 11.9 %unit_pairs.2 = (f32[1024,256]{1,0:T(8,128)S(1)}, f32[16,256,256]{2,1,0:T(8,128)}) custom-call(s32[114]{0:T(128)S(1)} %concatenate.8.refs_0_, s32[128]{0:T(128)S(1)} %reshape.31.wins.refs_1_, bf16[1024,512]{1,0:T(8,128)(2,1)S(1)} %get-tuple-element.11.refs_2_, f32[1024,256]{1,0:T(8,128)S(1)} %get-tuple-element.12.refs_3_, ...), custom_call_target="tpu_custom_call", output_to_operand_aliasing={{1}: (8, {})} | custom-call | flops 1610612736 | bytes 16777216 | tf_op jit(solution)/shard_map/unit_pairs/pallas_call | solution.py:240
  74.1 15.7 %unit_pairs.3 = (f32[1024,256]{1,0:T(8,128)S(1)}, f32[16,256,256]{2,1,0:T(8,128)}) custom-call(s32[114]{0:T(128)S(1)} %concatenate.8.refs_0_, s32[128]{0:T(128)S(1)} %reshape.31.wins.refs_1_, bf16[1024,512]{1,0:T(8,128)(2,1)S(1)} %get-tuple-element.11.refs_2_, f32[1024,256]{1,0:T(8,128)S(1)} %get-tuple-element.14.refs_3_, ...), custom_call_target="tpu_custom_call", output_to_operand_aliasing={{1}: (10, {})} | custom-call | flops 2415919104 | bytes 25165824 | tf_op jit(solution)/shard_map/unit_pairs/pallas_call | solution.py:240
  89.9 6.6 %last_pairs.1 = (bf16[1024,256]{1,0:T(8,128)(2,1)}, f32[16,256,256]{2,1,0:T(8,128)}) custom-call(s32[114]{0:T(128)S(1)} %concatenate.8.refs_0_, s32[128]{0:T(128)S(1)} %reshape.31.wins.refs_1_, bf16[1024,512]{1,0:T(8,128)(2,1)S(1)} %get-tuple-element.11.refs_2_, f32[1024,256]{1,0:T(8,128)S(1)} %get-tuple-element.16.refs_3_, ...), custom_call_target="tpu_custom_call", output_to_operand_aliasing={{1}: (8, {})} | custom-call | flops 805306368 | bytes 8388608 | tf_op jit(solution)/shard_map/last_pairs/pallas_call | solution.py:240
  (34 shorter events, 0.9 us)
Async XLA Ops:
  0.6 14.1 %collective-permute-start.6 = (bf16[1024,256]{1,0:T(8,128)(2,1)}, bf16[1024,256]{1,0:T(8,128)(2,1)S(1)}, u32[]{:S(2)}, u32[]{:S(2)}) collective-permute-start(bf16[1024,256]{1,0:T(8,128)(2,1)} %own_ref.1), channel_id=1, source_target_pairs={{0,4},{2,6},{4,0},{6,2},{8,12},{10,14},{12,8},{14,10},{16,20},{18,... | collective-permute-start | bytes 1572872 | tf_op jit(solution)/shard_map/ppermute | solution.py:38
  2.8 15.1 %collective-permute-start.4 = (bf16[1024,256]{1,0:T(8,128)(2,1)}, bf16[1024,256]{1,0:T(8,128)(2,1)S(1)}, u32[]{:S(2)}, u32[]{:S(2)}) collective-permute-start(bf16[1024,256]{1,0:T(8,128)(2,1)} %own_ref.1), channel_id=1, source_target_pairs={{0,2},{2,0},{4,6},{6,4},{8,10},{10,8},{12,14},{14,12},{16,18},{18,... | collective-permute-start | bytes 1572872 | tf_op jit(solution)/shard_map/ppermute | solution.py:38
  4.0 14.4 %collective-permute-start.10 = (bf16[1024,256]{1,0:T(8,128)(2,1)}, bf16[1024,256]{1,0:T(8,128)(2,1)}, u32[]{:S(2)}, u32[]{:S(2)}) collective-permute-start(bf16[1024,256]{1,0:T(8,128)(2,1)} %own_ref.1), channel_id=1, source_target_pairs={{2,10},{6,14},{8,0},{10,18},{12,4},{14,22},{16,8},{18,26},{20,12},... | collective-permute-start | bytes 1572872 | tf_op jit(solution)/shard_map/ppermute | solution.py:38
  5.3 36.7 %collective-permute-start.3 = (bf16[1024,256]{1,0:T(8,128)(2,1)}, bf16[1024,256]{1,0:T(8,128)(2,1)}, u32[]{:S(2)}, u32[]{:S(2)}) collective-permute-start(bf16[1024,256]{1,0:T(8,128)(2,1)} %own_ref.1), channel_id=1, source_target_pairs={{0,1},{1,0},{2,3},{3,2},{4,5},{5,4},{6,7},{7,6},{8,9},{9,8},{10,11... | collective-permute-start | bytes 1572872 | tf_op jit(solution)/shard_map/ppermute | solution.py:42
  14.7 27.3 %collective-permute-start.13 = (bf16[1024,256]{1,0:T(8,128)(2,1)S(1)}, bf16[1024,256]{1,0:T(8,128)(2,1)S(1)}, u32[]{:S(2)}, u32[]{:S(2)}) collective-permute-start(bf16[1024,256]{1,0:T(8,128)(2,1)S(1)} %collective-permute-done.6.refs_6_), channel_id=1, source_target_pairs={{0,8},{2,10},{8,16},{10,18},{12,4},{14,6},{16,24},{18,26},{20,12},... | collective-permute-start | bytes 1572872 | tf_op jit(solution)/shard_map/ppermute | solution.py:38
  17.9 24.8 %collective-permute-start.8 = (bf16[1024,256]{1,0:T(8,128)(2,1)S(1)}, bf16[1024,256]{1,0:T(8,128)(2,1)S(1)}, u32[]{:S(2)}, u32[]{:S(2)}) collective-permute-start(bf16[1024,256]{1,0:T(8,128)(2,1)S(1)} %collective-permute-done.4.refs_4_), channel_id=1, source_target_pairs={{0,4},{2,6},{4,0},{6,2},{8,12},{10,14},{12,8},{14,10},{16,20},{18,... | collective-permute-start | bytes 1572872 | tf_op jit(solution)/shard_map/ppermute | solution.py:38
  18.4 24.4 %collective-permute-start.11 = (bf16[1024,256]{1,0:T(8,128)(2,1)}, bf16[1024,256]{1,0:T(8,128)(2,1)S(1)}, u32[]{:S(2)}, u32[]{:S(2)}) collective-permute-start(bf16[1024,256]{1,0:T(8,128)(2,1)} %collective-permute-done.10), channel_id=1, source_target_pairs={{0,2},{2,0},{4,6},{6,4},{8,10},{10,8},{12,14},{14,12},{16,18},{18,... | collective-permute-start | bytes 1572872 | tf_op jit(solution)/shard_map/ppermute | solution.py:38
  20.1 8.9 %collective-permute-start = (s32[8,2]{0,1:T(2,128)S(1)}, s32[8,2]{0,1:T(2,128)S(1)}, u32[]{:S(2)}, u32[]{:S(2)}) collective-permute-start(s32[8,2]{0,1:T(2,128)S(1)} %get-tuple-element.22), channel_id=1, source_target_pairs={{0,6},{2,8},{4,10},{6,12},{8,14},{10,16},{12,18},{14,20},{16,22},{... | collective-permute-start | bytes 200 | tf_op jit(solution)/shard_map/ppermute | solution.py:38
  29.0 2.1 %collective-permute-start.1 = (s32[8,2]{0,1:T(2,128)S(1)}, s32[8,2]{0,1:T(2,128)S(1)}, u32[]{:S(2)}, u32[]{:S(2)}) collective-permute-start(s32[8,2]{0,1:T(2,128)S(1)} %get-tuple-element.21), channel_id=1, source_target_pairs={{0,4},{2,6},{4,8},{6,10},{8,12},{10,14},{12,16},{14,18},{16,20},{1... | collective-permute-start | bytes 200 | tf_op jit(solution)/shard_map/ppermute | solution.py:38
  31.1 6.2 %collective-permute-start.2 = (s32[8,2]{0,1:T(2,128)S(1)}, s32[8,2]{0,1:T(2,128)S(1)}, u32[]{:S(2)}, u32[]{:S(2)}) collective-permute-start(s32[8,2]{0,1:T(2,128)S(1)} %get-tuple-element.20), channel_id=1, source_target_pairs={{0,2},{2,4},{4,6},{6,8},{8,10},{10,12},{12,14},{14,16},{16,18},{18... | collective-permute-start | bytes 200 | tf_op jit(solution)/shard_map/ppermute | solution.py:38
  37.3 7.6 %collective-permute-start.5 = (bf16[1024,256]{1,0:T(8,128)(2,1)S(1)}, bf16[1024,256]{1,0:T(8,128)(2,1)S(1)}, u32[]{:S(2)}, u32[]{:S(2)}) collective-permute-start(bf16[1024,256]{1,0:T(8,128)(2,1)S(1)} %collective-permute-done.4.refs_4_), channel_id=1, source_target_pairs={{0,1},{1,0},{2,3},{3,2},{4,5},{5,4},{6,7},{7,6},{8,9},{9,8},{10,11... | collective-permute-start | bytes 1572872 | tf_op jit(solution)/shard_map/ppermute | solution.py:42
  41.9 5.1 %collective-permute-start.7 = (bf16[1024,256]{1,0:T(8,128)(2,1)S(1)}, bf16[1024,256]{1,0:T(8,128)(2,1)}, u32[]{:S(2)}, u32[]{:S(2)}) collective-permute-start(bf16[1024,256]{1,0:T(8,128)(2,1)S(1)} %collective-permute-done.6.refs_6_), channel_id=1, source_target_pairs={{0,1},{1,0},{2,3},{3,2},{4,5},{5,4},{6,7},{7,6},{8,9},{9,8},{10,11... | collective-permute-start | bytes 1572872 | tf_op jit(solution)/shard_map/ppermute | solution.py:42
  42.1 32.0 %collective-permute-start.14 = (bf16[1024,256]{1,0:T(8,128)(2,1)S(1)}, bf16[1024,256]{1,0:T(8,128)(2,1)}, u32[]{:S(2)}, u32[]{:S(2)}) collective-permute-start(bf16[1024,256]{1,0:T(8,128)(2,1)S(1)} %collective-permute-done.13.refs_8_), channel_id=1, source_target_pairs={{0,1},{1,0},{2,3},{3,2},{4,5},{5,4},{6,7},{7,6},{8,9},{9,8},{10,11... | collective-permute-start | bytes 1572872 | tf_op jit(solution)/shard_map/ppermute | solution.py:42
  42.6 31.4 %collective-permute-start.9 = (bf16[1024,256]{1,0:T(8,128)(2,1)S(1)}, bf16[1024,256]{1,0:T(8,128)(2,1)}, u32[]{:S(2)}, u32[]{:S(2)}) collective-permute-start(bf16[1024,256]{1,0:T(8,128)(2,1)S(1)} %collective-permute-done.8.refs_4_), channel_id=1, source_target_pairs={{0,1},{1,0},{2,3},{3,2},{4,5},{5,4},{6,7},{7,6},{8,9},{9,8},{10,11... | collective-permute-start | bytes 1572872 | tf_op jit(solution)/shard_map/ppermute | solution.py:42
  42.7 31.4 %collective-permute-start.12 = (bf16[1024,256]{1,0:T(8,128)(2,1)S(1)}, bf16[1024,256]{1,0:T(8,128)(2,1)}, u32[]{:S(2)}, u32[]{:S(2)}) collective-permute-start(bf16[1024,256]{1,0:T(8,128)(2,1)S(1)} %collective-permute-done.11.refs_6_), channel_id=1, source_target_pairs={{0,1},{1,0},{2,3},{3,2},{4,5},{5,4},{6,7},{7,6},{8,9},{9,8},{10,11... | collective-permute-start | bytes 1572872 | tf_op jit(solution)/shard_map/ppermute | solution.py:42
  45.0 15.3 %collective-permute-start.15 = (bf16[512,256]{1,0:T(8,128)(2,1)}, bf16[512,256]{1,0:T(8,128)(2,1)S(1)}, u32[]{:S(2)}, u32[]{:S(2)}) collective-permute-start(bf16[512,256]{1,0:T(8,128)(2,1)} %slice.23), channel_id=1, source_target_pairs={{0,2},{2,0},{4,6},{6,4},{8,10},{10,8},{12,14},{14,12},{16,18},{18,... | collective-permute-start | bytes 786440 | tf_op jit(solution)/shard_map/ppermute | solution.py:38
  47.0 15.1 %collective-permute-start.17 = (bf16[512,256]{1,0:T(8,128)(2,1)}, bf16[512,256]{1,0:T(8,128)(2,1)}, u32[]{:S(2)}, u32[]{:S(2)}) collective-permute-start(bf16[512,256]{1,0:T(8,128)(2,1)} %slice.24), channel_id=1, source_target_pairs={{0,8},{2,10},{8,16},{10,18},{12,4},{14,6},{16,24},{18,26},{20,12},... | collective-permute-start | bytes 786440 | tf_op jit(solution)/shard_map/ppermute | solution.py:38
  52.7 1.1 %copy-start = (bf16[1024,256]{1,0:T(8,128)(2,1)S(1)}, bf16[1024,256]{1,0:T(8,128)(2,1)}, u32[]{:S(2)}) copy-start(bf16[1024,256]{1,0:T(8,128)(2,1)} %own_ref.1) | copy-start | bytes 1572868
  60.3 29.5 %collective-permute-start.16 = (bf16[512,256]{1,0:T(8,128)(2,1)S(1)}, bf16[512,256]{1,0:T(8,128)(2,1)S(1)}, u32[]{:S(2)}, u32[]{:S(2)}) collective-permute-start(bf16[512,256]{1,0:T(8,128)(2,1)S(1)} %collective-permute-done.15.refs_4_), channel_id=1, source_target_pairs={{0,1},{1,0},{2,3},{3,2},{4,5},{5,4},{6,7},{7,6},{8,9},{9,8},{10,11... | collective-permute-start | bytes 786440 | tf_op jit(solution)/shard_map/ppermute | solution.py:42
  62.0 27.8 %collective-permute-start.18 = (bf16[512,256]{1,0:T(8,128)(2,1)}, bf16[512,256]{1,0:T(8,128)(2,1)S(1)}, u32[]{:S(2)}, u32[]{:S(2)}) collective-permute-start(bf16[512,256]{1,0:T(8,128)(2,1)} %collective-permute-done.17.refs_6_), channel_id=1, source_target_pairs={{0,1},{1,0},{2,3},{3,2},{4,5},{5,4},{6,7},{7,6},{8,9},{9,8},{10,11... | collective-permute-start | bytes 786440 | tf_op jit(solution)/shard_map/ppermute | solution.py:42

commit v2 on v1

v2 whole, which is shorter than its diff:
```python
import functools

import jax
import jax.numpy as jnp
from jax import lax
from jax.experimental import pallas as pl
from jax.experimental.pallas import tpu as pltpu
from jax.sharding import PartitionSpec as P

BS = 256
BLK_DEV = 4
CAP = 8
REACH = 3
QUAD = 4
EPS = 1e-05
STEP = 256
TABLE = 2 * CAP
VMEM = 24 * 1024 * 1024


def along_x(i, n):
    return i ^ 1


def along_y(i, n):
    return i ^ 2


def along_z_own(i, n):
    return (i - QUAD if i % 2 == 0 else i + QUAD) % n


def along_z_side(i, n):
    return (i + QUAD if i % QUAD < 2 else i - QUAD) % n


def send(value, move):
    length = lax.axis_size("feat")
    return lax.ppermute(value, "feat", [(i, move(i, length)) for i in range(length)])


def swap(value):
    return lax.ppermute(value, "samp", [(0, 1), (1, 0)])


def off_self(r):
    return 0 * r


def off_x(r):
    return 1 - 2 * lax.rem(r, 2)


def off_y(r):
    return 2 - 4 * lax.div(r, 2)


def off_diag(r):
    return 3 - 2 * r


def off_zx(r):
    return 6 * lax.rem(r, 2) - 3


def off_zy(r):
    return 4 * lax.div(r, 2) - 2


def off_last(r):
    return jnp.where(r == 0, -1, jnp.where(r == 1, -3, jnp.where(r == 2, 3, 1)))


def normalise(own_ref, par_ref, z_ref, start, rows):
    width = own_ref.shape[1]
    total = 2 * width
    for at in range(0, rows, STEP):
        a = own_ref[at : at + STEP, :].astype(jnp.float32)
        b = par_ref[at : at + STEP, :].astype(jnp.float32)
        mean = jnp.sum(a + b, axis=1, keepdims=True) / total
        var = jnp.sum(a * a + b * b, axis=1, keepdims=True) / total - mean * mean
        inv = lax.rsqrt(var + EPS)
        to = slice(start + at, start + at + STEP)
        z_ref[to, :width] = ((a - mean) * inv).astype(jnp.bfloat16)
        z_ref[to, width:] = ((b - mean) * inv).astype(jnp.bfloat16)


def slot_of(meta, wins, off, slot, code):
    position = meta[0]
    ahead = off >= 0
    at = 2 + (jnp.maximum(off, 0) * CAP + slot) * 2
    left = jnp.where(ahead, meta[at] - position * BLK_DEV, lax.div(code, BLK_DEV))
    right = jnp.where(ahead, meta[at + 1] - (position + off) * BLK_DEV, lax.rem(code, BLK_DEV))
    live = jnp.where(ahead, meta[at], code) >= 0
    live = jnp.logical_and(live, position + off >= 0)
    b = jnp.where(live, jnp.where(ahead, left, right), 0)
    o = jnp.where(live, jnp.where(ahead, right, left), 0)
    mine = position * BLK_DEV + b
    other = jnp.where(live, (position + off) * BLK_DEV + o, 0)
    lo_b = wins[2 * mine]
    hi_b = wins[2 * mine + 1]
    lo_o = wins[2 * other]
    hi_o = wins[2 * other + 1]
    meet = jnp.maximum(jnp.minimum(hi_b, hi_o) - jnp.maximum(lo_b, lo_o), 0)
    num = jnp.where(live, meet + 16, 0)
    den = hi_b - lo_b + hi_o - lo_o + 16
    return b, o, num, den


def codes_of(table, off):
    values = table.astype(jnp.float32)
    row = lax.broadcasted_iota(jnp.int32, values.shape, 0)
    lane = lax.broadcasted_iota(jnp.int32, values.shape, 1)
    first = jnp.where(off == -2, CAP, 0)
    column = jnp.where(off == -3, 1, 0)
    return [
        jnp.sum(
            jnp.where(jnp.logical_and(row == first + slot, lane == column), values, 0.0)
        ).astype(jnp.int32)
        for slot in range(CAP)
    ]


def scale_of(num, den, samples):
    top = jnp.full((1, BS), num, jnp.int32).astype(jnp.float32)
    low = jnp.full((1, BS), den, jnp.int32).astype(jnp.float32)
    return top / low / samples


def at_block(index):
    return pl.ds(pl.multiple_of(index * BS, BS), BS)


def grams(meta, wins, off, codes, zown_ref, z_ref, tile_ref):
    samples = zown_ref.shape[1]
    found = [slot_of(meta, wins, off, slot, codes[slot]) for slot in range(CAP)]
    for slot, (b, o, num, den) in enumerate(found):
        gram = lax.dot_general(
            zown_ref[at_block(b), :],
            z_ref[at_block(o), :],
            (((1,), (1,)), ((), ())),
            preferred_element_type=jnp.float32,
        )
        tile_ref[slot] = gram * scale_of(num, den, samples)
    return found


def products(found, zown_ref, z_ref, tile_ref, acc_ref, itself):
    width = acc_ref.shape[1]
    for slot, (b, o, _, _) in enumerate(found):
        tile = tile_ref[slot].astype(jnp.bfloat16)
        acc_ref[at_block(b), :] += jnp.dot(
            tile, z_ref[at_block(o), :width], preferred_element_type=jnp.float32
        )
        if itself:
            back = lax.dot_general(
                tile,
                zown_ref[at_block(b), :width],
                (((0,), (0,)), ((), ())),
                preferred_element_type=jnp.float32,
            )
            acc_ref[at_block(o), :] += back * jnp.where(b == o, 0.0, 1.0)


def put_tiles(meta, off, tile_ref, corr_ref, sem):
    mine = jnp.logical_and(off >= 0, lax.div(off, 2) == meta[1])
    first = jnp.where(jnp.logical_or(off == 1, off == 3), CAP, 0)
    copy = pltpu.make_async_copy(
        tile_ref, corr_ref.at[pl.ds(pl.multiple_of(first, CAP), CAP)], sem
    )

    @pl.when(mine)
    def _():
        copy.start()

    return mine, copy


def end_tiles(pending):
    mine, copy = pending

    @pl.when(mine)
    def _():
        copy.wait()


def self_kernel(meta, wins, own_ref, par_ref, zown_ref, acc_ref, corr_ref, tile_ref, sem):
    width = own_ref.shape[1]
    normalise(own_ref, par_ref, zown_ref, 0, own_ref.shape[0])
    found = grams(meta, wins, jnp.int32(0), [jnp.int32(-1)] * CAP, zown_ref, zown_ref, tile_ref)
    pending = put_tiles(meta, jnp.int32(0), tile_ref, corr_ref, sem)
    acc_ref[...] = zown_ref[:, :width].astype(jnp.float32)
    products(found, zown_ref, zown_ref, tile_ref, acc_ref, True)
    end_tiles(pending)


def unit_kernel(offs, pieces, *refs):
    count = len(offs)
    meta, wins, zown_ref, acc_in = refs[:4]
    raws = refs[4 : 4 + 2 * count * pieces]
    out_ref, corr_ref, acc_ref, z_ref, tile_ref, sems = refs[4 + 2 * count * pieces + 1 :]
    rows = acc_in.shape[0]
    acc_ref[...] = acc_in[...]
    r = lax.rem(meta[0], QUAD)
    pending = []
    for k, off_of in enumerate(offs):
        off = off_of(r)
        start = 0
        zs, tiles = z_ref.at[k], tile_ref.at[k]
        for piece in range(pieces):
            own_ref, par_ref = raws[2 * (k * pieces + piece) : 2 * (k * pieces + piece) + 2]
            count_rows = min(own_ref.shape[0], rows - start)
            normalise(own_ref, par_ref, zs, start, count_rows)
            start += count_rows
        table = own_ref[count_rows : count_rows + TABLE, :128]
        codes = codes_of(table, off)
        found = grams(meta, wins, off, codes, zown_ref, zs, tiles)
        pending.append(put_tiles(meta, off, tiles, corr_ref, sems.at[k]))
        products(found, zown_ref, zs, tiles, acc_ref, False)
    out_ref[...] = acc_ref[...].astype(out_ref.dtype)
    for one in pending:
        end_tiles(one)


def estimate(units):
    return pl.CostEstimate(
        flops=units * CAP * 2 * BS * BS * BS * 3, bytes_accessed=units * 8 * 2**20, transcendentals=0
    )


SMEM = pl.BlockSpec(memory_space=pltpu.SMEM)
INSIDE = pl.BlockSpec(memory_space=pltpu.VMEM)
ANY = pl.BlockSpec(memory_space=pl.ANY)


def run_self(meta, wins, own, par):
    rows, width = own.shape
    return pl.pallas_call(
        self_kernel,
        out_shape=(
            jax.ShapeDtypeStruct((rows, 2 * width), jnp.bfloat16),
            jax.ShapeDtypeStruct((rows, width), jnp.float32),
            jax.ShapeDtypeStruct((2 * CAP, BS, BS), jnp.float32),
        ),
        in_specs=[SMEM, SMEM, INSIDE, INSIDE],
        out_specs=(INSIDE, INSIDE, ANY),
        scratch_shapes=[pltpu.VMEM((CAP, BS, BS), jnp.float32), pltpu.SemaphoreType.DMA],
        compiler_params=pltpu.CompilerParams(vmem_limit_bytes=VMEM),
        cost_estimate=estimate(1),
        name="self_pairs",
    )(meta, wins, own, par)


def run_units(meta, wins, zown, acc, corr, offs, raws, pieces=1, final=False):
    rows, width = acc.shape
    count = len(offs)
    return pl.pallas_call(
        functools.partial(unit_kernel, offs, pieces),
        out_shape=(
            jax.ShapeDtypeStruct((rows, width), jnp.bfloat16 if final else jnp.float32),
            jax.ShapeDtypeStruct(corr.shape, corr.dtype),
        ),
        in_specs=[SMEM, SMEM, INSIDE, INSIDE] + [INSIDE] * len(raws) + [ANY],
        out_specs=(INSIDE, ANY),
        scratch_shapes=[
            pltpu.VMEM((rows, width), jnp.float32),
            pltpu.VMEM((count, rows, 2 * width), jnp.bfloat16),
            pltpu.VMEM((count, CAP, BS, BS), jnp.float32),
            pltpu.SemaphoreType.DMA((count,)),
        ],
        input_output_aliases={4 + len(raws): 1},
        compiler_params=pltpu.CompilerParams(vmem_limit_bytes=VMEM),
        cost_estimate=estimate(count),
        name="last_pairs" if final else "unit_pairs",
    )(meta, wins, zown, acc, *raws, corr)


def with_table(spectra, pair_blocks, position):
    first = pair_blocks[:, :1] - position * BLK_DEV
    group = lax.broadcasted_iota(jnp.int32, first.shape, 0) // CAP
    second = pair_blocks[:, 1:] - (position + group) * BLK_DEV
    code = jnp.where(pair_blocks[:, :1] >= 0, first * BLK_DEV + second, -1).astype(spectra.dtype)
    width = spectra.shape[1]
    near = jnp.pad(code[CAP : 3 * CAP], ((0, 0), (0, width - 1)))
    far = jnp.pad(code[3 * CAP :], ((0, CAP), (1, width - 2)))
    return jnp.concatenate([spectra, near + far], axis=0)


def body(spectra, pair_blocks, windows):
    hold = lax.optimization_barrier
    position = lax.axis_index("feat")
    half = spectra.shape[0] // 2
    par = swap(spectra)
    unit = with_table(spectra, pair_blocks, position)
    from_y = send(unit, along_y)
    from_x = send(unit, along_x)
    from_z = send(unit, along_z_own)
    ids = jnp.stack([position, lax.axis_index("samp")]).astype(jnp.int32)
    meta = jnp.concatenate([ids, pair_blocks.reshape(-1)])
    wins = windows.reshape(-1)
    zown, acc, corr = run_self(meta, wins, spectra, par)
    from_x, from_y, acc = hold((from_x, from_y, acc))
    diag = send(from_x, along_y)
    zy = send(from_y, along_z_side)
    from_z, acc = hold((from_z, acc))
    zx = send(from_z, along_x)
    raws = (from_x, swap(from_x), from_y, swap(from_y))
    acc, corr = run_units(meta, wins, zown, acc, corr, (off_x, off_y), raws)
    diag, acc = hold((diag, acc))
    last_a = send(diag[:half], along_z_side)
    zy, zx, acc = hold((zy, zx, acc))
    last_b = send(zy[half:], along_x)
    raws = (diag, swap(diag), zy, swap(zy), zx, swap(zx))
    acc, corr = run_units(meta, wins, zown, acc, corr, (off_diag, off_zy, off_zx), raws)
    last_a, last_b, acc = hold((last_a, last_b, acc))
    raws = (last_a, swap(last_a), last_b, swap(last_b))
    profiles, corr = run_units(meta, wins, zown, acc, corr, (off_last,), raws, 2, True)
    return (corr, profiles)


def solution(mesh):
    placed = (P("feat", "samp"), P("feat", None), P())
    return jax.shard_map(
        body,
        mesh=mesh,
        in_specs=placed,
        out_specs=(P(("feat", "samp"), None, None), P("feat", "samp")),
        check_vma=False,
    )
```

time: 97 us -> 56.4 us (0.58)
  Pallas kernels: 40.9 us -> 16.6 us
  starting transfers between devices: 35 us -> 17 us
  local copies, waits for them, and re-layouts: 5.78 us -> 3.02 us
  waiting for transfers between devices: 14 us -> 16.4 us
  other arithmetic: 0.09 us -> 2.01 us
    pallas_call x3, Pallas kernels: 34.3 us -> 13.8 us  [run_units(): pl.pallas_call(functools.partial(unit_kernel, offs, pieces), out_shape=(j...]
    ppermute x11 -> x8, starting transfers between devices: 26.2 us -> 11.5 us  [send(): lax.ppermute(value, 'feat', [(i, move(i, length)) for i in range(length)])]
    pallas_call x1, Pallas kernels: 6.58 us -> 2.75 us  [run_self(): pl.pallas_call(self_kernel, out_shape=(jax.ShapeDtypeStruct((rows, 2 * wi...]
    ppermute x8, starting transfers between devices: 8.77 us -> 5.45 us  [swap(): return lax.ppermute(value, 'samp', [(0, 1), (1, 0)])]
    ppermute x8, waiting for transfers between devices: 0.02 us -> 2.61 us  [swap(): return lax.ppermute(value, 'samp', [(0, 1), (1, 0)])]
    slice x3 -> x4, local copies, waits for them, and re-layouts: 2.31 us -> 0.04 us  [the longest x1 0.02 us: body(): last_b = send(zy[half:], along_x)]
    concatenate x1 -> x2, other arithmetic: 0.08 us -> 1.16 us  [the longest x1 1.08 us: with_table(): return jnp.concatenate([spectra, near + far], axis=0)]
    ppermute x11 -> x8, waiting for transfers between devices: 14 us -> 13.8 us  [send(): lax.ppermute(value, 'feat', [(i, move(i, length)) for i in range(length)])]
  transfers between devices with their start and end apart: 19 -> 16, of which waited for: 4 -> 9; matrix products, arithmetic and copies ran while one was open for 5% -> 7% of each run, Pallas kernels for 35% -> 24%
where the time goes in v2:
time: 56.4 us; the launch traced here: 55.8 us
  starting transfers between devices  17 us (30%)
  Pallas kernels  16.6 us (29%)
  waiting for transfers between devices  16.4 us (29%)
  local copies, waits for them, and re-layouts  3.02 us (5%)
  other arithmetic  2.01 us (4%)
  between operations  0.87 us (2%)
    pallas_call x3, Pallas kernels, run_units(): pl.pallas_call(functools.partial(unit_kernel, offs, pieces), out_shape=(j...  13.8 us
    ppermute x8, waiting for transfers between devices, send(): lax.ppermute(value, 'feat', [(i, move(i, length)) for i in range(length)])  13.8 us
    ppermute x8, starting transfers between devices, send(): lax.ppermute(value, 'feat', [(i, move(i, length)) for i in range(length)])  11.5 us
    ppermute x8, starting transfers between devices, swap(): return lax.ppermute(value, 'samp', [(0, 1), (1, 0)])  5.45 us
    pallas_call x1, Pallas kernels, run_self(): pl.pallas_call(self_kernel, out_shape=(jax.ShapeDtypeStruct((rows, 2 * wi...  2.75 us
    ppermute x8, waiting for transfers between devices, swap(): return lax.ppermute(value, 'samp', [(0, 1), (1, 0)])  2.61 us
    unnamed x4, local copies, waits for them, and re-layouts  2.58 us
  transfers between devices with their start and end apart: 16, of which 9 were waited for; matrix products, arithmetic and copies ran while one was open for 7% of the time, Pallas kernels for 24%

profile of v2, /device:TPU:1, one launch (start us, length us, event | category | flops | bytes accessed | tf_op | source)
XLA Modules:
  0.0 55.8 jit_solution(3770024435879766456)
XLA Ops:
  0.6 0.1 collective-permute-start
  0.8 0.8 %compare_select_fusion = s32[32,1]{0,1:T(1,128)S(1)} fusion(s32[32,1]{0,1:T(1,128)S(1)} %copy.28, s32[32,2]{0,1:T(2,128)} %param.4, s32[]{:T(128)S(6)} %mul.17), kind=kLoop, calls=%fused_computation.11 | loop fusion | flops 192 | bytes 516 | tf_op jit(solution)/shard_map/jit(_where)/select_n | solution.py:282
  1.8 1.1 %pad_maximum_fusion = bf16[1040,256]{1,0:T(8,128)(2,1)S(1)} fusion(bf16[16,256]{1,0:T(8,128)(2,1)S(1)} %pad_add_fusion, bf16[1024,256]{1,0:T(8,128)(2,1)} %own_ref.1), kind=kLoop, calls=%fused_computation | loop fusion | flops 1064960 | bytes 1064960 | tf_op jit(solution)/shard_map/concatenate | solution.py:286
  2.9 2.7 %collective-permute-start.1 = (bf16[1040,256]{1,0:T(8,128)(2,1)S(1)}, bf16[1040,256]{1,0:T(8,128)(2,1)S(1)}, u32[]{:S(2)}, u32[]{:S(2)}) collective-permute-start(bf16[1040,256]{1,0:T(8,128)(2,1)S(1)} %pad_maximum_fusion), channel_id=1, source_target_pairs={{0,2},{2,0},{4,6},{6,4},{8,10},{10,8},{12,14},{14,12},{16,18},{18,... | collective-permute-start | bytes 1597448 | tf_op jit(solution)/shard_map/ppermute | solution.py:39
  5.6 1.2 %collective-permute-start.2 = (bf16[1040,256]{1,0:T(8,128)(2,1)S(1)}, bf16[1040,256]{1,0:T(8,128)(2,1)S(1)}, u32[]{:S(2)}, u32[]{:S(2)}) collective-permute-start(bf16[1040,256]{1,0:T(8,128)(2,1)S(1)} %pad_maximum_fusion), channel_id=1, source_target_pairs={{0,4},{2,6},{4,0},{6,2},{8,12},{10,14},{12,8},{14,10},{16,20},{18,... | collective-permute-start | bytes 1597448 | tf_op jit(solution)/shard_map/ppermute | solution.py:39
  6.8 3.3 %collective-permute-start.4 = (bf16[1040,256]{1,0:T(8,128)(2,1)S(1)}, bf16[1040,256]{1,0:T(8,128)(2,1)S(1)}, u32[]{:S(2)}, u32[]{:S(2)}) collective-permute-start(bf16[1040,256]{1,0:T(8,128)(2,1)S(1)} %pad_maximum_fusion), channel_id=1, source_target_pairs={{0,24},{2,10},{4,28},{6,14},{8,0},{10,18},{12,4},{14,22},{16,8},{1... | collective-permute-start | bytes 1597448 | tf_op jit(solution)/shard_map/ppermute | solution.py:39
  10.2 0.8 %copy.24 = s32[32,2]{1,0:T(8,128)S(1)} copy(s32[32,2]{0,1:T(2,128)} %param.4) | data formatting | bytes 512 | tf_op args[1]
  11.0 0.8 %copy.25 = s32[64,2]{1,0:T(8,128)S(1)} copy(s32[64,2]{0,1:T(2,128)} %param.5) | data formatting | bytes 1024 | tf_op args[2]
  11.8 0.1 reshape.77.wins.refs_1_
  12.0 1.0 %copy-done = bf16[1024,256]{1,0:T(8,128)(2,1)S(1)} copy-done((bf16[1024,256]{1,0:T(8,128)(2,1)S(1)}, bf16[1024,256]{1,0:T(8,128)(2,1)}, u32[]{:S(2)}) %copy-start) | copy-done | bytes 524312
  13.1 2.7 %self_pairs.1 = (bf16[1024,512]{1,0:T(8,128)(2,1)S(1)}, f32[1024,256]{1,0:T(8,128)S(1)}, f32[16,256,256]{2,1,0:T(8,128)}) custom-call(s32[66]{0:T(128)S(1)} %pad_add_fusion.1.meta.refs_0_, s32[128]{0:T(128)S(1)} %reshape.77.wins.refs_1_, bf16[1024,256]{1,0:T(8,128)(2,1)S(1)} %copy-done, bf16[1024,256]{1,0:T(8,128)(2,1)S(1)} %collective-permute-done.par_ref), custom_call_target="tpu_custom_call" | custom-call | flops 805306368 | bytes 8388608 | tf_op jit(solution)/shard_map/self_pairs/pallas_call | solution.py:238
  15.8 2.2 %collective-permute-done.1.refs_4_ = bf16[1040,256]{1,0:T(8,128)(2,1)S(1)} collective-permute-done((bf16[1040,256]{1,0:T(8,128)(2,1)S(1)}, bf16[1040,256]{1,0:T(8,128)(2,1)S(1)}, u32[]{:S(2)}, u32[]{:S(2)}) %collective-permute-start.1) | collective-permute-done | bytes 532512 | tf_op jit(solution)/shard_map/ppermute | solution.py:39
  18.0 0.9 %collective-permute-done.2.refs_6_ = bf16[1040,256]{1,0:T(8,128)(2,1)S(1)} collective-permute-done((bf16[1040,256]{1,0:T(8,128)(2,1)S(1)}, bf16[1040,256]{1,0:T(8,128)(2,1)S(1)}, u32[]{:S(2)}, u32[]{:S(2)}) %collective-permute-start.2) | collective-permute-done | bytes 532512 | tf_op jit(solution)/shard_map/ppermute | solution.py:39
  19.0 1.1 %collective-permute-start.5 = (bf16[1040,256]{1,0:T(8,128)(2,1)S(1)}, bf16[1040,256]{1,0:T(8,128)(2,1)S(1)}, u32[]{:S(2)}, u32[]{:S(2)}) collective-permute-start(bf16[1040,256]{1,0:T(8,128)(2,1)S(1)} %collective-permute-done.1.refs_4_), channel_id=1, source_target_pairs={{0,1},{1,0},{2,3},{3,2},{4,5},{5,4},{6,7},{7,6},{8,9},{9,8},{10,11... | collective-permute-start | bytes 1597448 | tf_op jit(solution)/shard_map/ppermute | solution.py:43
  20.1 1.2 %collective-permute-start.3 = (bf16[1040,256]{1,0:T(8,128)(2,1)S(1)}, bf16[1040,256]{1,0:T(8,128)(2,1)S(1)}, u32[]{:S(2)}, u32[]{:S(2)}) collective-permute-start(bf16[1040,256]{1,0:T(8,128)(2,1)S(1)} %collective-permute-done.1.refs_4_), channel_id=1, source_target_pairs={{0,4},{2,6},{4,0},{6,2},{8,12},{10,14},{12,8},{14,10},{16,20},{18,... | collective-permute-start | bytes 1597448 | tf_op jit(solution)/shard_map/ppermute | solution.py:39
  21.4 0.7 %collective-permute-start.9 = (bf16[1040,256]{1,0:T(8,128)(2,1)S(1)}, bf16[1040,256]{1,0:T(8,128)(2,1)S(1)}, u32[]{:S(2)}, u32[]{:S(2)}) collective-permute-start(bf16[1040,256]{1,0:T(8,128)(2,1)S(1)} %collective-permute-done.4), channel_id=1, source_target_pairs={{0,2},{2,0},{4,6},{6,4},{8,10},{10,8},{12,14},{14,12},{16,18},{18,... | collective-permute-start | bytes 1597448 | tf_op jit(solution)/shard_map/ppermute | solution.py:39
  22.1 0.8 %collective-permute-start.8 = (bf16[1040,256]{1,0:T(8,128)(2,1)S(1)}, bf16[1040,256]{1,0:T(8,128)(2,1)S(1)}, u32[]{:S(2)}, u32[]{:S(2)}) collective-permute-start(bf16[1040,256]{1,0:T(8,128)(2,1)S(1)} %collective-permute-done.2.refs_6_), channel_id=1, source_target_pairs={{0,8},{2,10},{4,28},{6,30},{8,16},{10,18},{12,4},{14,6},{16,24},{1... | collective-permute-start | bytes 1597448 | tf_op jit(solution)/shard_map/ppermute | solution.py:39
  22.9 5.0 %unit_pairs.2 = (f32[1024,256]{1,0:T(8,128)S(1)}, f32[16,256,256]{2,1,0:T(8,128)}) custom-call(s32[66]{0:T(128)S(1)} %pad_add_fusion.1.meta.refs_0_, s32[128]{0:T(128)S(1)} %reshape.77.wins.refs_1_, bf16[1024,512]{1,0:T(8,128)(2,1)S(1)} %get-tuple-element.24.refs_2_, f32[1024,256]{1,0:T(8,128)S(1)} %get-tuple-element.28.refs_3_, ...), custom_call_target="tpu_custom_call", output_to_operand_aliasing={{1}: (8, {})} | custom-call | flops 1610612736 | bytes 16777216 | tf_op jit(solution)/shard_map/unit_pairs/pallas_call | solution.py:257
  27.9 5.4 %collective-permute-done.3.refs_4_ = bf16[1040,256]{1,0:T(8,128)(2,1)S(1)} collective-permute-done((bf16[1040,256]{1,0:T(8,128)(2,1)S(1)}, bf16[1040,256]{1,0:T(8,128)(2,1)S(1)}, u32[]{:S(2)}, u32[]{:S(2)}) %collective-permute-start.3) | collective-permute-done | bytes 532512 | tf_op jit(solution)/shard_map/ppermute | solution.py:39
  33.3 0.6 %collective-permute-done.9.refs_8_ = bf16[1040,256]{1,0:T(8,128)(2,1)S(1)} collective-permute-done((bf16[1040,256]{1,0:T(8,128)(2,1)S(1)}, bf16[1040,256]{1,0:T(8,128)(2,1)S(1)}, u32[]{:S(2)}, u32[]{:S(2)}) %collective-permute-start.9) | collective-permute-done | bytes 532512 | tf_op jit(solution)/shard_map/ppermute | solution.py:39
  33.8 2.0 %collective-permute-done.8.refs_6_ = bf16[1040,256]{1,0:T(8,128)(2,1)S(1)} collective-permute-done((bf16[1040,256]{1,0:T(8,128)(2,1)S(1)}, bf16[1040,256]{1,0:T(8,128)(2,1)S(1)}, u32[]{:S(2)}, u32[]{:S(2)}) %collective-permute-start.8) | collective-permute-done | bytes 532512 | tf_op jit(solution)/shard_map/ppermute | solution.py:39
  35.8 2.6 %collective-permute-start.12 = (bf16[1040,256]{1,0:T(8,128)(2,1)S(1)}, bf16[1040,256]{1,0:T(8,128)(2,1)S(1)}, u32[]{:S(2)}, u32[]{:S(2)}) collective-permute-start(bf16[1040,256]{1,0:T(8,128)(2,1)S(1)} %collective-permute-done.8.refs_6_), channel_id=1, source_target_pairs={{0,1},{1,0},{2,3},{3,2},{4,5},{5,4},{6,7},{7,6},{8,9},{9,8},{10,11... | collective-permute-start | bytes 1597448 | tf_op jit(solution)/shard_map/ppermute | solution.py:43
  38.4 0.5 collective-permute-start.11
  38.9 1.2 %collective-permute-start.10 = (bf16[528,256]{1,0:T(8,128)(2,1)S(1)}, bf16[528,256]{1,0:T(8,128)(2,1)S(1)}, u32[]{:S(2)}, u32[]{:S(2)}) collective-permute-start(bf16[528,256]{1,0:T(8,128)(2,1)S(1)} %slice.24), channel_id=1, source_target_pairs={{0,2},{2,0},{4,6},{6,4},{8,10},{10,8},{12,14},{14,12},{16,18},{18,... | collective-permute-start | bytes 811016 | tf_op jit(solution)/shard_map/ppermute | solution.py:39
  40.2 0.2 collective-permute-start.7
  40.4 0.3 collective-permute-done.13.refs_9_
  40.7 0.8 %collective-permute-done.11.refs_5_ = bf16[1040,256]{1,0:T(8,128)(2,1)S(1)} collective-permute-done((bf16[1040,256]{1,0:T(8,128)(2,1)S(1)}, bf16[1040,256]{1,0:T(8,128)(2,1)S(1)}, u32[]{:S(2)}, u32[]{:S(2)}) %collective-permute-start.11) | collective-permute-done | bytes 532512 | tf_op jit(solution)/shard_map/ppermute | solution.py:43
  41.5 5.7 %unit_pairs.3 = (f32[1024,256]{1,0:T(8,128)S(1)}, f32[16,256,256]{2,1,0:T(8,128)}) custom-call(s32[66]{0:T(128)S(1)} %pad_add_fusion.1.meta.refs_0_, s32[128]{0:T(128)S(1)} %reshape.77.wins.refs_1_, bf16[1024,512]{1,0:T(8,128)(2,1)S(1)} %get-tuple-element.24.refs_2_, f32[1024,256]{1,0:T(8,128)S(1)} %get-tuple-element.36.refs_3_, ...), custom_call_target="tpu_custom_call", output_to_operand_aliasing={{1}: (10, {})} | custom-call | flops 2415919104 | bytes 25165824 | tf_op jit(solution)/shard_map/unit_pairs/pallas_call | solution.py:257
  47.2 2.6 %collective-permute-done.7.refs_4_ = bf16[512,256]{1,0:T(8,128)(2,1)S(1)} collective-permute-done((bf16[512,256]{1,0:T(8,128)(2,1)S(1)}, bf16[512,256]{1,0:T(8,128)(2,1)S(1)}, u32[]{:S(2)}, u32[]{:S(2)}) %collective-permute-start.7) | collective-permute-done | bytes 262176 | tf_op jit(solution)/shard_map/ppermute | solution.py:39
  49.8 1.1 %collective-permute-start.15 = (bf16[528,256]{1,0:T(8,128)(2,1)S(1)}, bf16[528,256]{1,0:T(8,128)(2,1)S(1)}, u32[]{:S(2)}, u32[]{:S(2)}) collective-permute-start(bf16[528,256]{1,0:T(8,128)(2,1)S(1)} %collective-permute-done.10.refs_6_), channel_id=1, source_target_pairs={{0,1},{1,0},{2,3},{3,2},{4,5},{5,4},{6,7},{7,6},{8,9},{9,8},{10,11... | collective-permute-start | bytes 811016 | tf_op jit(solution)/shard_map/ppermute | solution.py:43
  50.9 1.5 %collective-permute-done.14.refs_5_ = bf16[512,256]{1,0:T(8,128)(2,1)S(1)} collective-permute-done((bf16[512,256]{1,0:T(8,128)(2,1)S(1)}, bf16[512,256]{1,0:T(8,128)(2,1)S(1)}, u32[]{:S(2)}, u32[]{:S(2)}) %collective-permute-start.14) | collective-permute-done | bytes 262176 | tf_op jit(solution)/shard_map/ppermute | solution.py:43
  52.5 3.2 %last_pairs.1 = (bf16[1024,256]{1,0:T(8,128)(2,1)}, f32[16,256,256]{2,1,0:T(8,128)}) custom-call(s32[66]{0:T(128)S(1)} %pad_add_fusion.1.meta.refs_0_, s32[128]{0:T(128)S(1)} %reshape.77.wins.refs_1_, bf16[1024,512]{1,0:T(8,128)(2,1)S(1)} %get-tuple-element.24.refs_2_, f32[1024,256]{1,0:T(8,128)S(1)} %get-tuple-element.40.refs_3_, ...), custom_call_target="tpu_custom_call", output_to_operand_aliasing={{1}: (8, {})} | custom-call | flops 805306368 | bytes 8388608 | tf_op jit(solution)/shard_map/last_pairs/pallas_call | solution.py:257
  (22 shorter events, 0.5 us)
Async XLA Ops:
  0.6 11.4 %collective-permute-start = (bf16[1024,256]{1,0:T(8,128)(2,1)}, bf16[1024,256]{1,0:T(8,128)(2,1)S(1)}, u32[]{:S(2)}, u32[]{:S(2)}) collective-permute-start(bf16[1024,256]{1,0:T(8,128)(2,1)} %own_ref.1), channel_id=1, source_target_pairs={{0,1},{1,0},{2,3},{3,2},{4,5},{5,4},{6,7},{7,6},{8,9},{9,8},{10,11... | collective-permute-start | bytes 1572872 | tf_op jit(solution)/shard_map/ppermute | solution.py:43
  2.9 15.2 %collective-permute-start.1 = (bf16[1040,256]{1,0:T(8,128)(2,1)S(1)}, bf16[1040,256]{1,0:T(8,128)(2,1)S(1)}, u32[]{:S(2)}, u32[]{:S(2)}) collective-permute-start(bf16[1040,256]{1,0:T(8,128)(2,1)S(1)} %pad_maximum_fusion), channel_id=1, source_target_pairs={{0,2},{2,0},{4,6},{6,4},{8,10},{10,8},{12,14},{14,12},{16,18},{18,... | collective-permute-start | bytes 1597448 | tf_op jit(solution)/shard_map/ppermute | solution.py:39
  5.6 13.4 %collective-permute-start.2 = (bf16[1040,256]{1,0:T(8,128)(2,1)S(1)}, bf16[1040,256]{1,0:T(8,128)(2,1)S(1)}, u32[]{:S(2)}, u32[]{:S(2)}) collective-permute-start(bf16[1040,256]{1,0:T(8,128)(2,1)S(1)} %pad_maximum_fusion), channel_id=1, source_target_pairs={{0,4},{2,6},{4,0},{6,2},{8,12},{10,14},{12,8},{14,10},{16,20},{18,... | collective-permute-start | bytes 1597448 | tf_op jit(solution)/shard_map/ppermute | solution.py:39
  6.8 14.5 %collective-permute-start.4 = (bf16[1040,256]{1,0:T(8,128)(2,1)S(1)}, bf16[1040,256]{1,0:T(8,128)(2,1)S(1)}, u32[]{:S(2)}, u32[]{:S(2)}) collective-permute-start(bf16[1040,256]{1,0:T(8,128)(2,1)S(1)} %pad_maximum_fusion), channel_id=1, source_target_pairs={{0,24},{2,10},{4,28},{6,14},{8,0},{10,18},{12,4},{14,22},{16,8},{1... | collective-permute-start | bytes 1597448 | tf_op jit(solution)/shard_map/ppermute | solution.py:39
  12.0 1.0 %copy-start = (bf16[1024,256]{1,0:T(8,128)(2,1)S(1)}, bf16[1024,256]{1,0:T(8,128)(2,1)}, u32[]{:S(2)}) copy-start(bf16[1024,256]{1,0:T(8,128)(2,1)} %own_ref.1) | copy-start | bytes 1572868
  19.0 3.9 %collective-permute-start.5 = (bf16[1040,256]{1,0:T(8,128)(2,1)S(1)}, bf16[1040,256]{1,0:T(8,128)(2,1)S(1)}, u32[]{:S(2)}, u32[]{:S(2)}) collective-permute-start(bf16[1040,256]{1,0:T(8,128)(2,1)S(1)} %collective-permute-done.1.refs_4_), channel_id=1, source_target_pairs={{0,1},{1,0},{2,3},{3,2},{4,5},{5,4},{6,7},{7,6},{8,9},{9,8},{10,11... | collective-permute-start | bytes 1597448 | tf_op jit(solution)/shard_map/ppermute | solution.py:43
  20.1 2.8 %collective-permute-start.6 = (bf16[1040,256]{1,0:T(8,128)(2,1)S(1)}, bf16[1040,256]{1,0:T(8,128)(2,1)S(1)}, u32[]{:S(2)}, u32[]{:S(2)}) collective-permute-start(bf16[1040,256]{1,0:T(8,128)(2,1)S(1)} %collective-permute-done.2.refs_6_), channel_id=1, source_target_pairs={{0,1},{1,0},{2,3},{3,2},{4,5},{5,4},{6,7},{7,6},{8,9},{9,8},{10,11... | collective-permute-start | bytes 1597448 | tf_op jit(solution)/shard_map/ppermute | solution.py:43
  20.1 13.2 %collective-permute-start.3 = (bf16[1040,256]{1,0:T(8,128)(2,1)S(1)}, bf16[1040,256]{1,0:T(8,128)(2,1)S(1)}, u32[]{:S(2)}, u32[]{:S(2)}) collective-permute-start(bf16[1040,256]{1,0:T(8,128)(2,1)S(1)} %collective-permute-done.1.refs_4_), channel_id=1, source_target_pairs={{0,4},{2,6},{4,0},{6,2},{8,12},{10,14},{12,8},{14,10},{16,20},{18,... | collective-permute-start | bytes 1597448 | tf_op jit(solution)/shard_map/ppermute | solution.py:39
  21.4 12.5 %collective-permute-start.9 = (bf16[1040,256]{1,0:T(8,128)(2,1)S(1)}, bf16[1040,256]{1,0:T(8,128)(2,1)S(1)}, u32[]{:S(2)}, u32[]{:S(2)}) collective-permute-start(bf16[1040,256]{1,0:T(8,128)(2,1)S(1)} %collective-permute-done.4), channel_id=1, source_target_pairs={{0,2},{2,0},{4,6},{6,4},{8,10},{10,8},{12,14},{14,12},{16,18},{18,... | collective-permute-start | bytes 1597448 | tf_op jit(solution)/shard_map/ppermute | solution.py:39
  22.1 13.7 %collective-permute-start.8 = (bf16[1040,256]{1,0:T(8,128)(2,1)S(1)}, bf16[1040,256]{1,0:T(8,128)(2,1)S(1)}, u32[]{:S(2)}, u32[]{:S(2)}) collective-permute-start(bf16[1040,256]{1,0:T(8,128)(2,1)S(1)} %collective-permute-done.2.refs_6_), channel_id=1, source_target_pairs={{0,8},{2,10},{4,28},{6,30},{8,16},{10,18},{12,4},{14,6},{16,24},{1... | collective-permute-start | bytes 1597448 | tf_op jit(solution)/shard_map/ppermute | solution.py:39
  35.8 4.6 %collective-permute-start.12 = (bf16[1040,256]{1,0:T(8,128)(2,1)S(1)}, bf16[1040,256]{1,0:T(8,128)(2,1)S(1)}, u32[]{:S(2)}, u32[]{:S(2)}) collective-permute-start(bf16[1040,256]{1,0:T(8,128)(2,1)S(1)} %collective-permute-done.8.refs_6_), channel_id=1, source_target_pairs={{0,1},{1,0},{2,3},{3,2},{4,5},{5,4},{6,7},{7,6},{8,9},{9,8},{10,11... | collective-permute-start | bytes 1597448 | tf_op jit(solution)/shard_map/ppermute | solution.py:43
  38.4 2.3 %collective-permute-start.13 = (bf16[1040,256]{1,0:T(8,128)(2,1)S(1)}, bf16[1040,256]{1,0:T(8,128)(2,1)S(1)}, u32[]{:S(2)}, u32[]{:S(2)}) collective-permute-start(bf16[1040,256]{1,0:T(8,128)(2,1)S(1)} %collective-permute-done.9.refs_8_), channel_id=1, source_target_pairs={{0,1},{1,0},{2,3},{3,2},{4,5},{5,4},{6,7},{7,6},{8,9},{9,8},{10,11... | collective-permute-start | bytes 1597448 | tf_op jit(solution)/shard_map/ppermute | solution.py:43
  38.4 3.1 %collective-permute-start.11 = (bf16[1040,256]{1,0:T(8,128)(2,1)S(1)}, bf16[1040,256]{1,0:T(8,128)(2,1)S(1)}, u32[]{:S(2)}, u32[]{:S(2)}) collective-permute-start(bf16[1040,256]{1,0:T(8,128)(2,1)S(1)} %collective-permute-done.3.refs_4_), channel_id=1, source_target_pairs={{0,1},{1,0},{2,3},{3,2},{4,5},{5,4},{6,7},{7,6},{8,9},{9,8},{10,11... | collective-permute-start | bytes 1597448 | tf_op jit(solution)/shard_map/ppermute | solution.py:43
  38.9 10.9 %collective-permute-start.10 = (bf16[528,256]{1,0:T(8,128)(2,1)S(1)}, bf16[528,256]{1,0:T(8,128)(2,1)S(1)}, u32[]{:S(2)}, u32[]{:S(2)}) collective-permute-start(bf16[528,256]{1,0:T(8,128)(2,1)S(1)} %slice.24), channel_id=1, source_target_pairs={{0,2},{2,0},{4,6},{6,4},{8,10},{10,8},{12,14},{14,12},{16,18},{18,... | collective-permute-start | bytes 811016 | tf_op jit(solution)/shard_map/ppermute | solution.py:39
  40.2 9.6 %collective-permute-start.7 = (bf16[512,256]{1,0:T(8,128)(2,1)S(1)}, bf16[512,256]{1,0:T(8,128)(2,1)S(1)}, u32[]{:S(2)}, u32[]{:S(2)}) collective-permute-start(bf16[512,256]{1,0:T(8,128)(2,1)S(1)} %slice.23), channel_id=1, source_target_pairs={{0,8},{2,10},{4,28},{6,30},{8,16},{10,18},{12,4},{14,6},{16,24},{1... | collective-permute-start | bytes 786440 | tf_op jit(solution)/shard_map/ppermute | solution.py:39
  49.8 2.7 %collective-permute-start.15 = (bf16[528,256]{1,0:T(8,128)(2,1)S(1)}, bf16[528,256]{1,0:T(8,128)(2,1)S(1)}, u32[]{:S(2)}, u32[]{:S(2)}) collective-permute-start(bf16[528,256]{1,0:T(8,128)(2,1)S(1)} %collective-permute-done.10.refs_6_), channel_id=1, source_target_pairs={{0,1},{1,0},{2,3},{3,2},{4,5},{5,4},{6,7},{7,6},{8,9},{9,8},{10,11... | collective-permute-start | bytes 811016 | tf_op jit(solution)/shard_map/ppermute | solution.py:43
  50.9 1.5 %collective-permute-start.14 = (bf16[512,256]{1,0:T(8,128)(2,1)S(1)}, bf16[512,256]{1,0:T(8,128)(2,1)S(1)}, u32[]{:S(2)}, u32[]{:S(2)}) collective-permute-start(bf16[512,256]{1,0:T(8,128)(2,1)S(1)} %collective-permute-done.7.refs_4_), channel_id=1, source_target_pairs={{0,1},{1,0},{2,3},{3,2},{4,5},{5,4},{6,7},{7,6},{8,9},{9,8},{10,11... | collective-permute-start | bytes 786440 | tf_op jit(solution)/shard_map/ppermute | solution.py:43

commit v3 on v2

v3 whole, which is shorter than its diff:
```python
import functools

import jax
import jax.numpy as jnp
from jax import lax
from jax.experimental import pallas as pl
from jax.experimental.pallas import tpu as pltpu
from jax.sharding import PartitionSpec as P

BS = 256
BLK_DEV = 4
CAP = 8
REACH = 3
SLOTS = (REACH + 1) * CAP
QUAD = 4
EPS = 1e-05
STEP = 256
TABLE = 2 * CAP
VMEM = 24 * 1024 * 1024


def along_x(i):
    return i ^ 1


def along_y(i):
    return i ^ 2


def along_z_side(i, n):
    return (i + QUAD if i % QUAD < 2 else i - QUAD) % n


def move_near(i, core, n):
    return (along_x(i), 0) if core == 0 else (along_y(i), 1)


def move_z(i, core, n):
    return (i - QUAD if i % 2 == 0 else i + QUAD) % n, core


def move_next(i, core, n):
    if core == 0:
        to = along_y(i)
        return to, (1 if to % QUAD == 0 else 0)
    to = along_z_side(i, n)
    return to, (0 if to % QUAD == 0 else 1)


def move_x(i, core, n):
    return along_x(i), core


def move_last(i, core, n):
    holds_diag = core == (1 if i % QUAD == 0 else 0)
    return (along_z_side(i, n), 0) if holds_diag else (along_x(i), 1)


def send(value, move):
    length, cores = lax.axis_size("feat"), lax.axis_size("samp")
    pairs = []
    for i in range(length):
        for core in range(cores):
            to, to_core = move(i, core, length)
            pairs.append((i * cores + core, to * cores + to_core))
    return lax.ppermute(value, ("feat", "samp"), pairs)


def swap(value):
    return lax.ppermute(value, "samp", [(0, 1), (1, 0)])


def off_near(r, core):
    return jnp.where(core == 0, 1 - 2 * lax.rem(r, 2), 2 - 4 * lax.div(r, 2))


def off_next(r, core):
    return jnp.where((core == 0) != (r == 0), 3 - 2 * r, 4 * lax.div(r, 2) - 2)


def off_zx(r, core):
    return 6 * lax.rem(r, 2) - 3


def off_last(r, core):
    return jnp.where(r == 0, -1, jnp.where(r == 1, -3, jnp.where(r == 2, 3, 1)))


def normalise(read_own, read_par, z_ref):
    rows = z_ref.shape[0]
    width = z_ref.shape[1] // 2
    total = 2 * width
    for at in range(0, rows, STEP):
        here = slice(at, at + STEP)
        a = read_own(here).astype(jnp.float32)
        b = read_par(here).astype(jnp.float32)
        mean = jnp.sum(a + b, axis=1, keepdims=True) / total
        var = jnp.sum(a * a + b * b, axis=1, keepdims=True) / total - mean * mean
        inv = lax.rsqrt(var + EPS)
        z_ref[here, :width] = ((a - mean) * inv).astype(jnp.bfloat16)
        z_ref[here, width:] = ((b - mean) * inv).astype(jnp.bfloat16)


def slot_of(ids, table, wins, off, slot, code):
    position = ids[0]
    ahead = off >= 0
    at = jnp.maximum(off, 0) * CAP + slot
    left = jnp.where(ahead, table[0, at] - position * BLK_DEV, lax.div(code, BLK_DEV))
    right = jnp.where(ahead, table[1, at] - (position + off) * BLK_DEV, lax.rem(code, BLK_DEV))
    live = jnp.where(ahead, table[0, at], code) >= 0
    live = jnp.logical_and(live, position + off >= 0)
    b = jnp.where(live, jnp.where(ahead, left, right), 0)
    o = jnp.where(live, jnp.where(ahead, right, left), 0)
    mine = position * BLK_DEV + b
    other = jnp.where(live, (position + off) * BLK_DEV + o, 0)
    lo_b, hi_b = wins[0, mine], wins[1, mine]
    lo_o, hi_o = wins[0, other], wins[1, other]
    meet = jnp.maximum(jnp.minimum(hi_b, hi_o) - jnp.maximum(lo_b, lo_o), 0)
    num = jnp.where(live, meet + 16, 0)
    den = hi_b - lo_b + hi_o - lo_o + 16
    return b, o, num, den


def codes_of(rows, off):
    values = rows.astype(jnp.float32)
    row = lax.broadcasted_iota(jnp.int32, values.shape, 0)
    lane = lax.broadcasted_iota(jnp.int32, values.shape, 1)
    first = jnp.maximum(-off, 0) * CAP
    return [
        jnp.sum(
            jnp.where(jnp.logical_and(row == 0, lane == first + slot), values, 0.0)
        ).astype(jnp.int32)
        for slot in range(CAP)
    ]


def scale_of(num, den, samples):
    top = jnp.full((1, BS), num, jnp.int32).astype(jnp.float32)
    low = jnp.full((1, BS), den, jnp.int32).astype(jnp.float32)
    return top / low / samples


def at_block(index):
    return pl.ds(pl.multiple_of(index * BS, BS), BS)


def grams(scalars, off, codes, zown_ref, z_ref, tile_ref):
    samples = zown_ref.shape[1]
    found = [slot_of(*scalars, off, slot, codes[slot]) for slot in range(CAP)]
    for slot, (b, o, num, den) in enumerate(found):
        gram = lax.dot_general(
            zown_ref[at_block(b), :],
            z_ref[at_block(o), :],
            (((1,), (1,)), ((), ())),
            preferred_element_type=jnp.float32,
        )
        tile_ref[slot] = gram * scale_of(num, den, samples)
    return found


def products(found, zown_ref, z_ref, tile_ref, acc_ref, itself):
    width = acc_ref.shape[1]
    for slot, (b, o, _, _) in enumerate(found):
        tile = tile_ref[slot].astype(jnp.bfloat16)
        acc_ref[at_block(b), :] += jnp.dot(
            tile, z_ref[at_block(o), :width], preferred_element_type=jnp.float32
        )
        if itself:
            back = lax.dot_general(
                tile,
                zown_ref[at_block(b), :width],
                (((0,), (0,)), ((), ())),
                preferred_element_type=jnp.float32,
            )
            acc_ref[at_block(o), :] += back * jnp.where(b == o, 0.0, 1.0)


def put_tiles(ids, off, tile_ref, corr_ref, sem):
    mine = jnp.logical_and(off >= 0, lax.div(off, 2) == ids[1])
    first = jnp.where(jnp.logical_or(off == 1, off == 3), CAP, 0)
    copy = pltpu.make_async_copy(
        tile_ref, corr_ref.at[pl.ds(pl.multiple_of(first, CAP), CAP)], sem
    )

    @pl.when(mine)
    def _():
        copy.start()

    return mine, copy


def end_tiles(pending):
    mine, copy = pending

    @pl.when(mine)
    def _():
        copy.wait()


def self_kernel(ids, table, wins, own_ref, par_ref, zown_ref, acc_ref, corr_ref, tile_ref, sem):
    scalars = (ids, table, wins)
    width = own_ref.shape[1]
    normalise(lambda at: own_ref[at, :], lambda at: par_ref[at, :], zown_ref)
    found = grams(scalars, jnp.int32(0), [jnp.int32(-1)] * CAP, zown_ref, zown_ref, tile_ref)
    pending = put_tiles(ids, jnp.int32(0), tile_ref, corr_ref, sem)
    acc_ref[...] = zown_ref[:, :width].astype(jnp.float32)
    products(found, zown_ref, zown_ref, tile_ref, acc_ref, True)
    end_tiles(pending)


def either(first, one_ref, two_ref):
    return lambda at: jnp.where(first, one_ref[at, :], two_ref[at, :])


def plain(ref):
    return lambda at: ref[at, :]


def unit(scalars, off_of, own, par, table_ref, zown_ref, acc_ref, corr_ref, z_ref, tile_ref, sem):
    rows = zown_ref.shape[0]
    ids = scalars[0]
    off = off_of(lax.rem(ids[0], QUAD), ids[1])
    normalise(own, par, z_ref)
    codes = codes_of(table_ref[rows : rows + TABLE, :128], off)
    found = grams(scalars, off, codes, zown_ref, z_ref, tile_ref)
    pending = put_tiles(ids, off, tile_ref, corr_ref, sem)
    products(found, zown_ref, z_ref, tile_ref, acc_ref, False)
    return pending


def near_kernel(
    ids, table, wins, zown_ref, acc_in, own_ref, par_ref, _, acc_ref, corr_ref, z_ref, tile_ref, sem
):
    scalars = (ids, table, wins)
    width = acc_in.shape[1]
    acc_ref[:, :width] = acc_in[...]
    acc_ref[:, width:] = jnp.zeros_like(acc_in)
    refs = (zown_ref, acc_ref, corr_ref, z_ref, tile_ref, sem)
    end_tiles(unit(scalars, off_near, plain(own_ref), plain(par_ref), own_ref, *refs))


def next_kernel(
    ids, table, wins, zown_ref, acc_in, one_ref, two_ref, _, out_ref, give_ref, corr_ref, *scratch
):
    scalars = (ids, table, wins)
    acc_ref, z_ref, tile_ref, sem = scratch
    width = out_ref.shape[1]
    acc_ref[...] = acc_in[...]
    straight = lax.rem(ids[0], QUAD) != 0
    own, par = either(straight, one_ref, two_ref), either(straight, two_ref, one_ref)
    refs = (zown_ref, acc_ref, corr_ref, z_ref, tile_ref, sem)
    pending = unit(scalars, off_next, own, par, one_ref, *refs)
    out_ref[...] = acc_ref[:, :width]
    give_ref[...] = acc_ref[:, width:].astype(give_ref.dtype)
    end_tiles(pending)


def both_kernel(
    ids, table, wins, zown_ref, acc_in, own_ref, par_ref, _, out_ref, corr_ref, z_ref, tile_ref, sem
):
    scalars = (ids, table, wins)
    out_ref[...] = acc_in[...]
    refs = (zown_ref, out_ref, corr_ref, z_ref, tile_ref, sem)
    end_tiles(unit(scalars, off_zx, plain(own_ref), plain(par_ref), own_ref, *refs))


def last_kernel(
    ids, table, wins, zown_ref, acc_in, own_ref, par_ref, got_ref, _, out_ref, corr_ref, *scratch
):
    scalars = (ids, table, wins)
    acc_ref, z_ref, tile_ref, sem = scratch
    acc_ref[...] = acc_in[...] + got_ref[...].astype(jnp.float32)
    refs = (zown_ref, acc_ref, corr_ref, z_ref, tile_ref, sem)
    pending = unit(scalars, off_last, plain(own_ref), plain(par_ref), own_ref, *refs)
    out_ref[...] = acc_ref[...].astype(out_ref.dtype)
    end_tiles(pending)


def last_two_kernel(
    ids, table, wins, zown_ref, acc_in, zx_ref, zx_par, own_ref, par_ref, got_ref, _, out_ref, corr_ref, *scratch
):
    scalars = (ids, table, wins)
    acc_ref, z_ref, tile_ref, sems = scratch
    acc_ref[...] = acc_in[...] + got_ref[...].astype(jnp.float32)
    pending = []
    for k, (off_of, own, swapped) in enumerate(
        ((off_zx, zx_ref, zx_par), (off_last, own_ref, par_ref))
    ):
        refs = (zown_ref, acc_ref, corr_ref, z_ref.at[k], tile_ref.at[k], sems.at[k])
        pending.append(unit(scalars, off_of, plain(own), plain(swapped), own, *refs))
    out_ref[...] = acc_ref[...].astype(out_ref.dtype)
    for one in pending:
        end_tiles(one)


SMEM = pl.BlockSpec(memory_space=pltpu.SMEM)
INSIDE = pl.BlockSpec(memory_space=pltpu.VMEM)
ANY = pl.BlockSpec(memory_space=pl.ANY)


def estimate(mib):
    return pl.CostEstimate(flops=1, bytes_accessed=1 + int(mib * 2**20), transcendentals=0)


EST = {"last": 20, "near": 4, "next": 0, "self": 0, "zx_p": 8}


def run_self(ids, table, wins, own, par):
    rows, width = own.shape
    return pl.pallas_call(
        self_kernel,
        out_shape=(
            jax.ShapeDtypeStruct((rows, 2 * width), jnp.bfloat16),
            jax.ShapeDtypeStruct((rows, width), jnp.float32),
            jax.ShapeDtypeStruct((2 * CAP, BS, BS), jnp.float32),
        ),
        in_specs=[SMEM, SMEM, SMEM, INSIDE, INSIDE],
        out_specs=(INSIDE, INSIDE, ANY),
        scratch_shapes=[pltpu.VMEM((CAP, BS, BS), jnp.float32), pltpu.SemaphoreType.DMA],
        compiler_params=pltpu.CompilerParams(vmem_limit_bytes=VMEM),
        cost_estimate=estimate(EST["self"]),
        name="self_pairs",
    )(ids, table, wins, own, par)


def run_unit(kernel, name, corr, inputs, outs, acc_shape=None, units=None):
    rows, both = inputs[3].shape
    many = (units,) if units else ()
    scratch = [pltpu.VMEM(acc_shape, jnp.float32)] if acc_shape else []
    outs = [jax.ShapeDtypeStruct((rows, width), dtype) for width, dtype in outs]
    return pl.pallas_call(
        kernel,
        out_shape=(*outs, jax.ShapeDtypeStruct(corr.shape, corr.dtype)),
        in_specs=[SMEM] * 3 + [INSIDE] * (len(inputs) - 3) + [ANY],
        out_specs=(*[INSIDE] * len(outs), ANY),
        scratch_shapes=scratch
        + [
            pltpu.VMEM((*many, rows, both), jnp.bfloat16),
            pltpu.VMEM((*many, CAP, BS, BS), jnp.float32),
            pltpu.SemaphoreType.DMA(many),
        ],
        input_output_aliases={len(inputs): len(outs)},
        compiler_params=pltpu.CompilerParams(vmem_limit_bytes=VMEM),
        cost_estimate=estimate(EST[name[:4]]),
        name=name,
    )(*inputs, corr)


def with_table(spectra, table, position):
    rows, width = spectra.shape
    first = table[:1] - position * BLK_DEV
    group = lax.broadcasted_iota(jnp.int32, first.shape, 1) // CAP
    second = table[1:] - (position + group) * BLK_DEV
    code = jnp.where(table[:1] >= 0, first * BLK_DEV + second, -1).astype(spectra.dtype)
    code = jnp.pad(code, ((rows, TABLE - 1), (0, width - code.shape[1])))
    return jnp.pad(spectra, ((0, TABLE), (0, 0))) + code


def body(spectra, pair_blocks, windows):
    hold = lax.optimization_barrier
    position = lax.axis_index("feat")
    rows, width = spectra.shape
    both = 2 * width
    par = swap(spectra)
    table, wins = pair_blocks.T, windows.T
    unit = with_table(spectra, table, position)
    near_own = send(unit, move_near)
    from_z = send(unit, move_z)
    near_par = send(par, move_near)
    ids = jnp.stack([position, lax.axis_index("samp")]).astype(jnp.int32)
    scalars = (ids, table, wins)
    zown, acc, corr = run_self(ids, table, wins, spectra, par)
    near_own, acc = hold((near_own, acc))
    next_own = send(near_own, move_next)
    from_z, acc = hold((from_z, acc))
    zx = send(from_z, move_x)
    near_par, _ = hold((near_par, acc))
    next_par = send(near_par, move_next)
    next_own, next_par, acc = hold((next_own, next_par, acc))
    acc, corr = run_unit(
        near_kernel,
        "near_pairs",
        corr,
        (*scalars, zown, acc, near_own, near_par),
        [(both, jnp.float32)],
    )
    next_own, near_par = hold((next_own, near_par))
    last = send(next_own, move_last)
    acc, give, corr = run_unit(
        next_kernel,
        "next_pairs",
        corr,
        (*scalars, zown, acc, next_own, next_par),
        [(width, jnp.float32), (width, jnp.bfloat16)],
        (rows, both),
    )
    zx, acc = hold((zx, acc))
    acc, corr = run_unit(
        both_kernel,
        "zx_pairs",
        corr,
        (*scalars, zown, acc, zx, swap(zx)),
        [(width, jnp.float32)],
    )
    profiles, corr = run_unit(
        last_kernel,
        "last_pairs",
        corr,
        (*scalars, zown, acc, last, swap(last), swap(give)),
        [(width, jnp.bfloat16)],
        (rows, width),
    )
    return (corr, profiles)


def solution(mesh):
    placed = (P("feat", "samp"), P("feat", None), P())
    return jax.shard_map(
        body,
        mesh=mesh,
        in_specs=placed,
        out_specs=(P(("feat", "samp"), None, None), P("feat", "samp")),
        check_vma=False,
    )
```

time: 56.4 us -> 51.3 us (0.910)
  the two profiles are of different devices: /device:TPU:1 before, /device:TPU:31 now
where the time goes in v3:
time: 51.3 us; the launch traced here: 51.1 us
  waiting for transfers between devices  18.1 us (35%)
  Pallas kernels  16.7 us (33%)
  starting transfers between devices  11.2 us (22%)
  local copies, waits for them, and re-layouts  2.4 us (5%)
  other arithmetic  1.92 us (4%)
  between operations  0.7 us (1%)
    ppermute x7, waiting for transfers between devices, send(): return lax.ppermute(value, ('feat', 'samp'), pairs)  18.1 us
    pallas_call x4, Pallas kernels, run_unit(): pl.pallas_call(kernel, out_shape=(*outs, jax.ShapeDtypeStruct(corr.shape,...  13.9 us
    ppermute x4, starting transfers between devices, swap(): return lax.ppermute(value, 'samp', [(0, 1), (1, 0)])  7.17 us
    ppermute x7, starting transfers between devices, send(): return lax.ppermute(value, ('feat', 'samp'), pairs)  4.01 us
    pallas_call x1, Pallas kernels, run_self(): pl.pallas_call(self_kernel, out_shape=(jax.ShapeDtypeStruct((rows, 2 * wi...  2.85 us
    unnamed x6, local copies, waits for them, and re-layouts  2.4 us
    add x1, other arithmetic, with_table(): return jnp.pad(spectra, ((0, TABLE), (0, 0))) + code  1.08 us
  transfers between devices with their start and end apart: 11, of which 5 were waited for; matrix products, arithmetic and copies ran while one was open for 4% of the time, Pallas kernels for 26%

profile of v3, /device:TPU:31, one launch (start us, length us, event | category | flops | bytes accessed | tf_op | source)
XLA Modules:
  0.0 51.1 jit_solution(1242072686152447217)
XLA Ops:
  0.6 0.7 %collective-permute-start = (bf16[1024,256]{1,0:T(8,128)(2,1)}, bf16[1024,256]{1,0:T(8,128)(2,1)S(1)}, u32[]{:S(2)}, u32[]{:S(2)}) collective-permute-start(bf16[1024,256]{1,0:T(8,128)(2,1)} %own_ref.1), channel_id=1, source_target_pairs={{0,1},{1,0},{2,3},{3,2},{4,5},{5,4},{6,7},{7,6},{8,9},{9,8},{10,11... | collective-permute-start | bytes 1572872 | tf_op jit(solution)/shard_map/ppermute | solution.py:70
  1.4 0.8 %fusion.4 = bf16[1,32]{1,0:T(2,128)(2,1)S(1)} fusion(s32[2,32]{1,0:T(2,128)} %bitcast.4, s32[]{:T(128)} %axis_index.23, s32[]{:T(128)S(6)} %mul.17), kind=kLoop, calls=%fused_computation.11 | loop fusion | flops 544 | bytes 328 | tf_op jit(solution)/shard_map/convert_element_type | solution.py:354
  2.1 1.1 %pad_add_fusion = bf16[1040,256]{1,0:T(8,128)(2,1)S(1)} fusion(bf16[1,32]{1,0:T(2,128)(2,1)S(1)} %fusion.4, bf16[1024,256]{1,0:T(8,128)(2,1)} %own_ref.1), kind=kLoop, calls=%fused_computation | loop fusion | flops 1064960 | bytes 1056832 | tf_op jit(solution)/shard_map/add | solution.py:356
  3.2 0.3 collective-permute-start.2
  3.5 0.0 collective-permute-start.1
  3.5 0.0 collective-permute-done.par_ref
  3.5 1.2 %collective-permute-start.5 = (bf16[1024,256]{1,0:T(8,128)(2,1)S(1)}, bf16[1024,256]{1,0:T(8,128)(2,1)S(1)}, u32[]{:S(2)}, u32[]{:S(2)}) collective-permute-start(bf16[1024,256]{1,0:T(8,128)(2,1)S(1)} %collective-permute-done.par_ref), channel_id=1, source_target_pairs={{0,2},{1,5},{2,0},{3,7},{4,6},{5,1},{6,4},{7,3},{8,10},{9,13},{10,... | collective-permute-start | bytes 1572872 | tf_op jit(solution)/shard_map/ppermute | solution.py:66
  4.8 0.1 pad_add_fusion.1.ids
  4.8 1.0 %copy-done = bf16[1024,256]{1,0:T(8,128)(2,1)S(1)} copy-done((bf16[1024,256]{1,0:T(8,128)(2,1)S(1)}, bf16[1024,256]{1,0:T(8,128)(2,1)}, u32[]{:S(2)}) %copy-start) | copy-done | bytes 524312
  5.9 0.7 %copy-done.1 = s32[32,2]{0,1:T(2,128)S(1)} copy-done((s32[32,2]{0,1:T(2,128)S(1)}, s32[32,2]{0,1:T(2,128)}, u32[]{:S(2)}) %copy-start.1) | copy-done | bytes 280
  6.6 0.7 %copy-done.2 = s32[64,2]{0,1:T(2,128)S(1)} copy-done((s32[64,2]{0,1:T(2,128)S(1)}, s32[64,2]{0,1:T(2,128)}, u32[]{:S(2)}) %copy-start.2) | copy-done | bytes 536
  7.2 2.9 %self_pairs.1 = (bf16[1024,512]{1,0:T(8,128)(2,1)S(1)}, f32[1024,256]{1,0:T(8,128)S(1)}, f32[16,256,256]{2,1,0:T(8,128)}) custom-call(s32[2]{0:T(128)S(1)} %pad_add_fusion.1.ids, s32[2,32]{1,0:T(2,128)S(1)} %bitcast.5, s32[2,64]{1,0:T(2,128)S(1)} %bitcast.10, bf16[1024,256]{1,0:T(8,128)(2,1)S(1)} %copy-done, bf16[1024,256]{1,0:T(8,128)(2,1)S(1)} %collective-permute-done.par_ref), custom_call_target="tpu_custom_call" | custom-call | flops 1 | bytes 1 | tf_op jit(solution)/shard_map/self_pairs/pallas_call | solution.py:310
  10.1 1.6 %collective-permute-done.2.own_ref = bf16[1040,256]{1,0:T(8,128)(2,1)S(1)} collective-permute-done((bf16[1040,256]{1,0:T(8,128)(2,1)S(1)}, bf16[1040,256]{1,0:T(8,128)(2,1)S(1)}, u32[]{:S(2)}, u32[]{:S(2)}) %collective-permute-start.2) | collective-permute-done | bytes 532512 | tf_op jit(solution)/shard_map/ppermute | solution.py:66
  11.7 0.2 collective-permute-start.4
  11.9 5.2 %collective-permute-done.1 = bf16[1040,256]{1,0:T(8,128)(2,1)S(1)} collective-permute-done((bf16[1040,256]{1,0:T(8,128)(2,1)S(1)}, bf16[1040,256]{1,0:T(8,128)(2,1)S(1)}, u32[]{:S(2)}, u32[]{:S(2)}) %collective-permute-start.1) | collective-permute-done | bytes 532512 | tf_op jit(solution)/shard_map/ppermute | solution.py:66
  17.1 1.7 %collective-permute-done.5.par_ref = bf16[1024,256]{1,0:T(8,128)(2,1)S(1)} collective-permute-done((bf16[1024,256]{1,0:T(8,128)(2,1)S(1)}, bf16[1024,256]{1,0:T(8,128)(2,1)S(1)}, u32[]{:S(2)}, u32[]{:S(2)}) %collective-permute-start.5) | collective-permute-done | bytes 524320 | tf_op jit(solution)/shard_map/ppermute | solution.py:66
  18.8 0.2 collective-permute-start.6
  19.0 0.1 collective-permute-start.3
  19.1 3.9 %collective-permute-done.4.one_ref = bf16[1040,256]{1,0:T(8,128)(2,1)S(1)} collective-permute-done((bf16[1040,256]{1,0:T(8,128)(2,1)S(1)}, bf16[1040,256]{1,0:T(8,128)(2,1)S(1)}, u32[]{:S(2)}, u32[]{:S(2)}) %collective-permute-start.4) | collective-permute-done | bytes 532512 | tf_op jit(solution)/shard_map/ppermute | solution.py:66
  23.0 5.7 %collective-permute-done.6.two_ref = bf16[1024,256]{1,0:T(8,128)(2,1)S(1)} collective-permute-done((bf16[1024,256]{1,0:T(8,128)(2,1)S(1)}, bf16[1024,256]{1,0:T(8,128)(2,1)S(1)}, u32[]{:S(2)}, u32[]{:S(2)}) %collective-permute-start.6) | collective-permute-done | bytes 524320 | tf_op jit(solution)/shard_map/ppermute | solution.py:66
  28.7 2.1 %collective-permute-start.8 = (bf16[1040,256]{1,0:T(8,128)(2,1)S(1)}, bf16[1040,256]{1,0:T(8,128)(2,1)S(1)}, u32[]{:S(2)}, u32[]{:S(2)}) collective-permute-start(bf16[1040,256]{1,0:T(8,128)(2,1)S(1)} %collective-permute-done.4.one_ref), channel_id=1, source_target_pairs={{0,3},{1,8},{2,10},{3,1},{4,28},{5,7},{6,30},{7,5},{8,11},{9,16},{... | collective-permute-start | bytes 1597448 | tf_op jit(solution)/shard_map/ppermute | solution.py:66
  30.7 2.9 %near_pairs.1 = (f32[1024,512]{1,0:T(8,128)S(1)}, f32[16,256,256]{2,1,0:T(8,128)}) custom-call(s32[2]{0:T(128)S(1)} %pad_add_fusion.1.ids, s32[2,32]{1,0:T(2,128)S(1)} %bitcast.6, s32[2,64]{1,0:T(2,128)S(1)} %bitcast.11, bf16[1024,512]{1,0:T(8,128)(2,1)S(1)} %get-tuple-element.25.zown_ref, ...), custom_call_target="tpu_custom_call", output_to_operand_aliasing={{1}: (7, {})} | custom-call | flops 1 | bytes 4194305 | tf_op jit(solution)/shard_map/near_pairs/pallas_call | solution.py:331
  33.6 4.0 %next_pairs.1 = (f32[1024,256]{1,0:T(8,128)S(1)}, bf16[1024,256]{1,0:T(8,128)(2,1)S(1)}, f32[16,256,256]{2,1,0:T(8,128)}) custom-call(s32[2]{0:T(128)S(1)} %pad_add_fusion.1.ids, s32[2,32]{1,0:T(2,128)S(1)} %bitcast.7, s32[2,64]{1,0:T(2,128)S(1)} %bitcast.12, bf16[1024,512]{1,0:T(8,128)(2,1)S(1)} %get-tuple-element.25.zown_ref, ...), custom_call_target="tpu_custom_call", output_to_operand_aliasing={{2}: (7, {})} | custom-call | flops 1 | bytes 1 | tf_op jit(solution)/shard_map/next_pairs/pallas_call | solution.py:331
  37.6 0.0 collective-permute-done.3.own_ref
  37.6 1.6 %collective-permute-start.7 = (bf16[1040,256]{1,0:T(8,128)(2,1)S(1)}, bf16[1040,256]{1,0:T(8,128)(2,1)S(1)}, u32[]{:S(2)}, u32[]{:S(2)}) collective-permute-start(bf16[1040,256]{1,0:T(8,128)(2,1)S(1)} %collective-permute-done.3.own_ref), channel_id=1, source_target_pairs={{0,1},{1,0},{2,3},{3,2},{4,5},{5,4},{6,7},{7,6},{8,9},{9,8},{10,11... | collective-permute-start | bytes 1597448 | tf_op jit(solution)/shard_map/ppermute | solution.py:70
  39.2 4.8 %collective-permute-start.9 = (bf16[1040,256]{1,0:T(8,128)(2,1)S(1)}, bf16[1040,256]{1,0:T(8,128)(2,1)S(1)}, u32[]{:S(2)}, u32[]{:S(2)}) collective-permute-start(bf16[1040,256]{1,0:T(8,128)(2,1)S(1)} %collective-permute-done.8.own_ref), channel_id=1, source_target_pairs={{0,1},{1,0},{2,3},{3,2},{4,5},{5,4},{6,7},{7,6},{8,9},{9,8},{10,11... | collective-permute-start | bytes 1597448 | tf_op jit(solution)/shard_map/ppermute | solution.py:70
  44.0 0.0 collective-permute-start.10
  44.0 0.0 collective-permute-done.7.par_ref
  44.0 3.6 %zx_pairs.1 = (f32[1024,256]{1,0:T(8,128)S(1)}, f32[16,256,256]{2,1,0:T(8,128)}) custom-call(s32[2]{0:T(128)S(1)} %pad_add_fusion.1.ids, s32[2,32]{1,0:T(2,128)S(1)} %bitcast.8, s32[2,64]{1,0:T(2,128)S(1)} %bitcast.13, bf16[1024,512]{1,0:T(8,128)(2,1)S(1)} %get-tuple-element.25.zown_ref, ...), custom_call_target="tpu_custom_call", output_to_operand_aliasing={{1}: (7, {})} | custom-call | flops 1 | bytes 8388609 | tf_op jit(solution)/shard_map/zx_pairs/pallas_call | solution.py:331
  47.7 0.0 collective-permute-done.10.got_ref
  47.7 0.0 collective-permute-done.9.par_ref
  47.7 3.4 %last_pairs.1 = (bf16[1024,256]{1,0:T(8,128)(2,1)}, f32[16,256,256]{2,1,0:T(8,128)}) custom-call(s32[2]{0:T(128)S(1)} %pad_add_fusion.1.ids, s32[2,32]{1,0:T(2,128)S(1)} %bitcast.9, s32[2,64]{1,0:T(2,128)S(1)} %bitcast.14, bf16[1024,512]{1,0:T(8,128)(2,1)S(1)} %get-tuple-element.25.zown_ref, ...), custom_call_target="tpu_custom_call", output_to_operand_aliasing={{1}: (8, {})} | custom-call | flops 1 | bytes 20971520 | tf_op jit(solution)/shard_map/last_pairs/pallas_call | solution.py:331
  (4 shorter events, 0.0 us)
Async XLA Ops:
  0.6 2.9 %collective-permute-start = (bf16[1024,256]{1,0:T(8,128)(2,1)}, bf16[1024,256]{1,0:T(8,128)(2,1)S(1)}, u32[]{:S(2)}, u32[]{:S(2)}) collective-permute-start(bf16[1024,256]{1,0:T(8,128)(2,1)} %own_ref.1), channel_id=1, source_target_pairs={{0,1},{1,0},{2,3},{3,2},{4,5},{5,4},{6,7},{7,6},{8,9},{9,8},{10,11... | collective-permute-start | bytes 1572872 | tf_op jit(solution)/shard_map/ppermute | solution.py:70
  3.2 8.5 %collective-permute-start.2 = (bf16[1040,256]{1,0:T(8,128)(2,1)S(1)}, bf16[1040,256]{1,0:T(8,128)(2,1)S(1)}, u32[]{:S(2)}, u32[]{:S(2)}) collective-permute-start(bf16[1040,256]{1,0:T(8,128)(2,1)S(1)} %pad_add_fusion), channel_id=1, source_target_pairs={{0,2},{1,5},{2,0},{3,7},{4,6},{5,1},{6,4},{7,3},{8,10},{9,13},{10,... | collective-permute-start | bytes 1597448 | tf_op jit(solution)/shard_map/ppermute | solution.py:66
  3.5 13.6 %collective-permute-start.1 = (bf16[1040,256]{1,0:T(8,128)(2,1)S(1)}, bf16[1040,256]{1,0:T(8,128)(2,1)S(1)}, u32[]{:S(2)}, u32[]{:S(2)}) collective-permute-start(bf16[1040,256]{1,0:T(8,128)(2,1)S(1)} %pad_add_fusion), channel_id=1, source_target_pairs={{0,24},{1,25},{2,10},{3,11},{4,28},{5,29},{6,14},{7,15},{8,0},{9,1... | collective-permute-start | bytes 1597448 | tf_op jit(solution)/shard_map/ppermute | solution.py:66
  3.5 15.3 %collective-permute-start.5 = (bf16[1024,256]{1,0:T(8,128)(2,1)S(1)}, bf16[1024,256]{1,0:T(8,128)(2,1)S(1)}, u32[]{:S(2)}, u32[]{:S(2)}) collective-permute-start(bf16[1024,256]{1,0:T(8,128)(2,1)S(1)} %collective-permute-done.par_ref), channel_id=1, source_target_pairs={{0,2},{1,5},{2,0},{3,7},{4,6},{5,1},{6,4},{7,3},{8,10},{9,13},{10,... | collective-permute-start | bytes 1572872 | tf_op jit(solution)/shard_map/ppermute | solution.py:66
  4.8 1.0 %copy-start = (bf16[1024,256]{1,0:T(8,128)(2,1)S(1)}, bf16[1024,256]{1,0:T(8,128)(2,1)}, u32[]{:S(2)}) copy-start(bf16[1024,256]{1,0:T(8,128)(2,1)} %own_ref.1) | copy-start | bytes 1572868
  5.9 0.7 %copy-start.1 = (s32[32,2]{0,1:T(2,128)S(1)}, s32[32,2]{0,1:T(2,128)}, u32[]{:S(2)}) copy-start(s32[32,2]{0,1:T(2,128)} %param.4) | copy-start | bytes 772
  6.6 0.7 %copy-start.2 = (s32[64,2]{0,1:T(2,128)S(1)}, s32[64,2]{0,1:T(2,128)}, u32[]{:S(2)}) copy-start(s32[64,2]{0,1:T(2,128)} %param.5) | copy-start | bytes 1540
  11.7 11.3 %collective-permute-start.4 = (bf16[1040,256]{1,0:T(8,128)(2,1)S(1)}, bf16[1040,256]{1,0:T(8,128)(2,1)S(1)}, u32[]{:S(2)}, u32[]{:S(2)}) collective-permute-start(bf16[1040,256]{1,0:T(8,128)(2,1)S(1)} %collective-permute-done.2.own_ref), channel_id=1, source_target_pairs={{0,4},{1,8},{2,6},{3,11},{4,1},{5,29},{6,2},{7,31},{8,12},{9,16},{... | collective-permute-start | bytes 1597448 | tf_op jit(solution)/shard_map/ppermute | solution.py:66
  18.8 9.8 %collective-permute-start.6 = (bf16[1024,256]{1,0:T(8,128)(2,1)S(1)}, bf16[1024,256]{1,0:T(8,128)(2,1)S(1)}, u32[]{:S(2)}, u32[]{:S(2)}) collective-permute-start(bf16[1024,256]{1,0:T(8,128)(2,1)S(1)} %collective-permute-done.5.par_ref), channel_id=1, source_target_pairs={{0,4},{1,8},{2,6},{3,11},{4,1},{5,29},{6,2},{7,31},{8,12},{9,16},{... | collective-permute-start | bytes 1572872 | tf_op jit(solution)/shard_map/ppermute | solution.py:66
  19.0 18.6 %collective-permute-start.3 = (bf16[1040,256]{1,0:T(8,128)(2,1)S(1)}, bf16[1040,256]{1,0:T(8,128)(2,1)S(1)}, u32[]{:S(2)}, u32[]{:S(2)}) collective-permute-start(bf16[1040,256]{1,0:T(8,128)(2,1)S(1)} %collective-permute-done.1), channel_id=1, source_target_pairs={{0,2},{1,3},{2,0},{3,1},{4,6},{5,7},{6,4},{7,5},{8,10},{9,11},{10,... | collective-permute-start | bytes 1597448 | tf_op jit(solution)/shard_map/ppermute | solution.py:66
  28.7 10.6 %collective-permute-start.8 = (bf16[1040,256]{1,0:T(8,128)(2,1)S(1)}, bf16[1040,256]{1,0:T(8,128)(2,1)S(1)}, u32[]{:S(2)}, u32[]{:S(2)}) collective-permute-start(bf16[1040,256]{1,0:T(8,128)(2,1)S(1)} %collective-permute-done.4.one_ref), channel_id=1, source_target_pairs={{0,3},{1,8},{2,10},{3,1},{4,28},{5,7},{6,30},{7,5},{8,11},{9,16},{... | collective-permute-start | bytes 1597448 | tf_op jit(solution)/shard_map/ppermute | solution.py:66
  37.6 6.4 %collective-permute-start.7 = (bf16[1040,256]{1,0:T(8,128)(2,1)S(1)}, bf16[1040,256]{1,0:T(8,128)(2,1)S(1)}, u32[]{:S(2)}, u32[]{:S(2)}) collective-permute-start(bf16[1040,256]{1,0:T(8,128)(2,1)S(1)} %collective-permute-done.3.own_ref), channel_id=1, source_target_pairs={{0,1},{1,0},{2,3},{3,2},{4,5},{5,4},{6,7},{7,6},{8,9},{9,8},{10,11... | collective-permute-start | bytes 1597448 | tf_op jit(solution)/shard_map/ppermute | solution.py:70
  39.2 8.5 %collective-permute-start.9 = (bf16[1040,256]{1,0:T(8,128)(2,1)S(1)}, bf16[1040,256]{1,0:T(8,128)(2,1)S(1)}, u32[]{:S(2)}, u32[]{:S(2)}) collective-permute-start(bf16[1040,256]{1,0:T(8,128)(2,1)S(1)} %collective-permute-done.8.own_ref), channel_id=1, source_target_pairs={{0,1},{1,0},{2,3},{3,2},{4,5},{5,4},{6,7},{7,6},{8,9},{9,8},{10,11... | collective-permute-start | bytes 1597448 | tf_op jit(solution)/shard_map/ppermute | solution.py:70
  44.0 3.6 %collective-permute-start.10 = (bf16[1024,256]{1,0:T(8,128)(2,1)S(1)}, bf16[1024,256]{1,0:T(8,128)(2,1)S(1)}, u32[]{:S(2)}, u32[]{:S(2)}) collective-permute-start(bf16[1024,256]{1,0:T(8,128)(2,1)S(1)} %get-tuple-element.44), channel_id=1, source_target_pairs={{0,1},{1,0},{2,3},{3,2},{4,5},{5,4},{6,7},{7,6},{8,9},{9,8},{10,11... | collective-permute-start | bytes 1572872 | tf_op jit(solution)/shard_map/ppermute | solution.py:70

commit v4 on v3

--- a/solution.py
+++ b/solution.py
@@ -16,6 +16,7 @@
 EPS = 1e-05
 STEP = 256
 TABLE = 2 * CAP
+PARTS = 2
 VMEM = 24 * 1024 * 1024
 
 
@@ -144,10 +145,9 @@
     return pl.ds(pl.multiple_of(index * BS, BS), BS)
 
 
-def grams(scalars, off, codes, zown_ref, z_ref, tile_ref):
+def grams(found, zown_ref, z_ref, tile_ref):
     samples = zown_ref.shape[1]
-    found = [slot_of(*scalars, off, slot, codes[slot]) for slot in range(CAP)]
-    for slot, (b, o, num, den) in enumerate(found):
+    for slot, (b, o, num, den) in found:
         gram = lax.dot_general(
             zown_ref[at_block(b), :],
             z_ref[at_block(o), :],
@@ -155,12 +155,11 @@
             preferred_element_type=jnp.float32,
         )
         tile_ref[slot] = gram * scale_of(num, den, samples)
-    return found
 
 
 def products(found, zown_ref, z_ref, tile_ref, acc_ref, itself):
     width = acc_ref.shape[1]
-    for slot, (b, o, _, _) in enumerate(found):
+    for slot, (b, o, _, _) in found:
         tile = tile_ref[slot].astype(jnp.bfloat16)
         acc_ref[at_block(b), :] += jnp.dot(
             tile, z_ref[at_block(o), :width], preferred_element_type=jnp.float32
@@ -175,11 +174,11 @@
             acc_ref[at_block(o), :] += back * jnp.where(b == o, 0.0, 1.0)
 
 
-def put_tiles(ids, off, tile_ref, corr_ref, sem):
+def put_tiles(ids, off, some, tile_ref, corr_ref, sem):
     mine = jnp.logical_and(off >= 0, lax.div(off, 2) == ids[1])
-    first = jnp.where(jnp.logical_or(off == 1, off == 3), CAP, 0)
+    first = jnp.where(jnp.logical_or(off == 1, off == 3), CAP, 0) + some.start
     copy = pltpu.make_async_copy(
-        tile_ref, corr_ref.at[pl.ds(pl.multiple_of(first, CAP), CAP)], sem
+        tile_ref.at[some], corr_ref.at[pl.ds(first, some.stop - some.start)], sem
     )
 
     @pl.when(mine)
@@ -190,19 +189,31 @@
 
 
 def end_tiles(pending):
-    mine, copy = pending
-
-    @pl.when(mine)
-    def _():
-        copy.wait()
-
-
-def self_kernel(ids, table, wins, own_ref, par_ref, zown_ref, acc_ref, corr_ref, tile_ref, sem):
+    for mine, copy in pending:
+
+        @pl.when(mine)
+        def _(copy=copy):
+            copy.wait()
+
+
+def grams_out(scalars, off, codes, zown_ref, z_ref, tile_ref, corr_ref, sems):
+    found = [(slot, slot_of(*scalars, off, slot, codes[slot])) for slot in range(CAP)]
+    pending = []
+    for part in range(PARTS):
+        some = slice(part * CAP // PARTS, (part + 1) * CAP // PARTS)
+        grams(found[some], zown_ref, z_ref, tile_ref)
+        pending.append(put_tiles(scalars[0], off, some, tile_ref, corr_ref, sems.at[part]))
+    return found, pending
+
+
+def self_kernel(ids, table, wins, own_ref, par_ref, zown_ref, acc_ref, corr_ref, tile_ref, sems):
     scalars = (ids, table, wins)
     width = own_ref.shape[1]
     normalise(lambda at: own_ref[at, :], lambda at: par_ref[at, :], zown_ref)
-    found = grams(scalars, jnp.int32(0), [jnp.int32(-1)] * CAP, zown_ref, zown_ref, tile_ref)
-    pending = put_tiles(ids, jnp.int32(0), tile_ref, corr_ref, sem)
+    none = [jnp.int32(-1)] * CAP
+    found, pending = grams_out(
+        scalars, jnp.int32(0), none, zown_ref, zown_ref, tile_ref, corr_ref, sems
+    )
     acc_ref[...] = zown_ref[:, :width].astype(jnp.float32)
     products(found, zown_ref, zown_ref, tile_ref, acc_ref, True)
     end_tiles(pending)
@@ -222,8 +233,7 @@
     off = off_of(lax.rem(ids[0], QUAD), ids[1])
     normalise(own, par, z_ref)
     codes = codes_of(table_ref[rows : rows + TABLE, :128], off)
-    found = grams(scalars, off, codes, zown_ref, z_ref, tile_ref)
-    pending = put_tiles(ids, off, tile_ref, corr_ref, sem)
+    found, pending = grams_out(scalars, off, codes, zown_ref, z_ref, tile_ref, corr_ref, sem)
     products(found, zown_ref, z_ref, tile_ref, acc_ref, False)
     return pending
 
@@ -302,7 +312,7 @@
     return pl.CostEstimate(flops=1, bytes_accessed=1 + int(mib * 2**20), transcendentals=0)
 
 
-EST = {"last": 20, "near": 4, "next": 0, "self": 0, "zx_p": 8}
+EST = {"last": 4, "near": 0.5, "next": 0, "self": 2, "zx_p": 60}
 
 
 def run_self(ids, table, wins, own, par):
@@ -316,7 +326,7 @@
         ),
         in_specs=[SMEM, SMEM, SMEM, INSIDE, INSIDE],
         out_specs=(INSIDE, INSIDE, ANY),
-        scratch_shapes=[pltpu.VMEM((CAP, BS, BS), jnp.float32), pltpu.SemaphoreType.DMA],
+        scratch_shapes=[pltpu.VMEM((CAP, BS, BS), jnp.float32), pltpu.SemaphoreType.DMA((PARTS,))],
         compiler_params=pltpu.CompilerParams(vmem_limit_bytes=VMEM),
         cost_estimate=estimate(EST["self"]),
         name="self_pairs",
@@ -337,7 +347,7 @@
         + [
             pltpu.VMEM((*many, rows, both), jnp.bfloat16),
             pltpu.VMEM((*many, CAP, BS, BS), jnp.float32),
-            pltpu.SemaphoreType.DMA(many),
+            pltpu.SemaphoreType.DMA((*many, PARTS)),
         ],
         input_output_aliases={len(inputs): len(outs)},
         compiler_params=pltpu.CompilerParams(vmem_limit_bytes=VMEM),
@@ -361,22 +371,20 @@
     position = lax.axis_index("feat")
     rows, width = spectra.shape
     both = 2 * width
-    par = swap(spectra)
     table, wins = pair_blocks.T, windows.T
     unit = with_table(spectra, table, position)
+    par = swap(unit)
     near_own = send(unit, move_near)
     from_z = send(unit, move_z)
     near_par = send(par, move_near)
     ids = jnp.stack([position, lax.axis_index("samp")]).astype(jnp.int32)
     scalars = (ids, table, wins)
     zown, acc, corr = run_self(ids, table, wins, spectra, par)
-    near_own, acc = hold((near_own, acc))
+    near_own, _ = hold((near_own, acc))
     next_own = send(near_own, move_next)
-    from_z, acc = hold((from_z, acc))
+    from_z, _ = hold((from_z, acc))
     zx = send(from_z, move_x)
-    near_par, _ = hold((near_par, acc))
     next_par = send(near_par, move_next)
-    next_own, next_par, acc = hold((next_own, next_par, acc))
     acc, corr = run_unit(
         near_kernel,
         "near_pairs",
@@ -384,8 +392,9 @@
         (*scalars, zown, acc, near_own, near_par),
         [(both, jnp.float32)],
     )
-    next_own, near_par = hold((next_own, near_par))
+    next_own, _ = hold((next_own, acc))
     last = send(next_own, move_last)
+    next_par, acc = hold((next_par, acc))
     acc, give, corr = run_unit(
         next_kernel,
         "next_pairs",
@@ -395,6 +404,7 @@
         (rows, both),
     )
     zx, acc = hold((zx, acc))
+    got = swap(give)
     acc, corr = run_unit(
         both_kernel,
         "zx_pairs",
@@ -406,7 +416,7 @@
         last_kernel,
         "last_pairs",
         corr,
-        (*scalars, zown, acc, last, swap(last), swap(give)),
+        (*scalars, zown, acc, last, swap(last), got),
         [(width, jnp.bfloat16)],
         (rows, width),
     )

time: 51.3 us -> 48.2 us (0.940)
  the two profiles are of different devices: /device:TPU:31 before, /device:TPU:5 now
where the time goes in v4:
time: 48.2 us; the launch traced here: 48 us
  Pallas kernels  15.8 us (33%)
  starting transfers between devices  14 us (29%)
  waiting for transfers between devices  13.1 us (27%)
  local copies, waits for them, and re-layouts  2.4 us (5%)
  other arithmetic  1.92 us (4%)
  between operations  0.72 us (1%)
    ppermute x7, waiting for transfers between devices, send(): return lax.ppermute(value, ('feat', 'samp'), pairs)  13.1 us
    pallas_call x4, Pallas kernels, run_unit(): pl.pallas_call(kernel, out_shape=(*outs, jax.ShapeDtypeStruct(corr.shape,...  13 us
    ppermute x7, starting transfers between devices, send(): return lax.ppermute(value, ('feat', 'samp'), pairs)  12.6 us
    pallas_call x1, Pallas kernels, run_self(): pl.pallas_call(self_kernel, out_shape=(jax.ShapeDtypeStruct((rows, 2 * wi...  2.83 us
    unnamed x6, local copies, waits for them, and re-layouts  2.4 us
    ppermute x4, starting transfers between devices, swap(): return lax.ppermute(value, 'samp', [(0, 1), (1, 0)])  1.45 us
    add x1, other arithmetic, with_table(): return jnp.pad(spectra, ((0, TABLE), (0, 0))) + code  1.08 us
  transfers between devices with their start and end apart: 11, of which 4 were waited for; matrix products, arithmetic and copies ran while one was open for 0% of the time, Pallas kernels for 25%

profile of v4, /device:TPU:5, one launch (start us, length us, event | category | flops | bytes accessed | tf_op | source)
XLA Modules:
  0.0 48.0 jit_solution(453120890961384161)
XLA Ops:
  0.6 0.8 %fusion.4 = bf16[1,32]{1,0:T(2,128)(2,1)S(1)} fusion(s32[2,32]{1,0:T(2,128)} %bitcast.4, s32[]{:T(128)} %axis_index.23, s32[]{:T(128)S(6)} %mul.17), kind=kLoop, calls=%fused_computation.11 | loop fusion | flops 544 | bytes 328 | tf_op jit(solution)/shard_map/convert_element_type | solution.py:364
  1.4 1.1 %pad_add_fusion = bf16[1040,256]{1,0:T(8,128)(2,1)S(1)} fusion(bf16[1,32]{1,0:T(2,128)(2,1)S(1)} %fusion.4, bf16[1024,256]{1,0:T(8,128)(2,1)} %own_ref.1), kind=kLoop, calls=%fused_computation | loop fusion | flops 1064960 | bytes 1056832 | tf_op jit(solution)/shard_map/add | solution.py:366
  2.5 0.7 %collective-permute-start = (bf16[1040,256]{1,0:T(8,128)(2,1)S(1)}, bf16[1040,256]{1,0:T(8,128)(2,1)S(1)}, u32[]{:S(2)}, u32[]{:S(2)}) collective-permute-start(bf16[1040,256]{1,0:T(8,128)(2,1)S(1)} %pad_add_fusion), channel_id=1, source_target_pairs={{0,1},{1,0},{2,3},{3,2},{4,5},{5,4},{6,7},{7,6},{8,9},{9,8},{10,11... | collective-permute-start | bytes 1597448 | tf_op jit(solution)/shard_map/ppermute | solution.py:71
  3.2 0.0 collective-permute-start.5
  3.2 3.5 %collective-permute-start.1 = (bf16[1040,256]{1,0:T(8,128)(2,1)S(1)}, bf16[1040,256]{1,0:T(8,128)(2,1)S(1)}, u32[]{:S(2)}, u32[]{:S(2)}) collective-permute-start(bf16[1040,256]{1,0:T(8,128)(2,1)S(1)} %pad_add_fusion), channel_id=1, source_target_pairs={{0,24},{1,25},{2,10},{3,11},{4,28},{5,29},{6,14},{7,15},{8,0},{9,1... | collective-permute-start | bytes 1597448 | tf_op jit(solution)/shard_map/ppermute | solution.py:67
  6.8 0.0 collective-permute-done.par_ref
  6.8 1.2 %collective-permute-start.3 = (bf16[1040,256]{1,0:T(8,128)(2,1)S(1)}, bf16[1040,256]{1,0:T(8,128)(2,1)S(1)}, u32[]{:S(2)}, u32[]{:S(2)}) collective-permute-start(bf16[1040,256]{1,0:T(8,128)(2,1)S(1)} %collective-permute-done.par_ref), channel_id=1, source_target_pairs={{0,2},{1,5},{2,0},{3,7},{4,6},{5,1},{6,4},{7,3},{8,10},{9,13},{10,... | collective-permute-start | bytes 1597448 | tf_op jit(solution)/shard_map/ppermute | solution.py:67
  8.0 0.1 pad_add_fusion.1.ids
  8.1 1.0 %copy-done = bf16[1024,256]{1,0:T(8,128)(2,1)S(1)} copy-done((bf16[1024,256]{1,0:T(8,128)(2,1)S(1)}, bf16[1024,256]{1,0:T(8,128)(2,1)}, u32[]{:S(2)}) %copy-start) | copy-done | bytes 524312
  9.1 0.7 %copy-done.1 = s32[32,2]{0,1:T(2,128)S(1)} copy-done((s32[32,2]{0,1:T(2,128)S(1)}, s32[32,2]{0,1:T(2,128)}, u32[]{:S(2)}) %copy-start.1) | copy-done | bytes 280
  9.8 0.7 %copy-done.2 = s32[64,2]{0,1:T(2,128)S(1)} copy-done((s32[64,2]{0,1:T(2,128)S(1)}, s32[64,2]{0,1:T(2,128)}, u32[]{:S(2)}) %copy-start.2) | copy-done | bytes 536
  10.5 2.8 %self_pairs.1 = (bf16[1024,512]{1,0:T(8,128)(2,1)S(1)}, f32[1024,256]{1,0:T(8,128)S(1)}, f32[16,256,256]{2,1,0:T(8,128)}) custom-call(s32[2]{0:T(128)S(1)} %pad_add_fusion.1.ids, s32[2,32]{1,0:T(2,128)S(1)} %bitcast.5, s32[2,64]{1,0:T(2,128)S(1)} %bitcast.10, bf16[1024,256]{1,0:T(8,128)(2,1)S(1)} %copy-done, bf16[1040,256]{1,0:T(8,128)(2,1)S(1)} %collective-permute-done.par_ref), custom_call_target="tpu_custom_call" | custom-call | flops 1 | bytes 2097153 | tf_op jit(solution)/shard_map/self_pairs/pallas_call | solution.py:320
  13.3 0.0 collective-permute-done.5.own_ref
  13.3 1.6 %collective-permute-start.6 = (bf16[1040,256]{1,0:T(8,128)(2,1)S(1)}, bf16[1040,256]{1,0:T(8,128)(2,1)S(1)}, u32[]{:S(2)}, u32[]{:S(2)}) collective-permute-start(bf16[1040,256]{1,0:T(8,128)(2,1)S(1)} %collective-permute-done.5.own_ref), channel_id=1, source_target_pairs={{0,4},{1,8},{2,6},{3,11},{4,1},{5,29},{6,2},{7,31},{8,12},{9,16},{... | collective-permute-start | bytes 1597448 | tf_op jit(solution)/shard_map/ppermute | solution.py:67
  15.0 2.4 %collective-permute-done.3.par_ref = bf16[1040,256]{1,0:T(8,128)(2,1)S(1)} collective-permute-done((bf16[1040,256]{1,0:T(8,128)(2,1)S(1)}, bf16[1040,256]{1,0:T(8,128)(2,1)S(1)}, u32[]{:S(2)}, u32[]{:S(2)}) %collective-permute-start.3) | collective-permute-done | bytes 532512 | tf_op jit(solution)/shard_map/ppermute | solution.py:67
  17.3 4.6 %collective-permute-start.4 = (bf16[1040,256]{1,0:T(8,128)(2,1)S(1)}, bf16[1040,256]{1,0:T(8,128)(2,1)S(1)}, u32[]{:S(2)}, u32[]{:S(2)}) collective-permute-start(bf16[1040,256]{1,0:T(8,128)(2,1)S(1)} %collective-permute-done.3.par_ref), channel_id=1, source_target_pairs={{0,4},{1,8},{2,6},{3,11},{4,1},{5,29},{6,2},{7,31},{8,12},{9,16},{... | collective-permute-start | bytes 1597448 | tf_op jit(solution)/shard_map/ppermute | solution.py:67
  22.0 0.0 collective-permute-done.1
  22.0 1.4 %collective-permute-start.2 = (bf16[1040,256]{1,0:T(8,128)(2,1)S(1)}, bf16[1040,256]{1,0:T(8,128)(2,1)S(1)}, u32[]{:S(2)}, u32[]{:S(2)}) collective-permute-start(bf16[1040,256]{1,0:T(8,128)(2,1)S(1)} %collective-permute-done.1), channel_id=1, source_target_pairs={{0,2},{1,3},{2,0},{3,1},{4,6},{5,7},{6,4},{7,5},{8,10},{9,11},{10,... | collective-permute-start | bytes 1597448 | tf_op jit(solution)/shard_map/ppermute | solution.py:67
  23.4 2.9 %near_pairs.1 = (f32[1024,512]{1,0:T(8,128)S(1)}, f32[16,256,256]{2,1,0:T(8,128)}) custom-call(s32[2]{0:T(128)S(1)} %pad_add_fusion.1.ids, s32[2,32]{1,0:T(2,128)S(1)} %bitcast.6, s32[2,64]{1,0:T(2,128)S(1)} %bitcast.11, bf16[1024,512]{1,0:T(8,128)(2,1)S(1)} %get-tuple-element.21.zown_ref, ...), custom_call_target="tpu_custom_call", output_to_operand_aliasing={{1}: (7, {})} | custom-call | flops 1 | bytes 524289 | tf_op jit(solution)/shard_map/near_pairs/pallas_call | solution.py:341
  26.3 0.0 collective-permute-done.6.one_ref
  26.3 0.1 collective-permute-start.8
  26.4 3.7 %collective-permute-done.4.two_ref = bf16[1040,256]{1,0:T(8,128)(2,1)S(1)} collective-permute-done((bf16[1040,256]{1,0:T(8,128)(2,1)S(1)}, bf16[1040,256]{1,0:T(8,128)(2,1)S(1)}, u32[]{:S(2)}, u32[]{:S(2)}) %collective-permute-start.4) | collective-permute-done | bytes 532512 | tf_op jit(solution)/shard_map/ppermute | solution.py:67
  30.1 3.7 %next_pairs.1 = (f32[1024,256]{1,0:T(8,128)S(1)}, bf16[1024,256]{1,0:T(8,128)(2,1)S(1)}, f32[16,256,256]{2,1,0:T(8,128)}) custom-call(s32[2]{0:T(128)S(1)} %pad_add_fusion.1.ids, s32[2,32]{1,0:T(2,128)S(1)} %bitcast.7, s32[2,64]{1,0:T(2,128)S(1)} %bitcast.12, bf16[1024,512]{1,0:T(8,128)(2,1)S(1)} %get-tuple-element.21.zown_ref, ...), custom_call_target="tpu_custom_call", output_to_operand_aliasing={{2}: (7, {})} | custom-call | flops 1 | bytes 1 | tf_op jit(solution)/shard_map/next_pairs/pallas_call | solution.py:341
  33.8 1.5 %collective-permute-done.2.own_ref = bf16[1040,256]{1,0:T(8,128)(2,1)S(1)} collective-permute-done((bf16[1040,256]{1,0:T(8,128)(2,1)S(1)}, bf16[1040,256]{1,0:T(8,128)(2,1)S(1)}, u32[]{:S(2)}, u32[]{:S(2)}) %collective-permute-start.2) | collective-permute-done | bytes 532512 | tf_op jit(solution)/shard_map/ppermute | solution.py:67
  35.2 0.2 collective-permute-start.7
  35.4 5.5 %collective-permute-done.8.own_ref = bf16[1040,256]{1,0:T(8,128)(2,1)S(1)} collective-permute-done((bf16[1040,256]{1,0:T(8,128)(2,1)S(1)}, bf16[1040,256]{1,0:T(8,128)(2,1)S(1)}, u32[]{:S(2)}, u32[]{:S(2)}) %collective-permute-start.8) | collective-permute-done | bytes 532512 | tf_op jit(solution)/shard_map/ppermute | solution.py:67
  41.0 0.5 %collective-permute-start.10 = (bf16[1024,256]{1,0:T(8,128)(2,1)S(1)}, bf16[1024,256]{1,0:T(8,128)(2,1)S(1)}, u32[]{:S(2)}, u32[]{:S(2)}) collective-permute-start(bf16[1024,256]{1,0:T(8,128)(2,1)S(1)} %get-tuple-element.36), channel_id=1, source_target_pairs={{0,1},{1,0},{2,3},{3,2},{4,5},{5,4},{6,7},{7,6},{8,9},{9,8},{10,11... | collective-permute-start | bytes 1572872 | tf_op jit(solution)/shard_map/ppermute | solution.py:71
  41.5 0.0 collective-permute-done.7.par_ref
  41.5 2.5 %zx_pairs.1 = (f32[1024,256]{1,0:T(8,128)S(1)}, f32[16,256,256]{2,1,0:T(8,128)}) custom-call(s32[2]{0:T(128)S(1)} %pad_add_fusion.1.ids, s32[2,32]{1,0:T(2,128)S(1)} %bitcast.8, s32[2,64]{1,0:T(2,128)S(1)} %bitcast.13, bf16[1024,512]{1,0:T(8,128)(2,1)S(1)} %get-tuple-element.21.zown_ref, ...), custom_call_target="tpu_custom_call", output_to_operand_aliasing={{1}: (7, {})} | custom-call | flops 1 | bytes 62914560 | tf_op jit(solution)/shard_map/zx_pairs/pallas_call | solution.py:341
  44.0 0.0 collective-permute-done.10.got_ref
  44.0 0.0 collective-permute-done.9.par_ref
  44.0 4.0 %last_pairs.1 = (bf16[1024,256]{1,0:T(8,128)(2,1)}, f32[16,256,256]{2,1,0:T(8,128)}) custom-call(s32[2]{0:T(128)S(1)} %pad_add_fusion.1.ids, s32[2,32]{1,0:T(2,128)S(1)} %bitcast.9, s32[2,64]{1,0:T(2,128)S(1)} %bitcast.14, bf16[1024,512]{1,0:T(8,128)(2,1)S(1)} %get-tuple-element.21.zown_ref, ...), custom_call_target="tpu_custom_call", output_to_operand_aliasing={{1}: (8, {})} | custom-call | flops 1 | bytes 4194305 | tf_op jit(solution)/shard_map/last_pairs/pallas_call | solution.py:341
  (4 shorter events, 0.0 us)
Async XLA Ops:
  2.5 4.3 %collective-permute-start = (bf16[1040,256]{1,0:T(8,128)(2,1)S(1)}, bf16[1040,256]{1,0:T(8,128)(2,1)S(1)}, u32[]{:S(2)}, u32[]{:S(2)}) collective-permute-start(bf16[1040,256]{1,0:T(8,128)(2,1)S(1)} %pad_add_fusion), channel_id=1, source_target_pairs={{0,1},{1,0},{2,3},{3,2},{4,5},{5,4},{6,7},{7,6},{8,9},{9,8},{10,11... | collective-permute-start | bytes 1597448 | tf_op jit(solution)/shard_map/ppermute | solution.py:71
  3.2 10.1 %collective-permute-start.5 = (bf16[1040,256]{1,0:T(8,128)(2,1)S(1)}, bf16[1040,256]{1,0:T(8,128)(2,1)S(1)}, u32[]{:S(2)}, u32[]{:S(2)}) collective-permute-start(bf16[1040,256]{1,0:T(8,128)(2,1)S(1)} %pad_add_fusion), channel_id=1, source_target_pairs={{0,2},{1,5},{2,0},{3,7},{4,6},{5,1},{6,4},{7,3},{8,10},{9,13},{10,... | collective-permute-start | bytes 1597448 | tf_op jit(solution)/shard_map/ppermute | solution.py:67
  3.2 18.7 %collective-permute-start.1 = (bf16[1040,256]{1,0:T(8,128)(2,1)S(1)}, bf16[1040,256]{1,0:T(8,128)(2,1)S(1)}, u32[]{:S(2)}, u32[]{:S(2)}) collective-permute-start(bf16[1040,256]{1,0:T(8,128)(2,1)S(1)} %pad_add_fusion), channel_id=1, source_target_pairs={{0,24},{1,25},{2,10},{3,11},{4,28},{5,29},{6,14},{7,15},{8,0},{9,1... | collective-permute-start | bytes 1597448 | tf_op jit(solution)/shard_map/ppermute | solution.py:67
  6.8 10.6 %collective-permute-start.3 = (bf16[1040,256]{1,0:T(8,128)(2,1)S(1)}, bf16[1040,256]{1,0:T(8,128)(2,1)S(1)}, u32[]{:S(2)}, u32[]{:S(2)}) collective-permute-start(bf16[1040,256]{1,0:T(8,128)(2,1)S(1)} %collective-permute-done.par_ref), channel_id=1, source_target_pairs={{0,2},{1,5},{2,0},{3,7},{4,6},{5,1},{6,4},{7,3},{8,10},{9,13},{10,... | collective-permute-start | bytes 1597448 | tf_op jit(solution)/shard_map/ppermute | solution.py:67
  8.1 1.0 %copy-start = (bf16[1024,256]{1,0:T(8,128)(2,1)S(1)}, bf16[1024,256]{1,0:T(8,128)(2,1)}, u32[]{:S(2)}) copy-start(bf16[1024,256]{1,0:T(8,128)(2,1)} %own_ref.1) | copy-start | bytes 1572868
  9.1 0.7 %copy-start.1 = (s32[32,2]{0,1:T(2,128)S(1)}, s32[32,2]{0,1:T(2,128)}, u32[]{:S(2)}) copy-start(s32[32,2]{0,1:T(2,128)} %param.4) | copy-start | bytes 772
  9.8 0.7 %copy-start.2 = (s32[64,2]{0,1:T(2,128)S(1)}, s32[64,2]{0,1:T(2,128)}, u32[]{:S(2)}) copy-start(s32[64,2]{0,1:T(2,128)} %param.5) | copy-start | bytes 1540
  13.3 12.9 %collective-permute-start.6 = (bf16[1040,256]{1,0:T(8,128)(2,1)S(1)}, bf16[1040,256]{1,0:T(8,128)(2,1)S(1)}, u32[]{:S(2)}, u32[]{:S(2)}) collective-permute-start(bf16[1040,256]{1,0:T(8,128)(2,1)S(1)} %collective-permute-done.5.own_ref), channel_id=1, source_target_pairs={{0,4},{1,8},{2,6},{3,11},{4,1},{5,29},{6,2},{7,31},{8,12},{9,16},{... | collective-permute-start | bytes 1597448 | tf_op jit(solution)/shard_map/ppermute | solution.py:67
  17.3 12.8 %collective-permute-start.4 = (bf16[1040,256]{1,0:T(8,128)(2,1)S(1)}, bf16[1040,256]{1,0:T(8,128)(2,1)S(1)}, u32[]{:S(2)}, u32[]{:S(2)}) collective-permute-start(bf16[1040,256]{1,0:T(8,128)(2,1)S(1)} %collective-permute-done.3.par_ref), channel_id=1, source_target_pairs={{0,4},{1,8},{2,6},{3,11},{4,1},{5,29},{6,2},{7,31},{8,12},{9,16},{... | collective-permute-start | bytes 1597448 | tf_op jit(solution)/shard_map/ppermute | solution.py:67
  22.0 13.3 %collective-permute-start.2 = (bf16[1040,256]{1,0:T(8,128)(2,1)S(1)}, bf16[1040,256]{1,0:T(8,128)(2,1)S(1)}, u32[]{:S(2)}, u32[]{:S(2)}) collective-permute-start(bf16[1040,256]{1,0:T(8,128)(2,1)S(1)} %collective-permute-done.1), channel_id=1, source_target_pairs={{0,2},{1,3},{2,0},{3,1},{4,6},{5,7},{6,4},{7,5},{8,10},{9,11},{10,... | collective-permute-start | bytes 1597448 | tf_op jit(solution)/shard_map/ppermute | solution.py:67
  26.3 14.7 %collective-permute-start.8 = (bf16[1040,256]{1,0:T(8,128)(2,1)S(1)}, bf16[1040,256]{1,0:T(8,128)(2,1)S(1)}, u32[]{:S(2)}, u32[]{:S(2)}) collective-permute-start(bf16[1040,256]{1,0:T(8,128)(2,1)S(1)} %collective-permute-done.6.one_ref), channel_id=1, source_target_pairs={{0,3},{1,8},{2,10},{3,1},{4,28},{5,7},{6,30},{7,5},{8,11},{9,16},{... | collective-permute-start | bytes 1597448 | tf_op jit(solution)/shard_map/ppermute | solution.py:67
  35.2 6.2 %collective-permute-start.7 = (bf16[1040,256]{1,0:T(8,128)(2,1)S(1)}, bf16[1040,256]{1,0:T(8,128)(2,1)S(1)}, u32[]{:S(2)}, u32[]{:S(2)}) collective-permute-start(bf16[1040,256]{1,0:T(8,128)(2,1)S(1)} %collective-permute-done.2.own_ref), channel_id=1, source_target_pairs={{0,1},{1,0},{2,3},{3,2},{4,5},{5,4},{6,7},{7,6},{8,9},{9,8},{10,11... | collective-permute-start | bytes 1597448 | tf_op jit(solution)/shard_map/ppermute | solution.py:71
  40.9 3.0 %collective-permute-start.9 = (bf16[1040,256]{1,0:T(8,128)(2,1)S(1)}, bf16[1040,256]{1,0:T(8,128)(2,1)S(1)}, u32[]{:S(2)}, u32[]{:S(2)}) collective-permute-start(bf16[1040,256]{1,0:T(8,128)(2,1)S(1)} %collective-permute-done.8.own_ref), channel_id=1, source_target_pairs={{0,1},{1,0},{2,3},{3,2},{4,5},{5,4},{6,7},{7,6},{8,9},{9,8},{10,11... | collective-permute-start | bytes 1597448 | tf_op jit(solution)/shard_map/ppermute | solution.py:71
  41.0 3.0 %collective-permute-start.10 = (bf16[1024,256]{1,0:T(8,128)(2,1)S(1)}, bf16[1024,256]{1,0:T(8,128)(2,1)S(1)}, u32[]{:S(2)}, u32[]{:S(2)}) collective-permute-start(bf16[1024,256]{1,0:T(8,128)(2,1)S(1)} %get-tuple-element.36), channel_id=1, source_target_pairs={{0,1},{1,0},{2,3},{3,2},{4,5},{5,4},{6,7},{7,6},{8,9},{9,8},{10,11... | collective-permute-start | bytes 1572872 | tf_op jit(solution)/shard_map/ppermute | solution.py:71

commit v5 on v4

--- a/solution.py
+++ b/solution.py
@@ -125,11 +125,12 @@
 def codes_of(rows, off):
     values = rows.astype(jnp.float32)
     row = lax.broadcasted_iota(jnp.int32, values.shape, 0)
+    values = jnp.where(row == 0, BLK_DEV * values, values)
     lane = lax.broadcasted_iota(jnp.int32, values.shape, 1)
     first = jnp.maximum(-off, 0) * CAP
     return [
         jnp.sum(
-            jnp.where(jnp.logical_and(row == 0, lane == first + slot), values, 0.0)
+            jnp.where(jnp.logical_and(row < 2, lane == first + slot), values, 0.0)
         ).astype(jnp.int32)
         for slot in range(CAP)
     ]
@@ -312,7 +313,7 @@
     return pl.CostEstimate(flops=1, bytes_accessed=1 + int(mib * 2**20), transcendentals=0)
 
 
-EST = {"last": 4, "near": 0.5, "next": 0, "self": 2, "zx_p": 60}
+EST = {"last": 0, "near": 20, "next": 0.5, "self": 2, "zx_p": 60}
 
 
 def run_self(ids, table, wins, own, par):
@@ -356,14 +357,11 @@
     )(*inputs, corr)
 
 
-def with_table(spectra, table, position):
+def with_table(spectra, table):
     rows, width = spectra.shape
-    first = table[:1] - position * BLK_DEV
-    group = lax.broadcasted_iota(jnp.int32, first.shape, 1) // CAP
-    second = table[1:] - (position + group) * BLK_DEV
-    code = jnp.where(table[:1] >= 0, first * BLK_DEV + second, -1).astype(spectra.dtype)
-    code = jnp.pad(code, ((rows, TABLE - 1), (0, width - code.shape[1])))
-    return jnp.pad(spectra, ((0, TABLE), (0, 0))) + code
+    below = jnp.pad(table, ((rows, TABLE - 2), (0, width - table.shape[1])))
+    below = jnp.where(below >= 0, lax.rem(below, BLK_DEV), -1).astype(spectra.dtype)
+    return jnp.pad(spectra, ((0, TABLE), (0, 0))) + below
 
 
 def body(spectra, pair_blocks, windows):
@@ -372,7 +370,7 @@
     rows, width = spectra.shape
     both = 2 * width
     table, wins = pair_blocks.T, windows.T
-    unit = with_table(spectra, table, position)
+    unit = with_table(spectra, table)
     par = swap(unit)
     near_own = send(unit, move_near)
     from_z = send(unit, move_z)
@@ -380,11 +378,12 @@
     ids = jnp.stack([position, lax.axis_index("samp")]).astype(jnp.int32)
     scalars = (ids, table, wins)
     zown, acc, corr = run_self(ids, table, wins, spectra, par)
-    near_own, _ = hold((near_own, acc))
-    next_own = send(near_own, move_next)
     from_z, _ = hold((from_z, acc))
     zx = send(from_z, move_x)
+    near_par, acc = hold((near_par, acc))
     next_par = send(near_par, move_next)
+    next_own = send(near_own, move_next)
+    near_par, acc = hold((near_par, acc))
     acc, corr = run_unit(
         near_kernel,
         "near_pairs",
@@ -394,7 +393,6 @@
     )
     next_own, _ = hold((next_own, acc))
     last = send(next_own, move_last)
-    next_par, acc = hold((next_par, acc))
     acc, give, corr = run_unit(
         next_kernel,
         "next_pairs",

time: 48.2 us -> 46.1 us (0.956)
  the two profiles are of different devices: /device:TPU:5 before, /device:TPU:1 now
where the time goes in v5:
time: 46.1 us; the launch traced here: 45.9 us
  Pallas kernels  15.6 us (34%)
  starting transfers between devices  15.3 us (33%)
  waiting for transfers between devices  13 us (28%)
  other arithmetic  1.23 us (3%)
  between operations  0.72 us (2%)
    ppermute x7, starting transfers between devices, send(): return lax.ppermute(value, ('feat', 'samp'), pairs)  13.4 us
    ppermute x7, waiting for transfers between devices, send(): return lax.ppermute(value, ('feat', 'samp'), pairs)  13 us
    pallas_call x4, Pallas kernels, run_unit(): pl.pallas_call(kernel, out_shape=(*outs, jax.ShapeDtypeStruct(corr.shape,...  12.8 us
    pallas_call x1, Pallas kernels, run_self(): pl.pallas_call(self_kernel, out_shape=(jax.ShapeDtypeStruct((rows, 2 * wi...  2.83 us
    ppermute x4, starting transfers between devices, swap(): return lax.ppermute(value, 'samp', [(0, 1), (1, 0)])  1.94 us
    add x1, other arithmetic, with_table(): return jnp.pad(spectra, ((0, TABLE), (0, 0))) + below  1.15 us
  transfers between devices with their start and end apart: 11, of which 5 were waited for; matrix products, arithmetic and copies ran while one was open for 0% of the time, Pallas kernels for 27%

profile of v5, /device:TPU:1, one launch (start us, length us, event | category | flops | bytes accessed | tf_op | source)
XLA Modules:
  0.0 45.9 jit_solution(2143347890795544379)
XLA Ops:
  0.6 0.0 copy-start.1
  0.6 0.0 copy-start
  0.6 0.0 copy-start.2
  0.7 1.2 %fusion.3 = bf16[1040,256]{1,0:T(8,128)(2,1)S(1)} fusion(s32[2,32]{1,0:T(2,128)} %bitcast.4, bf16[1024,256]{1,0:T(8,128)(2,1)} %own_ref.1), kind=kLoop, calls=%fused_computation.8 | loop fusion | flops 3461120 | bytes 1057024 | tf_op jit(solution)/shard_map/add | solution.py:364
  1.8 0.1 collective-permute-start
  1.9 2.7 %collective-permute-start.4 = (bf16[1040,256]{1,0:T(8,128)(2,1)S(1)}, bf16[1040,256]{1,0:T(8,128)(2,1)S(1)}, u32[]{:S(2)}, u32[]{:S(2)}) collective-permute-start(bf16[1040,256]{1,0:T(8,128)(2,1)S(1)} %fusion.3), channel_id=1, source_target_pairs={{0,2},{1,5},{2,0},{3,7},{4,6},{5,1},{6,4},{7,3},{8,10},{9,13},{10,... | collective-permute-start | bytes 1597448 | tf_op jit(solution)/shard_map/ppermute | solution.py:67
  4.6 3.3 %collective-permute-start.1 = (bf16[1040,256]{1,0:T(8,128)(2,1)S(1)}, bf16[1040,256]{1,0:T(8,128)(2,1)}, u32[]{:S(2)}, u32[]{:S(2)}) collective-permute-start(bf16[1040,256]{1,0:T(8,128)(2,1)S(1)} %fusion.3), channel_id=1, source_target_pairs={{0,24},{1,25},{2,10},{3,11},{4,28},{5,29},{6,14},{7,15},{8,0},{9,1... | collective-permute-start | bytes 1597448 | tf_op jit(solution)/shard_map/ppermute | solution.py:67
  7.9 0.0 collective-permute-done.par_ref
  7.9 0.2 collective-permute-start.3
  8.2 3.5 %collective-permute-done.4.own_ref = bf16[1040,256]{1,0:T(8,128)(2,1)S(1)} collective-permute-done((bf16[1040,256]{1,0:T(8,128)(2,1)S(1)}, bf16[1040,256]{1,0:T(8,128)(2,1)S(1)}, u32[]{:S(2)}, u32[]{:S(2)}) %collective-permute-start.4) | collective-permute-done | bytes 532512 | tf_op jit(solution)/shard_map/ppermute | solution.py:67
  11.7 2.2 %collective-permute-start.5 = (bf16[1040,256]{1,0:T(8,128)(2,1)S(1)}, bf16[1040,256]{1,0:T(8,128)(2,1)S(1)}, u32[]{:S(2)}, u32[]{:S(2)}) collective-permute-start(bf16[1040,256]{1,0:T(8,128)(2,1)S(1)} %collective-permute-done.4.own_ref), channel_id=1, source_target_pairs={{0,4},{1,8},{2,6},{3,11},{4,1},{5,29},{6,2},{7,31},{8,12},{9,16},{... | collective-permute-start | bytes 1597448 | tf_op jit(solution)/shard_map/ppermute | solution.py:67
  13.9 0.1 pad_add_fusion.ids
  14.0 2.8 %self_pairs.1 = (bf16[1024,512]{1,0:T(8,128)(2,1)S(1)}, f32[1024,256]{1,0:T(8,128)S(1)}, f32[16,256,256]{2,1,0:T(8,128)}) custom-call(s32[2]{0:T(128)S(1)} %pad_add_fusion.ids, s32[2,32]{1,0:T(2,128)S(1)} %bitcast.5, s32[2,64]{1,0:T(2,128)S(1)} %bitcast.10, bf16[1024,256]{1,0:T(8,128)(2,1)S(1)} %copy-done, bf16[1040,256]{1,0:T(8,128)(2,1)S(1)} %collective-permute-done.par_ref), custom_call_target="tpu_custom_call" | custom-call | flops 1 | bytes 2097153 | tf_op jit(solution)/shard_map/self_pairs/pallas_call | solution.py:321
  16.8 2.3 %collective-permute-done.1 = bf16[1040,256]{1,0:T(8,128)(2,1)} collective-permute-done((bf16[1040,256]{1,0:T(8,128)(2,1)S(1)}, bf16[1040,256]{1,0:T(8,128)(2,1)}, u32[]{:S(2)}, u32[]{:S(2)}) %collective-permute-start.1) | collective-permute-done | bytes 532512 | tf_op jit(solution)/shard_map/ppermute | solution.py:67
  19.1 2.0 %collective-permute-start.2 = (bf16[1040,256]{1,0:T(8,128)(2,1)}, bf16[1040,256]{1,0:T(8,128)(2,1)S(1)}, u32[]{:S(2)}, u32[]{:S(2)}) collective-permute-start(bf16[1040,256]{1,0:T(8,128)(2,1)} %collective-permute-done.1), channel_id=1, source_target_pairs={{0,2},{1,3},{2,0},{3,1},{4,6},{5,7},{6,4},{7,5},{8,10},{9,11},{10,... | collective-permute-start | bytes 1597448 | tf_op jit(solution)/shard_map/ppermute | solution.py:67
  21.2 0.0 collective-permute-done.3.par_ref
  21.2 0.4 collective-permute-start.6
  21.6 3.3 %near_pairs.1 = (f32[1024,512]{1,0:T(8,128)S(1)}, f32[16,256,256]{2,1,0:T(8,128)}) custom-call(s32[2]{0:T(128)S(1)} %pad_add_fusion.ids, s32[2,32]{1,0:T(2,128)S(1)} %bitcast.6, s32[2,64]{1,0:T(2,128)S(1)} %bitcast.11, bf16[1024,512]{1,0:T(8,128)(2,1)S(1)} %get-tuple-element.21.zown_ref, ...), custom_call_target="tpu_custom_call", output_to_operand_aliasing={{1}: (7, {})} | custom-call | flops 1 | bytes 20971520 | tf_op jit(solution)/shard_map/near_pairs/pallas_call | solution.py:342
  24.8 0.8 %collective-permute-done.5.one_ref = bf16[1040,256]{1,0:T(8,128)(2,1)S(1)} collective-permute-done((bf16[1040,256]{1,0:T(8,128)(2,1)S(1)}, bf16[1040,256]{1,0:T(8,128)(2,1)S(1)}, u32[]{:S(2)}, u32[]{:S(2)}) %collective-permute-start.5) | collective-permute-done | bytes 532512 | tf_op jit(solution)/shard_map/ppermute | solution.py:67
  25.6 2.5 %collective-permute-start.8 = (bf16[1040,256]{1,0:T(8,128)(2,1)S(1)}, bf16[1040,256]{1,0:T(8,128)(2,1)S(1)}, u32[]{:S(2)}, u32[]{:S(2)}) collective-permute-start(bf16[1040,256]{1,0:T(8,128)(2,1)S(1)} %collective-permute-done.5.one_ref), channel_id=1, source_target_pairs={{0,3},{1,8},{2,10},{3,1},{4,28},{5,7},{6,30},{7,5},{8,11},{9,16},{... | collective-permute-start | bytes 1597448 | tf_op jit(solution)/shard_map/ppermute | solution.py:67
  28.1 3.2 %collective-permute-done.6.two_ref = bf16[1040,256]{1,0:T(8,128)(2,1)S(1)} collective-permute-done((bf16[1040,256]{1,0:T(8,128)(2,1)S(1)}, bf16[1040,256]{1,0:T(8,128)(2,1)S(1)}, u32[]{:S(2)}, u32[]{:S(2)}) %collective-permute-start.6) | collective-permute-done | bytes 532512 | tf_op jit(solution)/shard_map/ppermute | solution.py:67
  31.3 3.7 %next_pairs.1 = (f32[1024,256]{1,0:T(8,128)S(1)}, bf16[1024,256]{1,0:T(8,128)(2,1)S(1)}, f32[16,256,256]{2,1,0:T(8,128)}) custom-call(s32[2]{0:T(128)S(1)} %pad_add_fusion.ids, s32[2,32]{1,0:T(2,128)S(1)} %bitcast.7, s32[2,64]{1,0:T(2,128)S(1)} %bitcast.12, bf16[1024,512]{1,0:T(8,128)(2,1)S(1)} %get-tuple-element.21.zown_ref, ...), custom_call_target="tpu_custom_call", output_to_operand_aliasing={{2}: (7, {})} | custom-call | flops 1 | bytes 524289 | tf_op jit(solution)/shard_map/next_pairs/pallas_call | solution.py:342
  35.0 0.0 collective-permute-done.2.own_ref
  35.0 1.3 %collective-permute-start.7 = (bf16[1040,256]{1,0:T(8,128)(2,1)S(1)}, bf16[1040,256]{1,0:T(8,128)(2,1)S(1)}, u32[]{:S(2)}, u32[]{:S(2)}) collective-permute-start(bf16[1040,256]{1,0:T(8,128)(2,1)S(1)} %collective-permute-done.2.own_ref), channel_id=1, source_target_pairs={{0,1},{1,0},{2,3},{3,2},{4,5},{5,4},{6,7},{7,6},{8,9},{9,8},{10,11... | collective-permute-start | bytes 1597448 | tf_op jit(solution)/shard_map/ppermute | solution.py:71
  36.3 3.1 %collective-permute-done.8.own_ref = bf16[1040,256]{1,0:T(8,128)(2,1)S(1)} collective-permute-done((bf16[1040,256]{1,0:T(8,128)(2,1)S(1)}, bf16[1040,256]{1,0:T(8,128)(2,1)S(1)}, u32[]{:S(2)}, u32[]{:S(2)}) %collective-permute-start.8) | collective-permute-done | bytes 532512 | tf_op jit(solution)/shard_map/ppermute | solution.py:67
  39.5 0.0 collective-permute-start.9
  39.5 0.5 %collective-permute-start.10 = (bf16[1024,256]{1,0:T(8,128)(2,1)S(1)}, bf16[1024,256]{1,0:T(8,128)(2,1)S(1)}, u32[]{:S(2)}, u32[]{:S(2)}) collective-permute-start(bf16[1024,256]{1,0:T(8,128)(2,1)S(1)} %get-tuple-element.36), channel_id=1, source_target_pairs={{0,1},{1,0},{2,3},{3,2},{4,5},{5,4},{6,7},{7,6},{8,9},{9,8},{10,11... | collective-permute-start | bytes 1572872 | tf_op jit(solution)/shard_map/ppermute | solution.py:71
  40.0 0.0 collective-permute-done.7.par_ref
  40.0 2.5 %zx_pairs.1 = (f32[1024,256]{1,0:T(8,128)S(1)}, f32[16,256,256]{2,1,0:T(8,128)}) custom-call(s32[2]{0:T(128)S(1)} %pad_add_fusion.ids, s32[2,32]{1,0:T(2,128)S(1)} %bitcast.8, s32[2,64]{1,0:T(2,128)S(1)} %bitcast.13, bf16[1024,512]{1,0:T(8,128)(2,1)S(1)} %get-tuple-element.21.zown_ref, ...), custom_call_target="tpu_custom_call", output_to_operand_aliasing={{1}: (7, {})} | custom-call | flops 1 | bytes 62914560 | tf_op jit(solution)/shard_map/zx_pairs/pallas_call | solution.py:342
  42.5 0.0 collective-permute-done.10.got_ref
  42.5 0.0 collective-permute-done.9.par_ref
  42.5 3.4 %last_pairs.1 = (bf16[1024,256]{1,0:T(8,128)(2,1)}, f32[16,256,256]{2,1,0:T(8,128)}) custom-call(s32[2]{0:T(128)S(1)} %pad_add_fusion.ids, s32[2,32]{1,0:T(2,128)S(1)} %bitcast.9, s32[2,64]{1,0:T(2,128)S(1)} %bitcast.14, bf16[1024,512]{1,0:T(8,128)(2,1)S(1)} %get-tuple-element.21.zown_ref, ...), custom_call_target="tpu_custom_call", output_to_operand_aliasing={{1}: (8, {})} | custom-call | flops 1 | bytes 1 | tf_op jit(solution)/shard_map/last_pairs/pallas_call | solution.py:342
  (3 shorter events, 0.0 us)
Async XLA Ops:
  0.6 13.4 %copy-start.1 = (s32[32,2]{0,1:T(2,128)S(1)}, s32[32,2]{0,1:T(2,128)}, u32[]{:S(2)}) copy-start(s32[32,2]{0,1:T(2,128)} %param.4) | copy-start | bytes 772
  0.6 13.4 %copy-start = (bf16[1024,256]{1,0:T(8,128)(2,1)S(1)}, bf16[1024,256]{1,0:T(8,128)(2,1)}, u32[]{:S(2)}) copy-start(bf16[1024,256]{1,0:T(8,128)(2,1)} %own_ref.1) | copy-start | bytes 1572868
  0.6 13.3 %copy-start.2 = (s32[64,2]{0,1:T(2,128)S(1)}, s32[64,2]{0,1:T(2,128)}, u32[]{:S(2)}) copy-start(s32[64,2]{0,1:T(2,128)} %param.5) | copy-start | bytes 1540
  1.8 6.1 %collective-permute-start = (bf16[1040,256]{1,0:T(8,128)(2,1)S(1)}, bf16[1040,256]{1,0:T(8,128)(2,1)S(1)}, u32[]{:S(2)}, u32[]{:S(2)}) collective-permute-start(bf16[1040,256]{1,0:T(8,128)(2,1)S(1)} %fusion.3), channel_id=1, source_target_pairs={{0,1},{1,0},{2,3},{3,2},{4,5},{5,4},{6,7},{7,6},{8,9},{9,8},{10,11... | collective-permute-start | bytes 1597448 | tf_op jit(solution)/shard_map/ppermute | solution.py:71
  1.9 9.7 %collective-permute-start.4 = (bf16[1040,256]{1,0:T(8,128)(2,1)S(1)}, bf16[1040,256]{1,0:T(8,128)(2,1)S(1)}, u32[]{:S(2)}, u32[]{:S(2)}) collective-permute-start(bf16[1040,256]{1,0:T(8,128)(2,1)S(1)} %fusion.3), channel_id=1, source_target_pairs={{0,2},{1,5},{2,0},{3,7},{4,6},{5,1},{6,4},{7,3},{8,10},{9,13},{10,... | collective-permute-start | bytes 1597448 | tf_op jit(solution)/shard_map/ppermute | solution.py:67
  4.6 14.5 %collective-permute-start.1 = (bf16[1040,256]{1,0:T(8,128)(2,1)S(1)}, bf16[1040,256]{1,0:T(8,128)(2,1)}, u32[]{:S(2)}, u32[]{:S(2)}) collective-permute-start(bf16[1040,256]{1,0:T(8,128)(2,1)S(1)} %fusion.3), channel_id=1, source_target_pairs={{0,24},{1,25},{2,10},{3,11},{4,28},{5,29},{6,14},{7,15},{8,0},{9,1... | collective-permute-start | bytes 1597448 | tf_op jit(solution)/shard_map/ppermute | solution.py:67
  7.9 13.2 %collective-permute-start.3 = (bf16[1040,256]{1,0:T(8,128)(2,1)S(1)}, bf16[1040,256]{1,0:T(8,128)(2,1)S(1)}, u32[]{:S(2)}, u32[]{:S(2)}) collective-permute-start(bf16[1040,256]{1,0:T(8,128)(2,1)S(1)} %collective-permute-done.par_ref), channel_id=1, source_target_pairs={{0,2},{1,5},{2,0},{3,7},{4,6},{5,1},{6,4},{7,3},{8,10},{9,13},{10,... | collective-permute-start | bytes 1597448 | tf_op jit(solution)/shard_map/ppermute | solution.py:67
  11.7 13.9 %collective-permute-start.5 = (bf16[1040,256]{1,0:T(8,128)(2,1)S(1)}, bf16[1040,256]{1,0:T(8,128)(2,1)S(1)}, u32[]{:S(2)}, u32[]{:S(2)}) collective-permute-start(bf16[1040,256]{1,0:T(8,128)(2,1)S(1)} %collective-permute-done.4.own_ref), channel_id=1, source_target_pairs={{0,4},{1,8},{2,6},{3,11},{4,1},{5,29},{6,2},{7,31},{8,12},{9,16},{... | collective-permute-start | bytes 1597448 | tf_op jit(solution)/shard_map/ppermute | solution.py:67
  19.1 15.8 %collective-permute-start.2 = (bf16[1040,256]{1,0:T(8,128)(2,1)}, bf16[1040,256]{1,0:T(8,128)(2,1)S(1)}, u32[]{:S(2)}, u32[]{:S(2)}) collective-permute-start(bf16[1040,256]{1,0:T(8,128)(2,1)} %collective-permute-done.1), channel_id=1, source_target_pairs={{0,2},{1,3},{2,0},{3,1},{4,6},{5,7},{6,4},{7,5},{8,10},{9,11},{10,... | collective-permute-start | bytes 1597448 | tf_op jit(solution)/shard_map/ppermute | solution.py:67
  21.2 10.1 %collective-permute-start.6 = (bf16[1040,256]{1,0:T(8,128)(2,1)S(1)}, bf16[1040,256]{1,0:T(8,128)(2,1)S(1)}, u32[]{:S(2)}, u32[]{:S(2)}) collective-permute-start(bf16[1040,256]{1,0:T(8,128)(2,1)S(1)} %collective-permute-done.3.par_ref), channel_id=1, source_target_pairs={{0,4},{1,8},{2,6},{3,11},{4,1},{5,29},{6,2},{7,31},{8,12},{9,16},{... | collective-permute-start | bytes 1597448 | tf_op jit(solution)/shard_map/ppermute | solution.py:67
  25.6 13.8 %collective-permute-start.8 = (bf16[1040,256]{1,0:T(8,128)(2,1)S(1)}, bf16[1040,256]{1,0:T(8,128)(2,1)S(1)}, u32[]{:S(2)}, u32[]{:S(2)}) collective-permute-start(bf16[1040,256]{1,0:T(8,128)(2,1)S(1)} %collective-permute-done.5.one_ref), channel_id=1, source_target_pairs={{0,3},{1,8},{2,10},{3,1},{4,28},{5,7},{6,30},{7,5},{8,11},{9,16},{... | collective-permute-start | bytes 1597448 | tf_op jit(solution)/shard_map/ppermute | solution.py:67
  35.0 5.0 %collective-permute-start.7 = (bf16[1040,256]{1,0:T(8,128)(2,1)S(1)}, bf16[1040,256]{1,0:T(8,128)(2,1)S(1)}, u32[]{:S(2)}, u32[]{:S(2)}) collective-permute-start(bf16[1040,256]{1,0:T(8,128)(2,1)S(1)} %collective-permute-done.2.own_ref), channel_id=1, source_target_pairs={{0,1},{1,0},{2,3},{3,2},{4,5},{5,4},{6,7},{7,6},{8,9},{9,8},{10,11... | collective-permute-start | bytes 1597448 | tf_op jit(solution)/shard_map/ppermute | solution.py:71
  39.5 3.0 %collective-permute-start.9 = (bf16[1040,256]{1,0:T(8,128)(2,1)S(1)}, bf16[1040,256]{1,0:T(8,128)(2,1)S(1)}, u32[]{:S(2)}, u32[]{:S(2)}) collective-permute-start(bf16[1040,256]{1,0:T(8,128)(2,1)S(1)} %collective-permute-done.8.own_ref), channel_id=1, source_target_pairs={{0,1},{1,0},{2,3},{3,2},{4,5},{5,4},{6,7},{7,6},{8,9},{9,8},{10,11... | collective-permute-start | bytes 1597448 | tf_op jit(solution)/shard_map/ppermute | solution.py:71
  39.5 3.0 %collective-permute-start.10 = (bf16[1024,256]{1,0:T(8,128)(2,1)S(1)}, bf16[1024,256]{1,0:T(8,128)(2,1)S(1)}, u32[]{:S(2)}, u32[]{:S(2)}) collective-permute-start(bf16[1024,256]{1,0:T(8,128)(2,1)S(1)} %get-tuple-element.36), channel_id=1, source_target_pairs={{0,1},{1,0},{2,3},{3,2},{4,5},{5,4},{6,7},{7,6},{8,9},{9,8},{10,11... | collective-permute-start | bytes 1572872 | tf_op jit(solution)/shard_map/ppermute | solution.py:71

commit v6 on v5

--- a/solution.py
+++ b/solution.py
@@ -313,7 +313,7 @@
     return pl.CostEstimate(flops=1, bytes_accessed=1 + int(mib * 2**20), transcendentals=0)
 
 
-EST = {"last": 0, "near": 20, "next": 0.5, "self": 2, "zx_p": 60}
+EST = {"last": 4, "near": 8, "next": 0, "self": 0.5, "zx_p": 1}
 
 
 def run_self(ids, table, wins, own, par):
@@ -377,12 +377,14 @@
     near_par = send(par, move_near)
     ids = jnp.stack([position, lax.axis_index("samp")]).astype(jnp.int32)
     scalars = (ids, table, wins)
+    ids, near_own = hold((ids, near_own))
+    scalars = (ids, table, wins)
     zown, acc, corr = run_self(ids, table, wins, spectra, par)
-    from_z, _ = hold((from_z, acc))
-    zx = send(from_z, move_x)
+    near_own, _ = hold((near_own, acc))
+    next_own = send(near_own, move_next)
     near_par, acc = hold((near_par, acc))
     next_par = send(near_par, move_next)
-    next_own = send(near_own, move_next)
+    zx = send(from_z, move_x)
     near_par, acc = hold((near_par, acc))
     acc, corr = run_unit(
         near_kernel,

time: 46.1 us -> 45.8 us (level)
  waiting for transfers between devices: 13 us -> 12 us
  starting transfers between devices: 15.3 us -> 16 us
    ppermute x7, waiting for transfers between devices: 13 us -> 11.9 us  [send(): return lax.ppermute(value, ('feat', 'samp'), pairs)]
    ppermute x7, starting transfers between devices: 13.4 us -> 14.3 us  [send(): return lax.ppermute(value, ('feat', 'samp'), pairs)]
where the time goes in v6:
time: 45.8 us; the launch traced here: 45.6 us
  starting transfers between devices  16 us (35%)
  Pallas kernels  15.6 us (34%)
  waiting for transfers between devices  12 us (26%)
  other arithmetic  1.23 us (3%)
  between operations  0.73 us (2%)
    ppermute x7, starting transfers between devices, send(): return lax.ppermute(value, ('feat', 'samp'), pairs)  14.3 us
    pallas_call x4, Pallas kernels, run_unit(): pl.pallas_call(kernel, out_shape=(*outs, jax.ShapeDtypeStruct(corr.shape,...  12.8 us
    ppermute x7, waiting for transfers between devices, send(): return lax.ppermute(value, ('feat', 'samp'), pairs)  11.9 us
    pallas_call x1, Pallas kernels, run_self(): pl.pallas_call(self_kernel, out_shape=(jax.ShapeDtypeStruct((rows, 2 * wi...  2.83 us
    ppermute x4, starting transfers between devices, swap(): return lax.ppermute(value, 'samp', [(0, 1), (1, 0)])  1.73 us
    add x1, other arithmetic, with_table(): return jnp.pad(spectra, ((0, TABLE), (0, 0))) + below  1.15 us
  transfers between devices with their start and end apart: 11, of which 5 were waited for; matrix products, arithmetic and copies ran while one was open for 0% of the time, Pallas kernels for 27%

profile of v6, /device:TPU:1, one launch (start us, length us, event | category | flops | bytes accessed | tf_op | source)
XLA Modules:
  0.0 45.6 jit_solution(12078848623751444337)
XLA Ops:
  0.6 0.0 copy-start.1
  0.6 0.0 copy-start
  0.6 0.0 copy-start.2
  0.7 1.2 %fusion.3 = bf16[1040,256]{1,0:T(8,128)(2,1)S(1)} fusion(s32[2,32]{1,0:T(2,128)} %bitcast.4, bf16[1024,256]{1,0:T(8,128)(2,1)} %own_ref.1), kind=kLoop, calls=%fused_computation.8 | loop fusion | flops 3461120 | bytes 1057024 | tf_op jit(solution)/shard_map/add | solution.py:364
  1.8 0.1 collective-permute-start.1
  1.9 2.7 %collective-permute-start = (bf16[1040,256]{1,0:T(8,128)(2,1)S(1)}, bf16[1040,256]{1,0:T(8,128)(2,1)S(1)}, u32[]{:S(2)}, u32[]{:S(2)}) collective-permute-start(bf16[1040,256]{1,0:T(8,128)(2,1)S(1)} %fusion.3), channel_id=1, source_target_pairs={{0,2},{1,5},{2,0},{3,7},{4,6},{5,1},{6,4},{7,3},{8,10},{9,13},{10,... | collective-permute-start | bytes 1597448 | tf_op jit(solution)/shard_map/ppermute | solution.py:67
  4.6 3.3 %collective-permute-start.2 = (bf16[1040,256]{1,0:T(8,128)(2,1)S(1)}, bf16[1040,256]{1,0:T(8,128)(2,1)S(1)}, u32[]{:S(2)}, u32[]{:S(2)}) collective-permute-start(bf16[1040,256]{1,0:T(8,128)(2,1)S(1)} %fusion.3), channel_id=1, source_target_pairs={{0,24},{1,25},{2,10},{3,11},{4,28},{5,29},{6,14},{7,15},{8,0},{9,1... | collective-permute-start | bytes 1597448 | tf_op jit(solution)/shard_map/ppermute | solution.py:67
  7.9 0.1 pad_add_fusion.ids
  8.0 0.0 collective-permute-done.1.par_ref
  8.0 0.2 collective-permute-start.4
  8.3 3.3 %collective-permute-done.own_ref = bf16[1040,256]{1,0:T(8,128)(2,1)S(1)} collective-permute-done((bf16[1040,256]{1,0:T(8,128)(2,1)S(1)}, bf16[1040,256]{1,0:T(8,128)(2,1)S(1)}, u32[]{:S(2)}, u32[]{:S(2)}) %collective-permute-start) | collective-permute-done | bytes 532512 | tf_op jit(solution)/shard_map/ppermute | solution.py:67
  11.6 2.8 %self_pairs.1 = (bf16[1024,512]{1,0:T(8,128)(2,1)S(1)}, f32[1024,256]{1,0:T(8,128)S(1)}, f32[16,256,256]{2,1,0:T(8,128)}) custom-call(s32[2]{0:T(128)S(1)} %pad_add_fusion.ids, s32[2,32]{1,0:T(2,128)S(1)} %bitcast.5, s32[2,64]{1,0:T(2,128)S(1)} %bitcast.10, bf16[1024,256]{1,0:T(8,128)(2,1)S(1)} %copy-done, bf16[1040,256]{1,0:T(8,128)(2,1)S(1)} %collective-permute-done.1.par_ref), custom_call_target="tpu_custom_call" | custom-call | flops 1 | bytes 524289 | tf_op jit(solution)/shard_map/self_pairs/pallas_call | solution.py:321
  14.4 3.2 %collective-permute-start.5 = (bf16[1040,256]{1,0:T(8,128)(2,1)S(1)}, bf16[1040,256]{1,0:T(8,128)(2,1)S(1)}, u32[]{:S(2)}, u32[]{:S(2)}) collective-permute-start(bf16[1040,256]{1,0:T(8,128)(2,1)S(1)} %collective-permute-done.own_ref), channel_id=1, source_target_pairs={{0,4},{1,8},{2,6},{3,11},{4,1},{5,29},{6,2},{7,31},{8,12},{9,16},{... | collective-permute-start | bytes 1597448 | tf_op jit(solution)/shard_map/ppermute | solution.py:67
  17.6 1.5 %collective-permute-done.2 = bf16[1040,256]{1,0:T(8,128)(2,1)S(1)} collective-permute-done((bf16[1040,256]{1,0:T(8,128)(2,1)S(1)}, bf16[1040,256]{1,0:T(8,128)(2,1)S(1)}, u32[]{:S(2)}, u32[]{:S(2)}) %collective-permute-start.2) | collective-permute-done | bytes 532512 | tf_op jit(solution)/shard_map/ppermute | solution.py:67
  19.1 2.0 %collective-permute-start.3 = (bf16[1040,256]{1,0:T(8,128)(2,1)S(1)}, bf16[1040,256]{1,0:T(8,128)(2,1)S(1)}, u32[]{:S(2)}, u32[]{:S(2)}) collective-permute-start(bf16[1040,256]{1,0:T(8,128)(2,1)S(1)} %collective-permute-done.2), channel_id=1, source_target_pairs={{0,2},{1,3},{2,0},{3,1},{4,6},{5,7},{6,4},{7,5},{8,10},{9,11},{10,... | collective-permute-start | bytes 1597448 | tf_op jit(solution)/shard_map/ppermute | solution.py:67
  21.1 0.0 collective-permute-done.4.par_ref
  21.1 0.4 collective-permute-start.6
  21.5 3.3 %near_pairs.1 = (f32[1024,512]{1,0:T(8,128)S(1)}, f32[16,256,256]{2,1,0:T(8,128)}) custom-call(s32[2]{0:T(128)S(1)} %pad_add_fusion.ids, s32[2,32]{1,0:T(2,128)S(1)} %bitcast.6, s32[2,64]{1,0:T(2,128)S(1)} %bitcast.11, bf16[1024,512]{1,0:T(8,128)(2,1)S(1)} %get-tuple-element.24.zown_ref, ...), custom_call_target="tpu_custom_call", output_to_operand_aliasing={{1}: (7, {})} | custom-call | flops 1 | bytes 8388609 | tf_op jit(solution)/shard_map/near_pairs/pallas_call | solution.py:342
  24.8 0.8 %collective-permute-done.5.one_ref = bf16[1040,256]{1,0:T(8,128)(2,1)S(1)} collective-permute-done((bf16[1040,256]{1,0:T(8,128)(2,1)S(1)}, bf16[1040,256]{1,0:T(8,128)(2,1)S(1)}, u32[]{:S(2)}, u32[]{:S(2)}) %collective-permute-start.5) | collective-permute-done | bytes 532512 | tf_op jit(solution)/shard_map/ppermute | solution.py:67
  25.6 2.5 %collective-permute-start.8 = (bf16[1040,256]{1,0:T(8,128)(2,1)S(1)}, bf16[1040,256]{1,0:T(8,128)(2,1)S(1)}, u32[]{:S(2)}, u32[]{:S(2)}) collective-permute-start(bf16[1040,256]{1,0:T(8,128)(2,1)S(1)} %collective-permute-done.5.one_ref), channel_id=1, source_target_pairs={{0,3},{1,8},{2,10},{3,1},{4,28},{5,7},{6,30},{7,5},{8,11},{9,16},{... | collective-permute-start | bytes 1597448 | tf_op jit(solution)/shard_map/ppermute | solution.py:67
  28.1 3.2 %collective-permute-done.6.two_ref = bf16[1040,256]{1,0:T(8,128)(2,1)S(1)} collective-permute-done((bf16[1040,256]{1,0:T(8,128)(2,1)S(1)}, bf16[1040,256]{1,0:T(8,128)(2,1)S(1)}, u32[]{:S(2)}, u32[]{:S(2)}) %collective-permute-start.6) | collective-permute-done | bytes 532512 | tf_op jit(solution)/shard_map/ppermute | solution.py:67
  31.3 3.7 %next_pairs.1 = (f32[1024,256]{1,0:T(8,128)S(1)}, bf16[1024,256]{1,0:T(8,128)(2,1)S(1)}, f32[16,256,256]{2,1,0:T(8,128)}) custom-call(s32[2]{0:T(128)S(1)} %pad_add_fusion.ids, s32[2,32]{1,0:T(2,128)S(1)} %bitcast.7, s32[2,64]{1,0:T(2,128)S(1)} %bitcast.12, bf16[1024,512]{1,0:T(8,128)(2,1)S(1)} %get-tuple-element.24.zown_ref, ...), custom_call_target="tpu_custom_call", output_to_operand_aliasing={{2}: (7, {})} | custom-call | flops 1 | bytes 1 | tf_op jit(solution)/shard_map/next_pairs/pallas_call | solution.py:342
  34.9 0.0 collective-permute-done.3.own_ref
  35.0 1.1 %collective-permute-start.7 = (bf16[1040,256]{1,0:T(8,128)(2,1)S(1)}, bf16[1040,256]{1,0:T(8,128)(2,1)S(1)}, u32[]{:S(2)}, u32[]{:S(2)}) collective-permute-start(bf16[1040,256]{1,0:T(8,128)(2,1)S(1)} %collective-permute-done.3.own_ref), channel_id=1, source_target_pairs={{0,1},{1,0},{2,3},{3,2},{4,5},{5,4},{6,7},{7,6},{8,9},{9,8},{10,11... | collective-permute-start | bytes 1597448 | tf_op jit(solution)/shard_map/ppermute | solution.py:71
  36.1 3.1 %collective-permute-done.8.own_ref = bf16[1040,256]{1,0:T(8,128)(2,1)S(1)} collective-permute-done((bf16[1040,256]{1,0:T(8,128)(2,1)S(1)}, bf16[1040,256]{1,0:T(8,128)(2,1)S(1)}, u32[]{:S(2)}, u32[]{:S(2)}) %collective-permute-start.8) | collective-permute-done | bytes 532512 | tf_op jit(solution)/shard_map/ppermute | solution.py:67
  39.1 0.0 collective-permute-start.9
  39.1 0.5 %collective-permute-start.10 = (bf16[1024,256]{1,0:T(8,128)(2,1)S(1)}, bf16[1024,256]{1,0:T(8,128)(2,1)S(1)}, u32[]{:S(2)}, u32[]{:S(2)}) collective-permute-start(bf16[1024,256]{1,0:T(8,128)(2,1)S(1)} %get-tuple-element.40), channel_id=1, source_target_pairs={{0,1},{1,0},{2,3},{3,2},{4,5},{5,4},{6,7},{7,6},{8,9},{9,8},{10,11... | collective-permute-start | bytes 1572872 | tf_op jit(solution)/shard_map/ppermute | solution.py:71
  39.7 0.0 collective-permute-done.7.par_ref
  39.7 2.5 %zx_pairs.1 = (f32[1024,256]{1,0:T(8,128)S(1)}, f32[16,256,256]{2,1,0:T(8,128)}) custom-call(s32[2]{0:T(128)S(1)} %pad_add_fusion.ids, s32[2,32]{1,0:T(2,128)S(1)} %bitcast.8, s32[2,64]{1,0:T(2,128)S(1)} %bitcast.13, bf16[1024,512]{1,0:T(8,128)(2,1)S(1)} %get-tuple-element.24.zown_ref, ...), custom_call_target="tpu_custom_call", output_to_operand_aliasing={{1}: (7, {})} | custom-call | flops 1 | bytes 1048577 | tf_op jit(solution)/shard_map/zx_pairs/pallas_call | solution.py:342
  42.1 0.0 collective-permute-done.10.got_ref
  42.2 0.0 collective-permute-done.9.par_ref
  42.2 3.4 %last_pairs.1 = (bf16[1024,256]{1,0:T(8,128)(2,1)}, f32[16,256,256]{2,1,0:T(8,128)}) custom-call(s32[2]{0:T(128)S(1)} %pad_add_fusion.ids, s32[2,32]{1,0:T(2,128)S(1)} %bitcast.9, s32[2,64]{1,0:T(2,128)S(1)} %bitcast.14, bf16[1024,512]{1,0:T(8,128)(2,1)S(1)} %get-tuple-element.24.zown_ref, ...), custom_call_target="tpu_custom_call", output_to_operand_aliasing={{1}: (8, {})} | custom-call | flops 1 | bytes 4194305 | tf_op jit(solution)/shard_map/last_pairs/pallas_call | solution.py:342
  (3 shorter events, 0.0 us)
Async XLA Ops:
  0.6 10.9 %copy-start.1 = (s32[32,2]{0,1:T(2,128)S(1)}, s32[32,2]{0,1:T(2,128)}, u32[]{:S(2)}) copy-start(s32[32,2]{0,1:T(2,128)} %param.4) | copy-start | bytes 772
  0.6 10.9 %copy-start = (bf16[1024,256]{1,0:T(8,128)(2,1)S(1)}, bf16[1024,256]{1,0:T(8,128)(2,1)}, u32[]{:S(2)}) copy-start(bf16[1024,256]{1,0:T(8,128)(2,1)} %own_ref.1) | copy-start | bytes 1572868
  0.6 10.9 %copy-start.2 = (s32[64,2]{0,1:T(2,128)S(1)}, s32[64,2]{0,1:T(2,128)}, u32[]{:S(2)}) copy-start(s32[64,2]{0,1:T(2,128)} %param.5) | copy-start | bytes 1540
  1.8 6.2 %collective-permute-start.1 = (bf16[1040,256]{1,0:T(8,128)(2,1)S(1)}, bf16[1040,256]{1,0:T(8,128)(2,1)S(1)}, u32[]{:S(2)}, u32[]{:S(2)}) collective-permute-start(bf16[1040,256]{1,0:T(8,128)(2,1)S(1)} %fusion.3), channel_id=1, source_target_pairs={{0,1},{1,0},{2,3},{3,2},{4,5},{5,4},{6,7},{7,6},{8,9},{9,8},{10,11... | collective-permute-start | bytes 1597448 | tf_op jit(solution)/shard_map/ppermute | solution.py:71
  1.9 9.6 %collective-permute-start = (bf16[1040,256]{1,0:T(8,128)(2,1)S(1)}, bf16[1040,256]{1,0:T(8,128)(2,1)S(1)}, u32[]{:S(2)}, u32[]{:S(2)}) collective-permute-start(bf16[1040,256]{1,0:T(8,128)(2,1)S(1)} %fusion.3), channel_id=1, source_target_pairs={{0,2},{1,5},{2,0},{3,7},{4,6},{5,1},{6,4},{7,3},{8,10},{9,13},{10,... | collective-permute-start | bytes 1597448 | tf_op jit(solution)/shard_map/ppermute | solution.py:67
  4.6 14.5 %collective-permute-start.2 = (bf16[1040,256]{1,0:T(8,128)(2,1)S(1)}, bf16[1040,256]{1,0:T(8,128)(2,1)S(1)}, u32[]{:S(2)}, u32[]{:S(2)}) collective-permute-start(bf16[1040,256]{1,0:T(8,128)(2,1)S(1)} %fusion.3), channel_id=1, source_target_pairs={{0,24},{1,25},{2,10},{3,11},{4,28},{5,29},{6,14},{7,15},{8,0},{9,1... | collective-permute-start | bytes 1597448 | tf_op jit(solution)/shard_map/ppermute | solution.py:67
  8.0 13.1 %collective-permute-start.4 = (bf16[1040,256]{1,0:T(8,128)(2,1)S(1)}, bf16[1040,256]{1,0:T(8,128)(2,1)S(1)}, u32[]{:S(2)}, u32[]{:S(2)}) collective-permute-start(bf16[1040,256]{1,0:T(8,128)(2,1)S(1)} %collective-permute-done.1.par_ref), channel_id=1, source_target_pairs={{0,2},{1,5},{2,0},{3,7},{4,6},{5,1},{6,4},{7,3},{8,10},{9,13},{10,... | collective-permute-start | bytes 1597448 | tf_op jit(solution)/shard_map/ppermute | solution.py:67
  14.4 11.1 %collective-permute-start.5 = (bf16[1040,256]{1,0:T(8,128)(2,1)S(1)}, bf16[1040,256]{1,0:T(8,128)(2,1)S(1)}, u32[]{:S(2)}, u32[]{:S(2)}) collective-permute-start(bf16[1040,256]{1,0:T(8,128)(2,1)S(1)} %collective-permute-done.own_ref), channel_id=1, source_target_pairs={{0,4},{1,8},{2,6},{3,11},{4,1},{5,29},{6,2},{7,31},{8,12},{9,16},{... | collective-permute-start | bytes 1597448 | tf_op jit(solution)/shard_map/ppermute | solution.py:67
  19.1 15.8 %collective-permute-start.3 = (bf16[1040,256]{1,0:T(8,128)(2,1)S(1)}, bf16[1040,256]{1,0:T(8,128)(2,1)S(1)}, u32[]{:S(2)}, u32[]{:S(2)}) collective-permute-start(bf16[1040,256]{1,0:T(8,128)(2,1)S(1)} %collective-permute-done.2), channel_id=1, source_target_pairs={{0,2},{1,3},{2,0},{3,1},{4,6},{5,7},{6,4},{7,5},{8,10},{9,11},{10,... | collective-permute-start | bytes 1597448 | tf_op jit(solution)/shard_map/ppermute | solution.py:67
  21.1 10.2 %collective-permute-start.6 = (bf16[1040,256]{1,0:T(8,128)(2,1)S(1)}, bf16[1040,256]{1,0:T(8,128)(2,1)S(1)}, u32[]{:S(2)}, u32[]{:S(2)}) collective-permute-start(bf16[1040,256]{1,0:T(8,128)(2,1)S(1)} %collective-permute-done.4.par_ref), channel_id=1, source_target_pairs={{0,4},{1,8},{2,6},{3,11},{4,1},{5,29},{6,2},{7,31},{8,12},{9,16},{... | collective-permute-start | bytes 1597448 | tf_op jit(solution)/shard_map/ppermute | solution.py:67
  25.6 13.6 %collective-permute-start.8 = (bf16[1040,256]{1,0:T(8,128)(2,1)S(1)}, bf16[1040,256]{1,0:T(8,128)(2,1)S(1)}, u32[]{:S(2)}, u32[]{:S(2)}) collective-permute-start(bf16[1040,256]{1,0:T(8,128)(2,1)S(1)} %collective-permute-done.5.one_ref), channel_id=1, source_target_pairs={{0,3},{1,8},{2,10},{3,1},{4,28},{5,7},{6,30},{7,5},{8,11},{9,16},{... | collective-permute-start | bytes 1597448 | tf_op jit(solution)/shard_map/ppermute | solution.py:67
  35.0 4.7 %collective-permute-start.7 = (bf16[1040,256]{1,0:T(8,128)(2,1)S(1)}, bf16[1040,256]{1,0:T(8,128)(2,1)S(1)}, u32[]{:S(2)}, u32[]{:S(2)}) collective-permute-start(bf16[1040,256]{1,0:T(8,128)(2,1)S(1)} %collective-permute-done.3.own_ref), channel_id=1, source_target_pairs={{0,1},{1,0},{2,3},{3,2},{4,5},{5,4},{6,7},{7,6},{8,9},{9,8},{10,11... | collective-permute-start | bytes 1597448 | tf_op jit(solution)/shard_map/ppermute | solution.py:71
  39.1 3.0 %collective-permute-start.9 = (bf16[1040,256]{1,0:T(8,128)(2,1)S(1)}, bf16[1040,256]{1,0:T(8,128)(2,1)S(1)}, u32[]{:S(2)}, u32[]{:S(2)}) collective-permute-start(bf16[1040,256]{1,0:T(8,128)(2,1)S(1)} %collective-permute-done.8.own_ref), channel_id=1, source_target_pairs={{0,1},{1,0},{2,3},{3,2},{4,5},{5,4},{6,7},{7,6},{8,9},{9,8},{10,11... | collective-permute-start | bytes 1597448 | tf_op jit(solution)/shard_map/ppermute | solution.py:71
  39.1 3.0 %collective-permute-start.10 = (bf16[1024,256]{1,0:T(8,128)(2,1)S(1)}, bf16[1024,256]{1,0:T(8,128)(2,1)S(1)}, u32[]{:S(2)}, u32[]{:S(2)}) collective-permute-start(bf16[1024,256]{1,0:T(8,128)(2,1)S(1)} %get-tuple-element.40), channel_id=1, source_target_pairs={{0,1},{1,0},{2,3},{3,2},{4,5},{5,4},{6,7},{7,6},{8,9},{9,8},{10,11... | collective-permute-start | bytes 1572872 | tf_op jit(solution)/shard_map/ppermute | solution.py:71

commit v7 on v6

--- a/solution.py
+++ b/solution.py
@@ -16,7 +16,7 @@
 EPS = 1e-05
 STEP = 256
 TABLE = 2 * CAP
-PARTS = 2
+PARTS = 4
 VMEM = 24 * 1024 * 1024
 
 

time: 45.8 us -> 45.8 us (level)
  transfers between devices with their start and end apart: 11 -> 11, of which waited for: 5 -> 5; matrix products, arithmetic and copies ran while one was open for 0% -> 0% of each run, Pallas kernels for 27% -> 26%
where the time goes in v7:
time: 45.8 us; the launch traced here: 45.6 us
  starting transfers between devices  15.9 us (35%)
  Pallas kernels  15.4 us (34%)
  waiting for transfers between devices  12.3 us (27%)
  other arithmetic  1.23 us (3%)
  between operations  0.73 us (2%)
    ppermute x7, starting transfers between devices, send(): return lax.ppermute(value, ('feat', 'samp'), pairs)  14.1 us
    pallas_call x4, Pallas kernels, run_unit(): pl.pallas_call(kernel, out_shape=(*outs, jax.ShapeDtypeStruct(corr.shape,...  12.5 us
    ppermute x7, waiting for transfers between devices, send(): return lax.ppermute(value, ('feat', 'samp'), pairs)  12.3 us
    pallas_call x1, Pallas kernels, run_self(): pl.pallas_call(self_kernel, out_shape=(jax.ShapeDtypeStruct((rows, 2 * wi...  2.88 us
    ppermute x4, starting transfers between devices, swap(): return lax.ppermute(value, 'samp', [(0, 1), (1, 0)])  1.89 us
    add x1, other arithmetic, with_table(): return jnp.pad(spectra, ((0, TABLE), (0, 0))) + below  1.15 us
  transfers between devices with their start and end apart: 11, of which 5 were waited for; matrix products, arithmetic and copies ran while one was open for 0% of the time, Pallas kernels for 26%

profile of v7, /device:TPU:1, one launch (start us, length us, event | category | flops | bytes accessed | tf_op | source)
XLA Modules:
  0.0 45.6 jit_solution(3874989183113255350)
XLA Ops:
  0.6 0.0 copy-start.1
  0.6 0.0 copy-start
  0.6 0.0 copy-start.2
  0.7 1.2 %fusion.3 = bf16[1040,256]{1,0:T(8,128)(2,1)S(1)} fusion(s32[2,32]{1,0:T(2,128)} %bitcast.4, bf16[1024,256]{1,0:T(8,128)(2,1)} %own_ref.1), kind=kLoop, calls=%fused_computation.8 | loop fusion | flops 3461120 | bytes 1057024 | tf_op jit(solution)/shard_map/add | solution.py:364
  1.8 0.1 collective-permute-start.1
  1.9 2.7 %collective-permute-start = (bf16[1040,256]{1,0:T(8,128)(2,1)S(1)}, bf16[1040,256]{1,0:T(8,128)(2,1)S(1)}, u32[]{:S(2)}, u32[]{:S(2)}) collective-permute-start(bf16[1040,256]{1,0:T(8,128)(2,1)S(1)} %fusion.3), channel_id=1, source_target_pairs={{0,2},{1,5},{2,0},{3,7},{4,6},{5,1},{6,4},{7,3},{8,10},{9,13},{10,... | collective-permute-start | bytes 1597448 | tf_op jit(solution)/shard_map/ppermute | solution.py:67
  4.6 3.3 %collective-permute-start.2 = (bf16[1040,256]{1,0:T(8,128)(2,1)S(1)}, bf16[1040,256]{1,0:T(8,128)(2,1)S(1)}, u32[]{:S(2)}, u32[]{:S(2)}) collective-permute-start(bf16[1040,256]{1,0:T(8,128)(2,1)S(1)} %fusion.3), channel_id=1, source_target_pairs={{0,24},{1,25},{2,10},{3,11},{4,28},{5,29},{6,14},{7,15},{8,0},{9,1... | collective-permute-start | bytes 1597448 | tf_op jit(solution)/shard_map/ppermute | solution.py:67
  7.9 0.1 pad_add_fusion.ids
  8.0 0.0 collective-permute-done.1.par_ref
  8.0 0.2 collective-permute-start.4
  8.3 3.3 %collective-permute-done.own_ref = bf16[1040,256]{1,0:T(8,128)(2,1)S(1)} collective-permute-done((bf16[1040,256]{1,0:T(8,128)(2,1)S(1)}, bf16[1040,256]{1,0:T(8,128)(2,1)S(1)}, u32[]{:S(2)}, u32[]{:S(2)}) %collective-permute-start) | collective-permute-done | bytes 532512 | tf_op jit(solution)/shard_map/ppermute | solution.py:67
  11.6 2.9 %self_pairs.1 = (bf16[1024,512]{1,0:T(8,128)(2,1)S(1)}, f32[1024,256]{1,0:T(8,128)S(1)}, f32[16,256,256]{2,1,0:T(8,128)}) custom-call(s32[2]{0:T(128)S(1)} %pad_add_fusion.ids, s32[2,32]{1,0:T(2,128)S(1)} %bitcast.5, s32[2,64]{1,0:T(2,128)S(1)} %bitcast.10, bf16[1024,256]{1,0:T(8,128)(2,1)S(1)} %copy-done, bf16[1040,256]{1,0:T(8,128)(2,1)S(1)} %collective-permute-done.1.par_ref), custom_call_target="tpu_custom_call" | custom-call | flops 1 | bytes 524289 | tf_op jit(solution)/shard_map/self_pairs/pallas_call | solution.py:321
  14.5 3.0 %collective-permute-start.5 = (bf16[1040,256]{1,0:T(8,128)(2,1)S(1)}, bf16[1040,256]{1,0:T(8,128)(2,1)S(1)}, u32[]{:S(2)}, u32[]{:S(2)}) collective-permute-start(bf16[1040,256]{1,0:T(8,128)(2,1)S(1)} %collective-permute-done.own_ref), channel_id=1, source_target_pairs={{0,4},{1,8},{2,6},{3,11},{4,1},{5,29},{6,2},{7,31},{8,12},{9,16},{... | collective-permute-start | bytes 1597448 | tf_op jit(solution)/shard_map/ppermute | solution.py:67
  17.4 1.7 %collective-permute-done.2 = bf16[1040,256]{1,0:T(8,128)(2,1)S(1)} collective-permute-done((bf16[1040,256]{1,0:T(8,128)(2,1)S(1)}, bf16[1040,256]{1,0:T(8,128)(2,1)S(1)}, u32[]{:S(2)}, u32[]{:S(2)}) %collective-permute-start.2) | collective-permute-done | bytes 532512 | tf_op jit(solution)/shard_map/ppermute | solution.py:67
  19.1 2.0 %collective-permute-start.3 = (bf16[1040,256]{1,0:T(8,128)(2,1)S(1)}, bf16[1040,256]{1,0:T(8,128)(2,1)S(1)}, u32[]{:S(2)}, u32[]{:S(2)}) collective-permute-start(bf16[1040,256]{1,0:T(8,128)(2,1)S(1)} %collective-permute-done.2), channel_id=1, source_target_pairs={{0,2},{1,3},{2,0},{3,1},{4,6},{5,7},{6,4},{7,5},{8,10},{9,11},{10,... | collective-permute-start | bytes 1597448 | tf_op jit(solution)/shard_map/ppermute | solution.py:67
  21.1 0.0 collective-permute-done.4.par_ref
  21.1 0.4 collective-permute-start.6
  21.5 3.1 %near_pairs.1 = (f32[1024,512]{1,0:T(8,128)S(1)}, f32[16,256,256]{2,1,0:T(8,128)}) custom-call(s32[2]{0:T(128)S(1)} %pad_add_fusion.ids, s32[2,32]{1,0:T(2,128)S(1)} %bitcast.6, s32[2,64]{1,0:T(2,128)S(1)} %bitcast.11, bf16[1024,512]{1,0:T(8,128)(2,1)S(1)} %get-tuple-element.24.zown_ref, ...), custom_call_target="tpu_custom_call", output_to_operand_aliasing={{1}: (7, {})} | custom-call | flops 1 | bytes 8388609 | tf_op jit(solution)/shard_map/near_pairs/pallas_call | solution.py:342
  24.6 1.0 %collective-permute-done.5.one_ref = bf16[1040,256]{1,0:T(8,128)(2,1)S(1)} collective-permute-done((bf16[1040,256]{1,0:T(8,128)(2,1)S(1)}, bf16[1040,256]{1,0:T(8,128)(2,1)S(1)}, u32[]{:S(2)}, u32[]{:S(2)}) %collective-permute-start.5) | collective-permute-done | bytes 532512 | tf_op jit(solution)/shard_map/ppermute | solution.py:67
  25.6 2.5 %collective-permute-start.8 = (bf16[1040,256]{1,0:T(8,128)(2,1)S(1)}, bf16[1040,256]{1,0:T(8,128)(2,1)S(1)}, u32[]{:S(2)}, u32[]{:S(2)}) collective-permute-start(bf16[1040,256]{1,0:T(8,128)(2,1)S(1)} %collective-permute-done.5.one_ref), channel_id=1, source_target_pairs={{0,3},{1,8},{2,10},{3,1},{4,28},{5,7},{6,30},{7,5},{8,11},{9,16},{... | collective-permute-start | bytes 1597448 | tf_op jit(solution)/shard_map/ppermute | solution.py:67
  28.1 3.2 %collective-permute-done.6.two_ref = bf16[1040,256]{1,0:T(8,128)(2,1)S(1)} collective-permute-done((bf16[1040,256]{1,0:T(8,128)(2,1)S(1)}, bf16[1040,256]{1,0:T(8,128)(2,1)S(1)}, u32[]{:S(2)}, u32[]{:S(2)}) %collective-permute-start.6) | collective-permute-done | bytes 532512 | tf_op jit(solution)/shard_map/ppermute | solution.py:67
  31.3 3.5 %next_pairs.1 = (f32[1024,256]{1,0:T(8,128)S(1)}, bf16[1024,256]{1,0:T(8,128)(2,1)S(1)}, f32[16,256,256]{2,1,0:T(8,128)}) custom-call(s32[2]{0:T(128)S(1)} %pad_add_fusion.ids, s32[2,32]{1,0:T(2,128)S(1)} %bitcast.7, s32[2,64]{1,0:T(2,128)S(1)} %bitcast.12, bf16[1024,512]{1,0:T(8,128)(2,1)S(1)} %get-tuple-element.24.zown_ref, ...), custom_call_target="tpu_custom_call", output_to_operand_aliasing={{2}: (7, {})} | custom-call | flops 1 | bytes 1 | tf_op jit(solution)/shard_map/next_pairs/pallas_call | solution.py:342
  34.8 0.0 collective-permute-done.3.own_ref
  34.8 1.3 %collective-permute-start.7 = (bf16[1040,256]{1,0:T(8,128)(2,1)S(1)}, bf16[1040,256]{1,0:T(8,128)(2,1)S(1)}, u32[]{:S(2)}, u32[]{:S(2)}) collective-permute-start(bf16[1040,256]{1,0:T(8,128)(2,1)S(1)} %collective-permute-done.3.own_ref), channel_id=1, source_target_pairs={{0,1},{1,0},{2,3},{3,2},{4,5},{5,4},{6,7},{7,6},{8,9},{9,8},{10,11... | collective-permute-start | bytes 1597448 | tf_op jit(solution)/shard_map/ppermute | solution.py:71
  36.1 3.1 %collective-permute-done.8.own_ref = bf16[1040,256]{1,0:T(8,128)(2,1)S(1)} collective-permute-done((bf16[1040,256]{1,0:T(8,128)(2,1)S(1)}, bf16[1040,256]{1,0:T(8,128)(2,1)S(1)}, u32[]{:S(2)}, u32[]{:S(2)}) %collective-permute-start.8) | collective-permute-done | bytes 532512 | tf_op jit(solution)/shard_map/ppermute | solution.py:67
  39.1 0.0 collective-permute-start.9
  39.1 0.5 %collective-permute-start.10 = (bf16[1024,256]{1,0:T(8,128)(2,1)S(1)}, bf16[1024,256]{1,0:T(8,128)(2,1)S(1)}, u32[]{:S(2)}, u32[]{:S(2)}) collective-permute-start(bf16[1024,256]{1,0:T(8,128)(2,1)S(1)} %get-tuple-element.40), channel_id=1, source_target_pairs={{0,1},{1,0},{2,3},{3,2},{4,5},{5,4},{6,7},{7,6},{8,9},{9,8},{10,11... | collective-permute-start | bytes 1572872 | tf_op jit(solution)/shard_map/ppermute | solution.py:71
  39.7 0.0 collective-permute-done.7.par_ref
  39.7 2.5 %zx_pairs.1 = (f32[1024,256]{1,0:T(8,128)S(1)}, f32[16,256,256]{2,1,0:T(8,128)}) custom-call(s32[2]{0:T(128)S(1)} %pad_add_fusion.ids, s32[2,32]{1,0:T(2,128)S(1)} %bitcast.8, s32[2,64]{1,0:T(2,128)S(1)} %bitcast.13, bf16[1024,512]{1,0:T(8,128)(2,1)S(1)} %get-tuple-element.24.zown_ref, ...), custom_call_target="tpu_custom_call", output_to_operand_aliasing={{1}: (7, {})} | custom-call | flops 1 | bytes 1048577 | tf_op jit(solution)/shard_map/zx_pairs/pallas_call | solution.py:342
  42.2 0.0 collective-permute-done.10.got_ref
  42.2 0.0 collective-permute-done.9.par_ref
  42.2 3.4 %last_pairs.1 = (bf16[1024,256]{1,0:T(8,128)(2,1)}, f32[16,256,256]{2,1,0:T(8,128)}) custom-call(s32[2]{0:T(128)S(1)} %pad_add_fusion.ids, s32[2,32]{1,0:T(2,128)S(1)} %bitcast.9, s32[2,64]{1,0:T(2,128)S(1)} %bitcast.14, bf16[1024,512]{1,0:T(8,128)(2,1)S(1)} %get-tuple-element.24.zown_ref, ...), custom_call_target="tpu_custom_call", output_to_operand_aliasing={{1}: (8, {})} | custom-call | flops 1 | bytes 4194305 | tf_op jit(solution)/shard_map/last_pairs/pallas_call | solution.py:342
  (3 shorter events, 0.0 us)
Async XLA Ops:
  0.6 10.9 %copy-start.1 = (s32[32,2]{0,1:T(2,128)S(1)}, s32[32,2]{0,1:T(2,128)}, u32[]{:S(2)}) copy-start(s32[32,2]{0,1:T(2,128)} %param.4) | copy-start | bytes 772
  0.6 10.9 %copy-start = (bf16[1024,256]{1,0:T(8,128)(2,1)S(1)}, bf16[1024,256]{1,0:T(8,128)(2,1)}, u32[]{:S(2)}) copy-start(bf16[1024,256]{1,0:T(8,128)(2,1)} %own_ref.1) | copy-start | bytes 1572868
  0.6 10.9 %copy-start.2 = (s32[64,2]{0,1:T(2,128)S(1)}, s32[64,2]{0,1:T(2,128)}, u32[]{:S(2)}) copy-start(s32[64,2]{0,1:T(2,128)} %param.5) | copy-start | bytes 1540
  1.8 6.2 %collective-permute-start.1 = (bf16[1040,256]{1,0:T(8,128)(2,1)S(1)}, bf16[1040,256]{1,0:T(8,128)(2,1)S(1)}, u32[]{:S(2)}, u32[]{:S(2)}) collective-permute-start(bf16[1040,256]{1,0:T(8,128)(2,1)S(1)} %fusion.3), channel_id=1, source_target_pairs={{0,1},{1,0},{2,3},{3,2},{4,5},{5,4},{6,7},{7,6},{8,9},{9,8},{10,11... | collective-permute-start | bytes 1597448 | tf_op jit(solution)/shard_map/ppermute | solution.py:71
  1.9 9.6 %collective-permute-start = (bf16[1040,256]{1,0:T(8,128)(2,1)S(1)}, bf16[1040,256]{1,0:T(8,128)(2,1)S(1)}, u32[]{:S(2)}, u32[]{:S(2)}) collective-permute-start(bf16[1040,256]{1,0:T(8,128)(2,1)S(1)} %fusion.3), channel_id=1, source_target_pairs={{0,2},{1,5},{2,0},{3,7},{4,6},{5,1},{6,4},{7,3},{8,10},{9,13},{10,... | collective-permute-start | bytes 1597448 | tf_op jit(solution)/shard_map/ppermute | solution.py:67
  4.6 14.5 %collective-permute-start.2 = (bf16[1040,256]{1,0:T(8,128)(2,1)S(1)}, bf16[1040,256]{1,0:T(8,128)(2,1)S(1)}, u32[]{:S(2)}, u32[]{:S(2)}) collective-permute-start(bf16[1040,256]{1,0:T(8,128)(2,1)S(1)} %fusion.3), channel_id=1, source_target_pairs={{0,24},{1,25},{2,10},{3,11},{4,28},{5,29},{6,14},{7,15},{8,0},{9,1... | collective-permute-start | bytes 1597448 | tf_op jit(solution)/shard_map/ppermute | solution.py:67
  8.0 13.1 %collective-permute-start.4 = (bf16[1040,256]{1,0:T(8,128)(2,1)S(1)}, bf16[1040,256]{1,0:T(8,128)(2,1)S(1)}, u32[]{:S(2)}, u32[]{:S(2)}) collective-permute-start(bf16[1040,256]{1,0:T(8,128)(2,1)S(1)} %collective-permute-done.1.par_ref), channel_id=1, source_target_pairs={{0,2},{1,5},{2,0},{3,7},{4,6},{5,1},{6,4},{7,3},{8,10},{9,13},{10,... | collective-permute-start | bytes 1597448 | tf_op jit(solution)/shard_map/ppermute | solution.py:67
  14.5 11.1 %collective-permute-start.5 = (bf16[1040,256]{1,0:T(8,128)(2,1)S(1)}, bf16[1040,256]{1,0:T(8,128)(2,1)S(1)}, u32[]{:S(2)}, u32[]{:S(2)}) collective-permute-start(bf16[1040,256]{1,0:T(8,128)(2,1)S(1)} %collective-permute-done.own_ref), channel_id=1, source_target_pairs={{0,4},{1,8},{2,6},{3,11},{4,1},{5,29},{6,2},{7,31},{8,12},{9,16},{... | collective-permute-start | bytes 1597448 | tf_op jit(solution)/shard_map/ppermute | solution.py:67
  19.1 15.7 %collective-permute-start.3 = (bf16[1040,256]{1,0:T(8,128)(2,1)S(1)}, bf16[1040,256]{1,0:T(8,128)(2,1)S(1)}, u32[]{:S(2)}, u32[]{:S(2)}) collective-permute-start(bf16[1040,256]{1,0:T(8,128)(2,1)S(1)} %collective-permute-done.2), channel_id=1, source_target_pairs={{0,2},{1,3},{2,0},{3,1},{4,6},{5,7},{6,4},{7,5},{8,10},{9,11},{10,... | collective-permute-start | bytes 1597448 | tf_op jit(solution)/shard_map/ppermute | solution.py:67
  21.1 10.2 %collective-permute-start.6 = (bf16[1040,256]{1,0:T(8,128)(2,1)S(1)}, bf16[1040,256]{1,0:T(8,128)(2,1)S(1)}, u32[]{:S(2)}, u32[]{:S(2)}) collective-permute-start(bf16[1040,256]{1,0:T(8,128)(2,1)S(1)} %collective-permute-done.4.par_ref), channel_id=1, source_target_pairs={{0,4},{1,8},{2,6},{3,11},{4,1},{5,29},{6,2},{7,31},{8,12},{9,16},{... | collective-permute-start | bytes 1597448 | tf_op jit(solution)/shard_map/ppermute | solution.py:67
  25.6 13.6 %collective-permute-start.8 = (bf16[1040,256]{1,0:T(8,128)(2,1)S(1)}, bf16[1040,256]{1,0:T(8,128)(2,1)S(1)}, u32[]{:S(2)}, u32[]{:S(2)}) collective-permute-start(bf16[1040,256]{1,0:T(8,128)(2,1)S(1)} %collective-permute-done.5.one_ref), channel_id=1, source_target_pairs={{0,3},{1,8},{2,10},{3,1},{4,28},{5,7},{6,30},{7,5},{8,11},{9,16},{... | collective-permute-start | bytes 1597448 | tf_op jit(solution)/shard_map/ppermute | solution.py:67
  34.8 4.9 %collective-permute-start.7 = (bf16[1040,256]{1,0:T(8,128)(2,1)S(1)}, bf16[1040,256]{1,0:T(8,128)(2,1)S(1)}, u32[]{:S(2)}, u32[]{:S(2)}) collective-permute-start(bf16[1040,256]{1,0:T(8,128)(2,1)S(1)} %collective-permute-done.3.own_ref), channel_id=1, source_target_pairs={{0,1},{1,0},{2,3},{3,2},{4,5},{5,4},{6,7},{7,6},{8,9},{9,8},{10,11... | collective-permute-start | bytes 1597448 | tf_op jit(solution)/shard_map/ppermute | solution.py:71
  39.1 3.0 %collective-permute-start.9 = (bf16[1040,256]{1,0:T(8,128)(2,1)S(1)}, bf16[1040,256]{1,0:T(8,128)(2,1)S(1)}, u32[]{:S(2)}, u32[]{:S(2)}) collective-permute-start(bf16[1040,256]{1,0:T(8,128)(2,1)S(1)} %collective-permute-done.8.own_ref), channel_id=1, source_target_pairs={{0,1},{1,0},{2,3},{3,2},{4,5},{5,4},{6,7},{7,6},{8,9},{9,8},{10,11... | collective-permute-start | bytes 1597448 | tf_op jit(solution)/shard_map/ppermute | solution.py:71
  39.1 3.0 %collective-permute-start.10 = (bf16[1024,256]{1,0:T(8,128)(2,1)S(1)}, bf16[1024,256]{1,0:T(8,128)(2,1)S(1)}, u32[]{:S(2)}, u32[]{:S(2)}) collective-permute-start(bf16[1024,256]{1,0:T(8,128)(2,1)S(1)} %get-tuple-element.40), channel_id=1, source_target_pairs={{0,1},{1,0},{2,3},{3,2},{4,5},{5,4},{6,7},{7,6},{8,9},{9,8},{10,11... | collective-permute-start | bytes 1572872 | tf_op jit(solution)/shard_map/ppermute | solution.py:71
